TPU v7x, 256 devices: a whole 4x4x8 slice. The times are simulated.
256 devices in a mesh: lat: 16 (over z, core), lon: 16 (over x, y).
Axes of the slice: x: 4, y: 4, z: 8, core: 2. Of those that a mesh axis runs over, the one named last changes fastest.
Arguments:
- adjoint_state: float32 [3, 12, 256, 5760], P(None, None, 'lat', 'lon'), may hold values from -6 to 6
- innovation: float32 [3, 12, 256, 5760], P(None, None, 'lat', 'lon'), may hold values from -6 to 6
- coefficients: float32 [3, 5, 12, 256, 5760], P(None, None, None, 'lat', 'lon'), may hold values from 0.1 to 0.6
- polar_mask: int32 [256], P('lat'), may hold values from 0 to 1, as said below
- wave_cutoff: int32 [256], P('lat'), may hold values from 1 to 64, as said below
Outputs:
- adjoint_start: float32 [3, 12, 256, 5760], P(None, None, 'lat', 'lon')
Inputs may be any that keep to these rules, and one draw needn't show every extreme that they name: polar_mask is 1 on every row within 8 rows of either pole, 0 on every row 16 or more rows from both poles, and either on the rows between. `wave_cutoff`: rows with polar_mask 0 have the cutoff 64.
All inputs are finite; a program needn't handle non-finite values.
Results may differ from a plain program's by a relative error of at most 0.00008.
Values sent between devices are 32-bit elements; how exact they have to be, the bound alone decides.
No kernel may reach another device: no remote copies, remote signals or barrier semaphores. Data moves between devices by JAX's collectives and lax.ppermute only.
A program may use at most 128 MiB of HBM per device.

v0:
```python
import math

import jax
import jax.numpy as jnp
import numpy as np
from jax import lax
from jax.experimental import pallas as pl
from jax.experimental.pallas import tpu as pltpu
from jax.sharding import PartitionSpec as P

NLON = 5760
KMAX = 64
WAVES = 2 * KMAX
FIELDS = 3
LEV = 12
BAND = 16
HALF = BAND // 2
LON_DEV = 16
LAT_DEV = 16
TOP = LAT_DEV - 1
WIDTH = NLON // LON_DEV
WIDE = 384
SLABS = FIELDS * LEV
ROWS = SLABS * BAND
SHARE = WAVES // LON_DEV
UNROLL = 6
HIGHEST = lax.Precision.HIGHEST

FIELD = (FIELDS, LEV, BAND, WIDTH)
HALF_FIELD = (FIELDS, LEV, HALF, WIDTH)
COEFF = (FIELDS, 5, LEV, BAND, WIDTH)
CHUNKS = (LON_DEV, SHARE, ROWS + 64)
LINE = (SLABS, WIDTH)
LINES = (3, SLABS, WIDTH)
TILES = (2, HALF, 128)
EDGES = (2, BAND, 128)


def wave_tables():
    columns = np.concatenate([np.arange(WIDTH), [WIDTH, -1]])
    phases = (np.arange(LON_DEV)[:, None] * WIDTH + columns[None, :]) % NLON
    phases = phases[:, None, :] * np.arange(KMAX)[None, :, None] % NLON
    radians = phases * (2.0 * math.pi / NLON)
    both = np.concatenate([np.cos(radians), np.sin(radians)], axis=1)
    return np.pad(both, ((0, 0), (0, 0), (0, WIDE - WIDTH - 2))).astype(np.float32)


def dot(left, right, left_dim, right_dim):
    return lax.dot_general(
        left,
        right,
        (((left_dim,), (right_dim,)), ((), ())),
        precision=HIGHEST,
        preferred_element_type=jnp.float32,
    )


def iota(shape, dim):
    return lax.broadcasted_iota(jnp.int32, shape, dim)


def in_vmem(shape):
    return pltpu.VMEM(shape, jnp.float32)


def launch(kernel, operands, outs, far_outs=(), scratch=(), copies=0, aliases=None):
    shapes = [*outs, *far_outs]
    nbytes = sum(4 * math.prod(shape) for shape in shapes)
    nbytes += sum(4 * math.prod(operand.shape) for operand in operands)
    return pl.pallas_call(
        kernel,
        in_specs=[pl.BlockSpec(memory_space=pltpu.HBM)] * len(operands),
        out_specs=[pl.BlockSpec(memory_space=pltpu.VMEM)] * len(outs)
        + [pl.BlockSpec(memory_space=pltpu.HBM)] * len(far_outs),
        out_shape=[jax.ShapeDtypeStruct(shape, jnp.float32) for shape in shapes],
        scratch_shapes=[*scratch, pltpu.SemaphoreType.DMA((copies,))],
        input_output_aliases=aliases or {},
        compiler_params=pltpu.CompilerParams(vmem_limit_bytes=24 * 2**20),
        cost_estimate=pl.CostEstimate(flops=0, bytes_accessed=nbytes, transcendentals=0),
    )(*operands)


def begin(sems, *pairs):
    started = []
    for index, (source, target) in enumerate(pairs):
        copy = pltpu.make_async_copy(source, target, sems.at[index])
        copy.start()
        started.append(copy)
    return started


def finish(*started):
    for copy in started:
        copy.wait()


def for_slabs(one, carry=0):
    def some(step, carry):
        for slab in range(UNROLL):
            carry = one(step * UNROLL + slab, carry)
        return carry

    return lax.fori_loop(0, SLABS // UNROLL, some, carry)


def lane_of(tile, slab):
    return jnp.sum(jnp.where(iota(tile.shape, 1) == slab, tile, 0.0), axis=1, keepdims=True)


def with_lane(tile, slab, column):
    return jnp.where(iota(tile.shape, 1) == slab, column, tile)


def place():
    return lax.axis_index("lon"), lax.axis_index("lat")


def open_row(lat):
    return pl.multiple_of(jnp.where(lat == TOP, 0, HALF), HALF)


def row_weight(mask, first, shape):
    row = iota(shape, 0)
    weight = jnp.zeros(shape, jnp.float32)
    for r in range(shape[0]):
        weight = jnp.where(row == r, mask[first + r].astype(jnp.float32), weight)
    return weight


def forward_kernel(
    field_in, coeff_in, table_in, mask_in, send, field, table, to_east, to_west, mask, sems
):
    lon, lat = place()
    first = open_row(lat)
    rows = pl.ds(first, HALF)
    field_copy, table_copy, *rest = begin(
        sems,
        (field_in, field),
        (table_in.at[lon], table),
        (coeff_in.at[:, 3, :, rows], to_east),
        (coeff_in.at[:, 4, :, rows], to_west),
        (mask_in, mask),
    )
    finish(field_copy, table_copy)
    waves = dot(table[:, :WIDTH], field[...].reshape(ROWS, WIDTH), 1, 1)
    send[:, :, :ROWS] = waves.reshape(LON_DEV, SHARE, ROWS)
    finish(*rest)
    filtered = row_weight(mask, first, (HALF, 1)) > 0.5
    east = west = jnp.zeros((HALF, 128), jnp.float32)
    for slab in range(SLABS):
        at = slab // LEV, slab % LEV
        value = field[*at, rows]
        coeff = to_east[at][:, WIDTH - 1 :]
        east = with_lane(east, slab, jnp.where(filtered, coeff, coeff * value[:, WIDTH - 1 :]))
        coeff = to_west[at][:, 0:1]
        west = with_lane(west, slab, jnp.where(filtered, coeff, coeff * value[:, 0:1]))
    for target in range(LON_DEV):
        send[target, :, ROWS:] = jnp.where(target == (lon + 1) % LON_DEV, east, west)[:, :64]


def across_kernel(coeff_in, across, tiles, pole, to_east, to_west, sems):
    lon, lat = place()
    top = lat == TOP
    closed = pl.ds(pl.multiple_of(HALF - open_row(lat), HALF), HALF)
    term = jnp.where(top, 1, 2)
    finish(
        *begin(
            sems,
            (coeff_in.at[:, term, :, closed], pole),
            (coeff_in.at[:, 3, :, closed], to_east),
            (coeff_in.at[:, 4, :, closed], to_west),
        )
    )
    east = west = jnp.zeros((HALF, 128), jnp.float32)
    for slab in range(SLABS):
        at = slab // LEV, slab % LEV
        sign = 1.0 if at[0] == FIELDS - 1 else -1.0
        lines = pole[at]
        across[slab : slab + 1] = sign * jnp.where(top, lines[HALF - 1 :], lines[0:1])
        east = with_lane(east, slab, to_east[at][:, WIDTH - 1 :])
        west = with_lane(west, slab, to_west[at][:, 0:1])
    tiles[0] = east
    tiles[1] = west


def respond_kernel(received_in, cutoff_in, tiles_in, send, edges, received, cutoff, tiles, sems):
    lon, _ = place()
    main, *rest = begin(
        sems, (received_in, received), (cutoff_in, cutoff), (tiles_in, tiles)
    )
    finish(*rest)
    shape = (SHARE, ROWS)
    wave = (lon * SHARE + iota(shape, 0)) % KMAX
    row = iota(shape, 1) % BAND
    limit = jnp.zeros(shape, jnp.int32)
    for r in range(BAND):
        limit = jnp.where(row == r, cutoff[r], limit)
    ratio = limit.astype(jnp.float32) / jnp.maximum(wave, 1).astype(jnp.float32)
    response = jnp.where(wave <= limit, 1.0, ratio * ratio)
    response = response * jnp.where(wave == 0, 1.0 / NLON, 2.0 / NLON)
    finish(main)
    total = received[0, :, :ROWS]
    for source in range(1, LON_DEV):
        total = total + received[source, :, :ROWS]
    total = total * response
    for target in range(LON_DEV):
        send[target, :, :ROWS] = total
        tile = jnp.where(target == (lon + 1) % LON_DEV, tiles[0], tiles[1])
        send[target, :, ROWS:] = tile[:, :64]
    blank = jnp.zeros((HALF, 64), jnp.float32)
    west = received[(lon + LON_DEV - 1) % LON_DEV, :, ROWS:]
    east = received[(lon + 1) % LON_DEV, :, ROWS:]
    edges[0] = jnp.concatenate([west, blank], axis=1)
    edges[1] = jnp.concatenate([east, blank], axis=1)


def gather_terms(value, coeff, south_line, north_line, west_edge, east_edge):
    to_north, to_south = coeff[1] * value, coeff[2] * value
    total = coeff[0] * value
    total = total + jnp.concatenate([south_line, to_north[:-1]], axis=0)
    total = total + jnp.concatenate([to_south[1:], north_line], axis=0)
    total = total + jnp.concatenate([west_edge, (coeff[3] * value)[:, :-1]], axis=1)
    total = total + jnp.concatenate([(coeff[4] * value)[:, 1:], east_edge], axis=1)
    return total, to_north, to_south


def load_coeff(coeff, field, level):
    return [coeff[field, term, level] for term in range(5)]


def one_row(waves, table, row, opposite):
    picked = (iota((ROWS, 128), 0) == iota((ROWS, 128), 1) * BAND + row).astype(jnp.float32)
    chosen = dot(waves, picked, 1, 0)
    if opposite:
        chosen = jnp.where(iota((WAVES, 128), 0) % 2 == 1, -chosen, chosen)
    return dot(chosen, table, 0, 0)


def whole_band(closed, opened, top):
    return jnp.where(
        top, jnp.concatenate([opened, closed], axis=0), jnp.concatenate([closed, opened], axis=0)
    )


def middle_kernel(
    waves_in, table_in, mask_in, state_in, extra_in, coeff_in, opened_in, beyond_in, across_in,
    send, to_next, next_line, edges, middle_out,
    waves, table, mask, state, extra, coeff_ref, opened, beyond, across, middle,
    filtered, opposite, sems,
):
    lon, lat = place()
    top = lat == TOP
    waves_copy, table_copy, *rest = begin(
        sems,
        (waves_in, waves),
        (table_in.at[lon], table),
        (mask_in, mask),
        (state_in, state),
        (extra_in, extra),
        (coeff_in, coeff_ref),
        (opened_in, opened),
        (beyond_in, beyond),
        (across_in, across),
    )
    finish(waves_copy, table_copy)
    flat = waves[:, :, :ROWS].reshape(WAVES, ROWS)
    filtered[...] = dot(flat, table[...], 0, 0)
    polar_row = jnp.where(top, BAND - 1, 0)
    opposite[...] = one_row(flat, table[...], polar_row, True)
    finish(*rest)
    blank = jnp.zeros((HALF, 64), jnp.float32)
    sides = (lon + LON_DEV - 1) % LON_DEV, (lon + 1) % LON_DEV
    for side in range(2):
        closed = jnp.concatenate([waves[sides[side], :, ROWS:], blank], axis=1)
        edges[side] = whole_band(closed, opened[side], top)
    weight = row_weight(mask, 0, (BAND, WIDTH))
    is_filtered = weight[:, 0:1] > 0.5
    next_weight = jnp.where(top, weight[0:1], weight[BAND - 1 :])
    row = iota((BAND, WIDTH), 0)

    def one(slab, carry):
        east_tile, west_tile = carry
        field, level = slab // LEV, slab % LEV
        here = pl.ds(slab, 1)
        value = state[field, level]
        smooth = filtered[pl.ds(slab * BAND, BAND)]
        value = value + weight * (smooth[:, :WIDTH] - value)
        coeff = load_coeff(coeff_ref, field, level)
        west = lane_of(edges[0], slab)
        west = jnp.where(is_filtered, west * smooth[:, WIDTH + 1 : WIDTH + 2], west)
        east = lane_of(edges[1], slab)
        east = jnp.where(is_filtered, east * smooth[:, WIDTH : WIDTH + 1], east)
        halo = beyond[2, here]
        total, north, south = gather_terms(
            value, coeff, jnp.where(top, halo, 0.0), jnp.where(top, 0.0, halo), west, east
        )
        pole = across[here] * opposite[here][:, :WIDTH]
        total = total + jnp.where(row == polar_row, pole, 0.0) + extra[field, level]
        middle[field, level] = total
        product = jnp.where(top, south[0:1], north[BAND - 1 :])
        near = jnp.where(top, total[0:1], total[BAND - 1 :])
        near_coeff = jnp.where(top, coeff[2][0:1], coeff[1][BAND - 1 :])
        to_next[0, here] = product
        to_next[1, here] = (1.0 - next_weight) * near_coeff * near
        to_next[2, here] = next_weight * near_coeff
        next_line[here] = beyond[1, here] * (beyond[0, here] + product)
        column = (coeff[3] * total)[:, WIDTH - 1 :]
        east_tile = with_lane(east_tile, slab, jnp.where(top, column[:HALF], column[HALF:]))
        column = (coeff[4] * total)[:, 0:1]
        west_tile = with_lane(west_tile, slab, jnp.where(top, column[:HALF], column[HALF:]))
        return east_tile, west_tile

    none = jnp.zeros((HALF, 128), jnp.float32)
    east_tile, west_tile = for_slabs(one, (none, none))
    (out_copy,) = begin(sems, (middle, middle_out))
    sums = dot(table[:, :WIDTH], middle[...].reshape(ROWS, WIDTH), 1, 1)
    send[:, :, :ROWS] = sums.reshape(LON_DEV, SHARE, ROWS)
    for target in range(LON_DEV):
        tile = jnp.where(target == (lon + 1) % LON_DEV, east_tile, west_tile)
        send[target, :, ROWS:] = tile[:, :64]
    finish(out_copy)


def final_kernel(
    waves_in, table_in, mask_in, middle_in, coeff_in, edges_in, opened_in, line_in, across_in,
    out,
    waves, table, mask, middle, coeff_ref, edges, opened, next_line, across,
    filtered, opposite, sems,
):
    lon, lat = place()
    top = lat == TOP
    waves_copy, table_copy, *rest = begin(
        sems,
        (waves_in, waves),
        (table_in.at[lon], table),
        (mask_in, mask),
        (middle_in, middle),
        (coeff_in, coeff_ref),
        (edges_in, edges),
        (opened_in, opened),
        (line_in, next_line),
        (across_in, across),
    )
    finish(waves_copy, table_copy)
    flat = waves[:, :, :ROWS].reshape(WAVES, ROWS)
    filtered[...] = dot(flat, table[...], 0, 0)
    polar_row = jnp.where(top, BAND - 1, 0)
    opposite[...] = one_row(flat, table[...], polar_row, True)
    finish(*rest)
    weight = row_weight(mask, 0, (BAND, WIDTH))
    is_filtered = weight[:, 0:1] > 0.5
    row = iota((BAND, WIDTH), 0)
    none = jnp.zeros((HALF, 128), jnp.float32)
    west_band = whole_band(none, opened[0], top)
    east_band = whole_band(none, opened[1], top)

    def one(slab, carry):
        field, level = slab // LEV, slab % LEV
        here = pl.ds(slab, 1)
        value = middle[field, level]
        smooth = filtered[pl.ds(slab * BAND, BAND)]
        value = value + weight * (smooth[:, :WIDTH] - value)
        coeff = load_coeff(coeff_ref, field, level)
        west = lane_of(edges[0], slab) * smooth[:, WIDTH + 1 : WIDTH + 2]
        west = jnp.where(is_filtered, west, lane_of(west_band, slab))
        east = lane_of(edges[1], slab) * smooth[:, WIDTH : WIDTH + 1]
        east = jnp.where(is_filtered, east, lane_of(east_band, slab))
        halo = next_line[here]
        total, _, _ = gather_terms(
            value, coeff, jnp.where(top, halo, 0.0), jnp.where(top, 0.0, halo), west, east
        )
        pole = across[here] * opposite[here][:, :WIDTH]
        out[field, level] = total + jnp.where(row == polar_row, pole, 0.0)
        return carry

    for_slabs(one)


def edge_kernel(field_in, coeff_in, edges, field, to_east, to_west, sems):
    finish(
        *begin(
            sems,
            (field_in, field),
            (coeff_in.at[:, 3], to_east),
            (coeff_in.at[:, 4], to_west),
        )
    )
    east = west = jnp.zeros((BAND, 128), jnp.float32)
    for slab in range(SLABS):
        at = slab // LEV, slab % LEV
        value = field[at]
        east = with_lane(east, slab, (to_east[at] * value)[:, WIDTH - 1 :])
        west = with_lane(west, slab, (to_west[at] * value)[:, 0:1])
    edges[0] = east
    edges[1] = west


def line_kernel(
    field_in, extra_in, coeff_in, west_in, east_in,
    to_north, to_south, to_polar,
    field_ref, extra, coeff_ref, west_edge, east_edge, sems,
):
    _, lat = place()
    finish(
        *begin(
            sems,
            (field_in, field_ref),
            (extra_in, extra),
            (coeff_in, coeff_ref),
            (west_in, west_edge),
            (east_in, east_edge),
        )
    )
    none = jnp.zeros((1, WIDTH), jnp.float32)

    def one(slab, carry):
        field, level = slab // LEV, slab % LEV
        here = pl.ds(slab, 1)
        coeff = load_coeff(coeff_ref, field, level)
        west, east = lane_of(west_edge[...], slab), lane_of(east_edge[...], slab)
        total, north, south = gather_terms(field_ref[field, level], coeff, none, none, west, east)
        total = total + extra[field, level]
        norths = total[BAND - 1 :], coeff[1][BAND - 1 :], north[BAND - 1 :]
        souths = total[0:1], coeff[2][0:1], south[0:1]
        for part in range(3):
            to_north[part, here] = norths[part]
            to_south[part, here] = souths[part]
            to_polar[part, here] = jnp.where(lat == 1, souths[part], norths[part])
        return carry

    for_slabs(one)


def plain_middle_kernel(
    state_in, extra_in, coeff_in, west_in, east_in, below_in, above_in, polar_in,
    edges, lines, middle_out,
    state, extra, coeff_ref, west_edge, east_edge, below, above, polar, middle, sems,
):
    _, lat = place()
    finish(
        *begin(
            sems,
            (state_in, state),
            (extra_in, extra),
            (coeff_in, coeff_ref),
            (west_in, west_edge),
            (east_in, east_edge),
            (below_in, below),
            (above_in, above),
            (polar_in, polar),
        )
    )

    def one(slab, carry):
        east_tile, west_tile = carry
        field, level = slab // LEV, slab % LEV
        here = pl.ds(slab, 1)
        coeff = load_coeff(coeff_ref, field, level)
        west, east = lane_of(west_edge[...], slab), lane_of(east_edge[...], slab)
        reached = polar[0, here]
        total, north, south = gather_terms(
            state[field, level],
            coeff,
            jnp.where(lat == 1, reached, below[2, here]),
            jnp.where(lat == TOP - 1, reached, above[2, here]),
            west,
            east,
        )
        total = total + extra[field, level]
        middle[field, level] = total
        low = below[1, here] * (below[0, here] + south[0:1])
        high = above[1, here] * (above[0, here] + north[BAND - 1 :])
        lines[0, here] = jnp.where(lat == 1, 0.0, low)
        lines[1, here] = jnp.where(lat == TOP - 1, 0.0, high)
        east_tile = with_lane(east_tile, slab, (coeff[3] * total)[:, WIDTH - 1 :])
        west_tile = with_lane(west_tile, slab, (coeff[4] * total)[:, 0:1])
        return east_tile, west_tile

    none = jnp.zeros((BAND, 128), jnp.float32)
    edges[0], edges[1] = for_slabs(one, (none, none))
    finish(*begin(sems, (middle, middle_out)))


def plain_final_kernel(
    middle_in, coeff_in, west_in, east_in, lines_in,
    out,
    middle, coeff_ref, west_edge, east_edge, lines, sems,
):
    finish(
        *begin(
            sems,
            (middle_in, middle),
            (coeff_in, coeff_ref),
            (west_in, west_edge),
            (east_in, east_edge),
            (lines_in, lines),
        )
    )

    def one(slab, carry):
        field, level = slab // LEV, slab % LEV
        here = pl.ds(slab, 1)
        coeff = load_coeff(coeff_ref, field, level)
        west, east = lane_of(west_edge[...], slab), lane_of(east_edge[...], slab)
        value = middle[field, level]
        out[field, level] = gather_terms(value, coeff, lines[0, here], lines[1, here], west, east)[0]
        return carry

    for_slabs(one)


def reach_kernel(result_in, waves_in, table_in, polar_in, result_out, part, waves, table, polar, sems):
    lon, lat = place()
    next_to = (lat == 1) | (lat == TOP - 1)
    bottom = lat == 1
    rows = pl.ds(pl.multiple_of(jnp.where(bottom, 0, HALF), HALF), HALF)

    @pl.when(next_to)
    def _():
        finish(
            *begin(
                sems,
                (result_in.at[:, :, rows], part),
                (waves_in, waves),
                (table_in.at[lon], table),
                (polar_in, polar),
            )
        )
        flat = waves[:, :, :ROWS].reshape(WAVES, ROWS)
        smooth = one_row(flat, table[...], jnp.where(bottom, BAND - 1, 0), False)
        line = polar[1] + polar[2] * smooth[:SLABS, :WIDTH]
        row = iota((HALF, WIDTH), 0)
        mine = row == jnp.where(bottom, 0, HALF - 1)
        for slab in range(SLABS):
            at = slab // LEV, slab % LEV
            part[at] = part[at] + jnp.where(mine, line[slab : slab + 1], 0.0)
        finish(*begin(sems, (part, result_out.at[:, :, rows])))


def exchanged(chunks):
    return lax.all_to_all(chunks, "lon", split_axis=0, concat_axis=0, tiled=True)


def moved(value, lats, north, east):
    pairs = []
    for lat, lon in [(lat, lon) for lat in lats for lon in range(LON_DEV)]:
        pairs.append((lat * LON_DEV + lon, (lat + north) * LON_DEV + (lon + east) % LON_DEV))
    return lax.ppermute(value, ("lat", "lon"), pairs)


def next_to_pole(value, outward):
    pairs = []
    for lon in range(LON_DEV):
        for polar, other in ((0, 1), (TOP, TOP - 1)):
            pair = polar * LON_DEV + lon, other * LON_DEV + lon
            pairs.append(pair if outward else pair[::-1])
    return lax.ppermute(value, ("lat", "lon"), pairs)


def local(adjoint_state, innovation, coefficients, polar_mask, wave_cutoff):
    lat = lax.axis_index("lat")
    polar = (lat == 0) | (lat == TOP)
    table = jnp.asarray(wave_tables())
    small = pltpu.SMEM((BAND,), jnp.int32)
    plain = range(1, TOP)
    table_scratch = in_vmem((WAVES, WIDE))
    wave_scratch = [in_vmem((ROWS, WIDE)), in_vmem((128, WIDE))]
    one_edge = (BAND, 128)

    def blanks(*shapes):
        return tuple(jnp.zeros(shape, jnp.float32) for shape in shapes)

    def polar_first():
        half = in_vmem(HALF_FIELD)
        send, to_polar, to_north, to_south, edge = launch(
            forward_kernel_with_blanks,
            [adjoint_state, coefficients, table, polar_mask],
            [CHUNKS],
            [LINES, LINES, LINES, (2, *one_edge)],
            [in_vmem(FIELD), table_scratch, half, half, small],
            copies=5,
        )
        received = exchanged(send)
        cross, tiles = launch(
            across_kernel, [coefficients], [LINE, TILES], (), [half, half, half], copies=3
        )
        across = moved(cross, (0, TOP), 0, LON_DEV // 2)
        return received, across, tiles, to_polar, to_north, to_south, edge

    def plain_first():
        (edges,) = launch(
            edge_kernel,
            [adjoint_state, coefficients],
            [(2, *one_edge)],
            (),
            [in_vmem(FIELD)] * 3,
            copies=3,
        )
        west = moved(edges[0], plain, 0, 1)
        east = moved(edges[1], plain, 0, -1)
        to_north, to_south, to_polar = launch(
            line_kernel,
            [adjoint_state, innovation, coefficients, west, east],
            [LINES, LINES, LINES],
            (),
            [in_vmem(FIELD), in_vmem(FIELD), in_vmem(COEFF), in_vmem(one_edge), in_vmem(one_edge)],
            copies=5,
        )
        received, across, tiles = blanks(CHUNKS, LINE, TILES)
        return received, across, tiles, to_polar, to_north, to_south, jnp.stack([west, east])

    received, across, tiles, to_polar, to_north, to_south, edge = lax.cond(
        polar, polar_first, plain_first
    )
    beyond = next_to_pole(to_polar, False)

    def respond(received):
        return launch(
            respond_kernel,
            [received, wave_cutoff, tiles],
            [CHUNKS, TILES],
            (),
            [in_vmem(CHUNKS), small, in_vmem(TILES)],
            copies=3,
        )

    def polar_second():
        send, opened = respond(received)
        return exchanged(send), opened, to_north, to_south

    def plain_second():
        below = moved(to_north, range(1, TOP - 1), 1, 0)
        above = moved(to_south, range(2, TOP), -1, 0)
        return *blanks(CHUNKS, TILES), below, above

    waves, opened, below, above = lax.cond(polar, polar_second, plain_second)

    def polar_third():
        return tuple(launch(
            middle_kernel,
            [waves, table, polar_mask, adjoint_state, innovation, coefficients, opened, beyond, across],
            [CHUNKS, LINES, LINE, EDGES],
            [FIELD],
            [in_vmem(CHUNKS), table_scratch, small, in_vmem(FIELD), in_vmem(FIELD), in_vmem(COEFF)]
            + [in_vmem(TILES), in_vmem(LINES), in_vmem(LINE), in_vmem(FIELD), *wave_scratch],
            copies=9,
        ))

    def plain_third():
        return blanks(CHUNKS, LINES, LINE, EDGES, FIELD)

    send, to_next, next_line, edges, middle = lax.cond(polar, polar_third, plain_third)
    reached = next_to_pole(to_next, True)

    def polar_fourth():
        received = exchanged(send)
        again, opened = respond(received)
        return exchanged(again), opened, middle

    def plain_fourth():
        west, east = edge[0], edge[1]
        second, lines, middle = launch(
            plain_middle_kernel,
            [adjoint_state, innovation, coefficients, west, east, below, above, reached],
            [(2, *one_edge), (2, *LINE)],
            [FIELD],
            [in_vmem(FIELD), in_vmem(FIELD), in_vmem(COEFF), in_vmem(one_edge), in_vmem(one_edge)]
            + [in_vmem(LINES), in_vmem(LINES), in_vmem(LINES), in_vmem(FIELD)],
            copies=8,
        )
        west = moved(second[0], plain, 0, 1)
        east = moved(second[1], plain, 0, -1)
        (result,) = launch(
            plain_final_kernel,
            [middle, coefficients, west, east, lines],
            [FIELD],
            (),
            [in_vmem(FIELD), in_vmem(COEFF), in_vmem(one_edge), in_vmem(one_edge), in_vmem((2, *LINE))],
            copies=5,
        )
        return *blanks(CHUNKS, TILES), result

    waves, opened, result = lax.cond(polar, polar_fourth, plain_fourth)
    waves_beyond = next_to_pole(waves, True)

    def polar_fifth():
        (out,) = launch(
            final_kernel,
            [waves, table, polar_mask, result, coefficients, edges, opened, next_line, across],
            [FIELD],
            (),
            [in_vmem(CHUNKS), table_scratch, small, in_vmem(FIELD), in_vmem(COEFF), in_vmem(EDGES)]
            + [in_vmem(TILES), in_vmem(LINE), in_vmem(LINE), *wave_scratch],
            copies=9,
        )
        return out

    def plain_fifth():
        (out,) = launch(
            reach_kernel,
            [result, waves_beyond, table, reached],
            (),
            [FIELD],
            [in_vmem(HALF_FIELD), in_vmem(CHUNKS), table_scratch, in_vmem(LINES)],
            copies=4,
            aliases={0: 0},
        )
        return out

    return lax.cond(polar, polar_fifth, plain_fifth)


def forward_kernel_with_blanks(*refs):
    forward_kernel(*refs[:5], *refs[9:])


def solution(mesh):
    return jax.shard_map(
        local,
        mesh=mesh,
        in_specs=(
            P(None, None, "lat", "lon"),
            P(None, None, "lat", "lon"),
            P(None, None, None, "lat", "lon"),
            P("lat"),
            P("lat"),
        ),
        out_specs=P(None, None, "lat", "lon"),
        check_vma=False,
    )
```

profile of v0, /device:TPU:8, one launch (start us, length us, event | category | flops | bytes accessed | tf_op | source)
XLA Modules:
  0.0 82.8 jit_solution(15368950521446133193)
XLA Ops:
  0.0 0.0 copy-start.5
  0.0 19.9 %conditional.5 = (f32[16,8,640]{2,1,0:T(8,128)}, f32[36,360]{1,0:T(8,128)}, f32[2,8,128]{2,1,0:T(8,128)S(1)}, f32[3,36,360]{2,1,0:T(8,128)S(1)}, f32[3,36,360]{2...) conditional(s32[]{:T(128)} %convert_element_type.2, (f32[3,12,16,360]{3,2,1,0:T(8,128)}, ...), branch_computations={%region_0.0_spmd, %region_1.0_spmd} | conditional | flops 4096 | bytes 31707596 | solution.py:612
  0.0 3.2 %branch_1_fun.6 = (f32[16,8,640]{2,1,0:T(8,128)}, f32[3,36,360]{2,1,0:T(8,128)S(1)}, f32[3,36,360]{2,1,0:T(8,128)S(1)}, f32[3,36,360]{2,1,0:T(8,128)S(1)}, f32[2,16,128]{2,1,0:T(8,128)S(1)}) custom-call(f32[3,12,16,360]{3,2,1,0:T(8,128)} %get-tuple-element.108.refs_0_, f32[3,5,12,16,360]{4,3,2,1,0:T(8,128)} %get-tuple-element.109.refs_1_.coeff_in, ...), custom_call_target="tpu_custom_call" | custom-call | bytes 8933056 | tf_op jit(solution)/shard_map/cond/branch_1_fun/pallas_call | solution.py:70
  3.3 7.4 %all-to-all-start = ((f32[16,8,640]{2,1,0:T(8,128)}), f32[16,8,640]{2,1,0:T(8,128)}, u32[]{:S(2)}, u32[]{:S(2)}) async-start(f32[16,8,640]{2,1,0:T(8,128)} %get-tuple-element.112), calls=%async_computation | async-start | bytes 655360 | tf_op jit(solution)/shard_map/cond/branch_1_fun/all_to_all | solution.py:541
  10.7 1.5 %branch_1_fun.7 = (f32[36,360]{1,0:T(8,128)S(1)}, f32[2,8,128]{2,1,0:T(8,128)S(1)}) custom-call(f32[3,5,12,16,360]{4,3,2,1,0:T(8,128)} %get-tuple-element.109.refs_1_.coeff_in), custom_call_target="tpu_custom_call" | custom-call | bytes 4207232 | tf_op jit(solution)/shard_map/cond/branch_1_fun/pallas_call | solution.py:70
  12.1 4.9 %collective-permute-start = (f32[36,360]{1,0:T(8,128)S(1)}, f32[36,360]{1,0:T(8,128)}, u32[]{:S(2)}, u32[]{:S(2)}) collective-permute-start(f32[36,360]{1,0:T(8,128)S(1)} %get-tuple-element.113), channel_id=1, source_target_pairs={{0,8},{1,9},{2,10},{3,11},{4,12},{5,13},{6,14},{7,15},{8,0},{9,1},... | collective-permute-start | bytes 155528 | tf_op jit(solution)/shard_map/cond/branch_1_fun/ppermute | solution.py:548
  17.0 2.8 %collective-permute-done = f32[36,360]{1,0:T(8,128)} collective-permute-done((f32[36,360]{1,0:T(8,128)S(1)}, f32[36,360]{1,0:T(8,128)}, u32[]{:S(2)}, u32[]{:S(2)}) %collective-permute-start) | collective-permute-done | bytes 51872 | tf_op jit(solution)/shard_map/cond/branch_1_fun/ppermute | solution.py:548
  19.9 0.0 all-to-all-done
  19.9 1.3 %collective-permute-start.7 = (f32[3,36,360]{2,1,0:T(8,128)S(1)}, f32[3,36,360]{2,1,0:T(8,128)S(1)}, u32[]{:S(2)}, u32[]{:S(2)}) collective-permute-start(f32[3,36,360]{2,1,0:T(8,128)S(1)} %get-tuple-element.194), channel_id=1, source_target_pairs={{16,0},{224,240},{17,1},{225,241},{18,2},{226,242},{19,3},{227,243... | collective-permute-start | bytes 466568 | tf_op jit(solution)/shard_map/ppermute | solution.py:557
  21.1 0.0 copy-done.5
  21.2 16.5 %conditional.6 = (f32[16,8,640]{2,1,0:T(8,128)}, f32[2,8,128]{2,1,0:T(8,128)S(1)}, f32[3,36,360]{2,1,0:T(8,128)S(1)}, f32[3,36,360]{2,1,0:T(8,128)S(1)}) conditional(s32[]{:T(128)} %convert_element_type.2, (f32[3,36,360]{2,1,0:T(8,128)S(1)}, f32[3,36,360]{2,1,0:T(8,128)S(1)}) %tuple.44, (f32[16,8,640]{2,1,0:T(8,128)}, s32[16]{0:T(128)S(1)}, ...), branch_computations={%region_2.0_spmd, %region_3.0_spmd} | conditional | bytes 2276992 | solution.py:636
  21.2 1.8 %branch_1_fun.8 = (f32[16,8,640]{2,1,0:T(8,128)}, f32[2,8,128]{2,1,0:T(8,128)S(1)}) custom-call(f32[16,8,640]{2,1,0:T(8,128)} %get-tuple-element.121.received_in, s32[16]{0:T(128)S(1)} %get-tuple-element.122.cutoff_in, f32[2,8,128]{2,1,0:T(8,128)S(1)} %get-tuple-element.123.tiles_in), custom_call_target="tpu_custom_call" | custom-call | bytes 671808 | tf_op jit(solution)/shard_map/cond/branch_1_fun/pallas_call | solution.py:70
  23.0 7.2 %all-to-all-start.1 = ((f32[16,8,640]{2,1,0:T(8,128)}), f32[16,8,640]{2,1,0:T(8,128)}, u32[]{:S(2)}, u32[]{:S(2)}) async-start(f32[16,8,640]{2,1,0:T(8,128)} %get-tuple-element.124), calls=%async_computation.1 | async-start | bytes 655360 | tf_op jit(solution)/shard_map/cond/branch_1_fun/all_to_all | solution.py:541
  30.3 7.4 %all-to-all-done.1 = f32[16,8,640]{2,1,0:T(8,128)} async-done(((f32[16,8,640]{2,1,0:T(8,128)}), f32[16,8,640]{2,1,0:T(8,128)}, u32[]{:S(2)}, u32[]{:S(2)}) %all-to-all-start.1) | async-done | bytes 327712 | tf_op jit(solution)/shard_map/cond/branch_1_fun/all_to_all | solution.py:541
  37.6 0.0 collective-permute-done.7
  37.6 7.7 %conditional.7 = ((f32[16,8,640]{2,1,0:T(8,128)S(1)}, f32[3,36,360]{2,1,0:T(8,128)S(1)}, f32[36,360]{1,0:T(8,128)S(1)}, f32[2,16,128]{2,1,0:T(8,128)S(1)}, f32[3,12,16,360]{3,2,1,0:T(8,128)S(1)})) conditional(s32[]{:T(128)} %convert_element_type.2, () %tuple.46, (f32[16,8,640]{2,1,0:T(8,128)}, f32[16,128,384]{2,1,0:T(8,128)}, s32[16]{0:T(128)}, ...), branch_computations={%region_4.0_spmd, %region_5.0_spmd} | conditional | bytes 10875976 | solution.py:652
  37.6 7.7 %branch_1_fun.9 = (f32[16,8,640]{2,1,0:T(8,128)S(1)}, f32[3,36,360]{2,1,0:T(8,128)S(1)}, f32[36,360]{1,0:T(8,128)S(1)}, f32[2,16,128]{2,1,0:T(8,128)S(1)}, f32[3,12,16,360]{3,2,1,0:T(8,128)S(1)}) custom-call(f32[16,8,640]{2,1,0:T(8,128)} %get-tuple-element.128.waves_in, f32[16,128,384]{2,1,0:T(8,128)} %get-tuple-element.129.table_in, ...), custom_call_target="tpu_custom_call" | custom-call | bytes 10875968 | tf_op jit(solution)/shard_map/cond/branch_1_fun/pallas_call | solution.py:70
  45.3 1.3 %collective-permute-start.8 = (f32[3,36,360]{2,1,0:T(8,128)S(1)}, f32[3,36,360]{2,1,0:T(8,128)S(1)}, u32[]{:S(2)}, u32[]{:S(2)}) collective-permute-start(f32[3,36,360]{2,1,0:T(8,128)S(1)} %get-tuple-element.196), channel_id=1, source_target_pairs={{0,16},{240,224},{1,17},{241,225},{2,18},{242,226},{3,19},{243,227... | collective-permute-start | bytes 466568 | tf_op jit(solution)/shard_map/ppermute | solution.py:557
  46.6 1.0 %collective-permute-done.8 = f32[3,36,360]{2,1,0:T(8,128)S(1)} collective-permute-done((f32[3,36,360]{2,1,0:T(8,128)S(1)}, f32[3,36,360]{2,1,0:T(8,128)S(1)}, u32[]{:S(2)}, u32[]{:S(2)}) %collective-permute-start.8) | collective-permute-done | bytes 155552 | tf_op jit(solution)/shard_map/ppermute | solution.py:557
  47.7 0.0 copy-start.4
  47.7 25.5 %conditional.8 = (f32[16,8,640]{2,1,0:T(8,128)S(1)}, f32[2,8,128]{2,1,0:T(8,128)S(1)}, f32[3,12,16,360]{3,2,1,0:T(8,128)S(1)}) conditional(s32[]{:T(128)} %convert_element_type.2, (f32[2,16,128]{2,1,0:T(8,128)S(1)}, f32[3,12,16,360]{3,2,1,0:T(8,128)}, f32[3,12,16,360]{3,2,1,0:T(8,128)}, f32[3,5,12,16,360]{4,3,2,1,0:T(8,128)}, ...), branch_computations={%region_6.0_spmd, %region_7.0_spmd} | conditional | bytes 30220556 | solution.py:683
  47.7 12.4 %all_to_all.16.received_in = f32[16,8,640]{2,1,0:T(8,128)S(1)} all-to-all(f32[16,8,640]{2,1,0:T(8,128)S(1)} %get-tuple-element.147), channel_id=1, replica_groups=mesh['lat'=16,'lon'=16] {'lon'}, dimensions={0} | all-to-all | bytes 655360 | tf_op jit(solution)/shard_map/cond/branch_1_fun/all_to_all | solution.py:541
  60.1 0.8 branch_1_fun.10
  60.9 12.3 %all_to_all.17 = f32[16,8,640]{2,1,0:T(8,128)S(1)} all-to-all(f32[16,8,640]{2,1,0:T(8,128)S(1)} %get-tuple-element.150), channel_id=1, replica_groups=mesh['lat'=16,'lon'=16] {'lon'}, dimensions={0} | all-to-all | bytes 655360 | tf_op jit(solution)/shard_map/cond/branch_1_fun/all_to_all | solution.py:541
  73.2 1.3 %collective-permute-start.9 = (f32[16,8,640]{2,1,0:T(8,128)S(1)}, f32[16,8,640]{2,1,0:T(8,128)S(1)}, u32[]{:S(2)}, u32[]{:S(2)}) collective-permute-start(f32[16,8,640]{2,1,0:T(8,128)S(1)} %get-tuple-element.200), channel_id=1, source_target_pairs={{0,16},{240,224},{1,17},{241,225},{2,18},{242,226},{3,19},{243,227... | collective-permute-start | bytes 983048 | tf_op jit(solution)/shard_map/ppermute | solution.py:557
  74.5 1.2 %collective-permute-done.9 = f32[16,8,640]{2,1,0:T(8,128)S(1)} collective-permute-done((f32[16,8,640]{2,1,0:T(8,128)S(1)}, f32[16,8,640]{2,1,0:T(8,128)S(1)}, u32[]{:S(2)}, u32[]{:S(2)}) %collective-permute-start.9) | collective-permute-done | bytes 327712 | tf_op jit(solution)/shard_map/ppermute | solution.py:557
  75.7 0.0 copy-done.4
  75.7 6.2 %conditional.9 = (f32[3,12,16,360]{3,2,1,0:T(8,128)S(1)}) conditional(s32[]{:T(128)} %convert_element_type.2, (f32[3,12,16,360]{3,2,1,0:T(8,128)S(1)}, f32[16,8,640]{2,1,0:T(8,128)S(1)}, f32[16,128,384]{2,1,0:T(8,128)}, f32[3,36,360]{2,1,0:T(8,128)S(1)}) %tuple.50, (f32[16,8,640]{2,1,0:T(8,128)S(1)}, f32[16,128,384]{2,1,0:T(8,128)}, s32[16]{0:T(128)S(1)}, ...), branch_computations={%region_8.0_spmd, %region_9.0_spmd} | conditional | bytes 11066696 | solution.py:710
  75.7 0.1 copy.52.middle_in
  75.8 6.1 %branch_1_fun.11 = f32[3,12,16,360]{3,2,1,0:T(8,128)S(1)} custom-call(f32[16,8,640]{2,1,0:T(8,128)S(1)} %get-tuple-element.157.waves_in, f32[16,128,384]{2,1,0:T(8,128)} %get-tuple-element.158.table_in, s32[16]{0:T(128)S(1)} %get-tuple-element.159.mask_in, f32[3,12,16,360]{3,2,1,0:T(8,128)S(1)} %copy.52.middle_in, ...), custom_call_target="tpu_custom_call" | custom-call | bytes 9407808 | tf_op jit(solution)/shard_map/cond/branch_1_fun/pallas_call | solution.py:70
  81.9 0.0 copy-start.3
  81.9 0.9 %copy-done.3 = f32[3,12,16,360]{3,2,1,0:T(8,128)} copy-done((f32[3,12,16,360]{3,2,1,0:T(8,128)}, f32[3,12,16,360]{3,2,1,0:T(8,128)S(1)}, u32[]{:S(2)}) %copy-start.3) | copy-done | bytes 829464
  (2 shorter events, 0.0 us)
Async XLA Ops:
  0.0 21.1 %copy-start.5 = (s32[16]{0:T(128)S(1)}, s32[16]{0:T(128)}, u32[]{:S(2)}) copy-start(s32[16]{0:T(128)} %param.20) | copy-start | bytes 196
  3.3 16.6 %all-to-all-start = ((f32[16,8,640]{2,1,0:T(8,128)}), f32[16,8,640]{2,1,0:T(8,128)}, u32[]{:S(2)}, u32[]{:S(2)}) async-start(f32[16,8,640]{2,1,0:T(8,128)} %get-tuple-element.112), calls=%async_computation | async-start | bytes 655360 | tf_op jit(solution)/shard_map/cond/branch_1_fun/all_to_all | solution.py:541
  12.1 7.7 %collective-permute-start = (f32[36,360]{1,0:T(8,128)S(1)}, f32[36,360]{1,0:T(8,128)}, u32[]{:S(2)}, u32[]{:S(2)}) collective-permute-start(f32[36,360]{1,0:T(8,128)S(1)} %get-tuple-element.113), channel_id=1, source_target_pairs={{0,8},{1,9},{2,10},{3,11},{4,12},{5,13},{6,14},{7,15},{8,0},{9,1},... | collective-permute-start | bytes 155528 | tf_op jit(solution)/shard_map/cond/branch_1_fun/ppermute | solution.py:548
  19.9 17.8 %collective-permute-start.7 = (f32[3,36,360]{2,1,0:T(8,128)S(1)}, f32[3,36,360]{2,1,0:T(8,128)S(1)}, u32[]{:S(2)}, u32[]{:S(2)}) collective-permute-start(f32[3,36,360]{2,1,0:T(8,128)S(1)} %get-tuple-element.194), channel_id=1, source_target_pairs={{16,0},{224,240},{17,1},{225,241},{18,2},{226,242},{19,3},{227,243... | collective-permute-start | bytes 466568 | tf_op jit(solution)/shard_map/ppermute | solution.py:557
  23.0 14.6 %all-to-all-start.1 = ((f32[16,8,640]{2,1,0:T(8,128)}), f32[16,8,640]{2,1,0:T(8,128)}, u32[]{:S(2)}, u32[]{:S(2)}) async-start(f32[16,8,640]{2,1,0:T(8,128)} %get-tuple-element.124), calls=%async_computation.1 | async-start | bytes 655360 | tf_op jit(solution)/shard_map/cond/branch_1_fun/all_to_all | solution.py:541
  45.3 2.3 %collective-permute-start.8 = (f32[3,36,360]{2,1,0:T(8,128)S(1)}, f32[3,36,360]{2,1,0:T(8,128)S(1)}, u32[]{:S(2)}, u32[]{:S(2)}) collective-permute-start(f32[3,36,360]{2,1,0:T(8,128)S(1)} %get-tuple-element.196), channel_id=1, source_target_pairs={{0,16},{240,224},{1,17},{241,225},{2,18},{242,226},{3,19},{243,227... | collective-permute-start | bytes 466568 | tf_op jit(solution)/shard_map/ppermute | solution.py:557
  47.7 28.0 %copy-start.4 = (s32[16]{0:T(128)S(1)}, s32[16]{0:T(128)}, u32[]{:S(2)}) copy-start(s32[16]{0:T(128)} %param.19) | copy-start | bytes 196
  73.2 2.5 %collective-permute-start.9 = (f32[16,8,640]{2,1,0:T(8,128)S(1)}, f32[16,8,640]{2,1,0:T(8,128)S(1)}, u32[]{:S(2)}, u32[]{:S(2)}) collective-permute-start(f32[16,8,640]{2,1,0:T(8,128)S(1)} %get-tuple-element.200), channel_id=1, source_target_pairs={{0,16},{240,224},{1,17},{241,225},{2,18},{242,226},{3,19},{243,227... | collective-permute-start | bytes 983048 | tf_op jit(solution)/shard_map/ppermute | solution.py:557
  81.9 0.9 %copy-start.3 = (f32[3,12,16,360]{3,2,1,0:T(8,128)}, f32[3,12,16,360]{3,2,1,0:T(8,128)S(1)}, u32[]{:S(2)}) copy-start(f32[3,12,16,360]{3,2,1,0:T(8,128)S(1)} %get-tuple-element.258) | copy-start | bytes 2488324
where the time goes:
time: 83.3 us; the launch traced here: 82.8 us
  blocking collectives  24.7 us (30%)
  starting transfers between devices  23.4 us (28%)
  Pallas kernels  21.1 us (25%)
  waiting for transfers between devices  12.5 us (15%)
  local copies, waits for them, and re-layouts  1 us (1%)
    all_to_all x2, blocking collectives, exchanged(): lax.all_to_all(chunks, 'lon', split_axis=0, concat_axis=0, tiled=True)  24.7 us
    pallas_call x6, Pallas kernels, launch(): pl.pallas_call(kernel, in_specs=[pl.BlockSpec(memory_space=pltpu.HBM)] *...  21.1 us
    all_to_all x2, starting transfers between devices, exchanged(): lax.all_to_all(chunks, 'lon', split_axis=0, concat_axis=0, tiled=True)  14.6 us
    all_to_all x2, waiting for transfers between devices, exchanged(): lax.all_to_all(chunks, 'lon', split_axis=0, concat_axis=0, tiled=True)  7.37 us
    ppermute x1, starting transfers between devices, moved(): return lax.ppermute(value, ('lat', 'lon'), pairs)  4.88 us
    ppermute x3, starting transfers between devices, next_to_pole(): return lax.ppermute(value, ('lat', 'lon'), pairs)  3.88 us
    ppermute x1, waiting for transfers between devices, moved(): return lax.ppermute(value, ('lat', 'lon'), pairs)  2.84 us
    ppermute x3, waiting for transfers between devices, next_to_pole(): return lax.ppermute(value, ('lat', 'lon'), pairs)  2.25 us
  transfers between devices with their start and end apart: 6, of which 4 were waited for; matrix products, arithmetic and copies ran while one was open for 0% of the time, Pallas kernels for 4%

commit v1 on v0

--- a/solution.py
+++ b/solution.py
@@ -23,8 +23,7 @@
 SLABS = FIELDS * LEV
 ROWS = SLABS * BAND
 SHARE = WAVES // LON_DEV
-UNROLL = 6
-HIGHEST = lax.Precision.HIGHEST
+UNROLL = 4
 
 FIELD = (FIELDS, LEV, BAND, WIDTH)
 HALF_FIELD = (FIELDS, LEV, HALF, WIDTH)
@@ -45,14 +44,22 @@
     return np.pad(both, ((0, 0), (0, 0), (0, WIDE - WIDTH - 2))).astype(np.float32)
 
 
+def split(value):
+    high = value.astype(jnp.bfloat16)
+    return high, (value - high.astype(jnp.float32)).astype(jnp.bfloat16)
+
+
+def pair_dot(left, right, left_dim, right_dim):
+    return lax.dot_general(
+        left, right, (((left_dim,), (right_dim,)), ((), ())), preferred_element_type=jnp.float32
+    )
+
+
 def dot(left, right, left_dim, right_dim):
-    return lax.dot_general(
-        left,
-        right,
-        (((left_dim,), (right_dim,)), ((), ())),
-        precision=HIGHEST,
-        preferred_element_type=jnp.float32,
-    )
+    (left_high, left_low), (right_high, right_low) = split(left), split(right)
+    total = pair_dot(left_high, right_low, left_dim, right_dim)
+    total = total + pair_dot(left_low, right_high, left_dim, right_dim)
+    return total + pair_dot(left_high, right_high, left_dim, right_dim)
 
 
 def iota(shape, dim):
@@ -89,18 +96,28 @@
     return started
 
 
+def by_field(*pairs):
+    return [(source.at[field], target.at[field]) for field in range(FIELDS) for source, target in pairs]
+
+
 def finish(*started):
     for copy in started:
         copy.wait()
 
 
+def for_levels(field, one, carry=0):
+    def some(step, carry):
+        for level in range(UNROLL):
+            carry = one(field, step * UNROLL + level, carry)
+        return carry
+
+    return lax.fori_loop(0, LEV // UNROLL, some, carry)
+
+
 def for_slabs(one, carry=0):
-    def some(step, carry):
-        for slab in range(UNROLL):
-            carry = one(step * UNROLL + slab, carry)
-        return carry
-
-    return lax.fori_loop(0, SLABS // UNROLL, some, carry)
+    for field in range(FIELDS):
+        carry = for_levels(field, one, carry)
+    return carry
 
 
 def lane_of(tile, slab):
@@ -229,8 +246,10 @@
 
 
 def one_row(waves, table, row, opposite):
-    picked = (iota((ROWS, 128), 0) == iota((ROWS, 128), 1) * BAND + row).astype(jnp.float32)
-    chosen = dot(waves, picked, 1, 0)
+    picked = iota((ROWS, 128), 0) == iota((ROWS, 128), 1) * BAND + row
+    picked = picked.astype(jnp.float32).astype(jnp.bfloat16)
+    high, low = split(waves)
+    chosen = pair_dot(high, picked, 1, 0) + pair_dot(low, picked, 1, 0)
     if opposite:
         chosen = jnp.where(iota((WAVES, 128), 0) % 2 == 1, -chosen, chosen)
     return dot(chosen, table, 0, 0)
@@ -255,13 +274,12 @@
         (waves_in, waves),
         (table_in.at[lon], table),
         (mask_in, mask),
-        (state_in, state),
-        (extra_in, extra),
-        (coeff_in, coeff_ref),
         (opened_in, opened),
         (beyond_in, beyond),
         (across_in, across),
-    )
+        *by_field((state_in, state), (extra_in, extra), (coeff_in, coeff_ref)),
+    )
+    rest, fields = rest[:4], rest[4:]
     finish(waves_copy, table_copy)
     flat = waves[:, :, :ROWS].reshape(WAVES, ROWS)
     filtered[...] = dot(flat, table[...], 0, 0)
@@ -278,9 +296,9 @@
     next_weight = jnp.where(top, weight[0:1], weight[BAND - 1 :])
     row = iota((BAND, WIDTH), 0)
 
-    def one(slab, carry):
+    def one(field, level, carry):
         east_tile, west_tile = carry
-        field, level = slab // LEV, slab % LEV
+        slab = field * LEV + level
         here = pl.ds(slab, 1)
         value = state[field, level]
         smooth = filtered[pl.ds(slab * BAND, BAND)]
@@ -311,20 +329,24 @@
         return east_tile, west_tile
 
     none = jnp.zeros((HALF, 128), jnp.float32)
-    east_tile, west_tile = for_slabs(one, (none, none))
-    (out_copy,) = begin(sems, (middle, middle_out))
+    carry, stored = (none, none), []
+    for field in range(FIELDS):
+        finish(*fields[3 * field : 3 * field + 3])
+        carry = for_levels(field, one, carry)
+        stored += begin(sems.at[field : field + 1], (middle.at[field], middle_out.at[field]))
+    east_tile, west_tile = carry
     sums = dot(table[:, :WIDTH], middle[...].reshape(ROWS, WIDTH), 1, 1)
     send[:, :, :ROWS] = sums.reshape(LON_DEV, SHARE, ROWS)
     for target in range(LON_DEV):
         tile = jnp.where(target == (lon + 1) % LON_DEV, east_tile, west_tile)
         send[target, :, ROWS:] = tile[:, :64]
-    finish(out_copy)
+    finish(*stored)
 
 
 def final_kernel(
     waves_in, table_in, mask_in, middle_in, coeff_in, edges_in, opened_in, line_in, across_in,
     out,
-    waves, table, mask, middle, coeff_ref, edges, opened, next_line, across,
+    waves, table, mask, middle, coeff_ref, edges, opened, next_line, across, result,
     filtered, opposite, sems,
 ):
     lon, lat = place()
@@ -334,13 +356,13 @@
         (waves_in, waves),
         (table_in.at[lon], table),
         (mask_in, mask),
-        (middle_in, middle),
-        (coeff_in, coeff_ref),
         (edges_in, edges),
         (opened_in, opened),
         (line_in, next_line),
         (across_in, across),
-    )
+        *by_field((middle_in, middle), (coeff_in, coeff_ref)),
+    )
+    rest, fields = rest[:5], rest[5:]
     finish(waves_copy, table_copy)
     flat = waves[:, :, :ROWS].reshape(WAVES, ROWS)
     filtered[...] = dot(flat, table[...], 0, 0)
@@ -354,8 +376,8 @@
     west_band = whole_band(none, opened[0], top)
     east_band = whole_band(none, opened[1], top)
 
-    def one(slab, carry):
-        field, level = slab // LEV, slab % LEV
+    def one(field, level, carry):
+        slab = field * LEV + level
         here = pl.ds(slab, 1)
         value = middle[field, level]
         smooth = filtered[pl.ds(slab * BAND, BAND)]
@@ -370,10 +392,15 @@
             value, coeff, jnp.where(top, halo, 0.0), jnp.where(top, 0.0, halo), west, east
         )
         pole = across[here] * opposite[here][:, :WIDTH]
-        out[field, level] = total + jnp.where(row == polar_row, pole, 0.0)
+        result[field, level] = total + jnp.where(row == polar_row, pole, 0.0)
         return carry
 
-    for_slabs(one)
+    stored = []
+    for field in range(FIELDS):
+        finish(*fields[2 * field : 2 * field + 2])
+        for_levels(field, one)
+        stored += begin(sems.at[field : field + 1], (result.at[field], out.at[field]))
+    finish(*stored)
 
 
 def edge_kernel(field_in, coeff_in, edges, field, to_east, to_west, sems):
@@ -413,8 +440,8 @@
     )
     none = jnp.zeros((1, WIDTH), jnp.float32)
 
-    def one(slab, carry):
-        field, level = slab // LEV, slab % LEV
+    def one(field, level, carry):
+        slab = field * LEV + level
         here = pl.ds(slab, 1)
         coeff = load_coeff(coeff_ref, field, level)
         west, east = lane_of(west_edge[...], slab), lane_of(east_edge[...], slab)
@@ -451,9 +478,9 @@
         )
     )
 
-    def one(slab, carry):
+    def one(field, level, carry):
         east_tile, west_tile = carry
-        field, level = slab // LEV, slab % LEV
+        slab = field * LEV + level
         here = pl.ds(slab, 1)
         coeff = load_coeff(coeff_ref, field, level)
         west, east = lane_of(west_edge[...], slab), lane_of(east_edge[...], slab)
@@ -497,8 +524,8 @@
         )
     )
 
-    def one(slab, carry):
-        field, level = slab // LEV, slab % LEV
+    def one(field, level, carry):
+        slab = field * LEV + level
         here = pl.ds(slab, 1)
         coeff = load_coeff(coeff_ref, field, level)
         west, east = lane_of(west_edge[...], slab), lane_of(east_edge[...], slab)
@@ -570,6 +597,16 @@
     def blanks(*shapes):
         return tuple(jnp.zeros(shape, jnp.float32) for shape in shapes)
 
+    def respond(received, tiles):
+        return launch(
+            respond_kernel,
+            [received, wave_cutoff, tiles],
+            [CHUNKS, TILES],
+            (),
+            [in_vmem(CHUNKS), small, in_vmem(TILES)],
+            copies=3,
+        )
+
     def polar_first():
         half = in_vmem(HALF_FIELD)
         send, to_polar, to_north, to_south, edge = launch(
@@ -584,8 +621,8 @@
         cross, tiles = launch(
             across_kernel, [coefficients], [LINE, TILES], (), [half, half, half], copies=3
         )
-        across = moved(cross, (0, TOP), 0, LON_DEV // 2)
-        return received, across, tiles, to_polar, to_north, to_south, edge
+        send, opened = respond(received, tiles)
+        return send, opened, cross, tiles, to_polar, to_north, to_south, edge
 
     def plain_first():
         (edges,) = launch(
@@ -606,34 +643,26 @@
             [in_vmem(FIELD), in_vmem(FIELD), in_vmem(COEFF), in_vmem(one_edge), in_vmem(one_edge)],
             copies=5,
         )
-        received, across, tiles = blanks(CHUNKS, LINE, TILES)
-        return received, across, tiles, to_polar, to_north, to_south, jnp.stack([west, east])
-
-    received, across, tiles, to_polar, to_north, to_south, edge = lax.cond(
+        send, opened, cross, tiles = blanks(CHUNKS, TILES, LINE, TILES)
+        edge = jnp.stack([west, east])
+        return send, opened, cross, tiles, to_polar, to_north, to_south, edge
+
+    send, opened, cross, tiles, to_polar, to_north, to_south, edge = lax.cond(
         polar, polar_first, plain_first
     )
     beyond = next_to_pole(to_polar, False)
 
-    def respond(received):
-        return launch(
-            respond_kernel,
-            [received, wave_cutoff, tiles],
-            [CHUNKS, TILES],
-            (),
-            [in_vmem(CHUNKS), small, in_vmem(TILES)],
-            copies=3,
-        )
-
     def polar_second():
-        send, opened = respond(received)
-        return exchanged(send), opened, to_north, to_south
+        waves = exchanged(send)
+        across = moved(cross, (0, TOP), 0, LON_DEV // 2)
+        return waves, across, to_north, to_south
 
     def plain_second():
         below = moved(to_north, range(1, TOP - 1), 1, 0)
         above = moved(to_south, range(2, TOP), -1, 0)
-        return *blanks(CHUNKS, TILES), below, above
-
-    waves, opened, below, above = lax.cond(polar, polar_second, plain_second)
+        return *blanks(CHUNKS, LINE), below, above
+
+    waves, across, below, above = lax.cond(polar, polar_second, plain_second)
 
     def polar_third():
         return tuple(launch(
@@ -643,7 +672,7 @@
             [FIELD],
             [in_vmem(CHUNKS), table_scratch, small, in_vmem(FIELD), in_vmem(FIELD), in_vmem(COEFF)]
             + [in_vmem(TILES), in_vmem(LINES), in_vmem(LINE), in_vmem(FIELD), *wave_scratch],
-            copies=9,
+            copies=15,
         ))
 
     def plain_third():
@@ -654,7 +683,7 @@
 
     def polar_fourth():
         received = exchanged(send)
-        again, opened = respond(received)
+        again, opened = respond(received, tiles)
         return exchanged(again), opened, middle
 
     def plain_fourth():
@@ -687,27 +716,25 @@
         (out,) = launch(
             final_kernel,
             [waves, table, polar_mask, result, coefficients, edges, opened, next_line, across],
-            [FIELD],
-            (),
-            [in_vmem(CHUNKS), table_scratch, small, in_vmem(FIELD), in_vmem(COEFF), in_vmem(EDGES)]
-            + [in_vmem(TILES), in_vmem(LINE), in_vmem(LINE), *wave_scratch],
-            copies=9,
-        )
-        return out
-
-    def plain_fifth():
-        (out,) = launch(
-            reach_kernel,
-            [result, waves_beyond, table, reached],
             (),
             [FIELD],
-            [in_vmem(HALF_FIELD), in_vmem(CHUNKS), table_scratch, in_vmem(LINES)],
-            copies=4,
-            aliases={0: 0},
+            [in_vmem(CHUNKS), table_scratch, small, in_vmem(FIELD), in_vmem(COEFF), in_vmem(EDGES)]
+            + [in_vmem(TILES), in_vmem(LINE), in_vmem(LINE), in_vmem(FIELD), *wave_scratch],
+            copies=13,
         )
         return out
 
-    return lax.cond(polar, polar_fifth, plain_fifth)
+    result = lax.cond(polar, polar_fifth, lambda kept=result: kept)
+    (out,) = launch(
+        reach_kernel,
+        [result, waves_beyond, table, reached],
+        (),
+        [FIELD],
+        [in_vmem(HALF_FIELD), in_vmem(CHUNKS), table_scratch, in_vmem(LINES)],
+        copies=4,
+        aliases={0: 0},
+    )
+    return out
 
 
 def forward_kernel_with_blanks(*refs):

time: 83.3 us -> 78.5 us (0.942)
  waiting for transfers between devices: 12.5 us -> 8.99 us
  Pallas kernels: 21.1 us -> 18.8 us
  blocking collectives: 24.7 us -> 26.9 us
  starting transfers between devices: 23.4 us -> 21.8 us
    pallas_call x6 -> x7, Pallas kernels: 21.1 us -> 18.8 us  [launch(): pl.pallas_call(kernel, in_specs=[pl.BlockSpec(memory_space=pltpu.HBM)] *...]
    all_to_all x2, blocking collectives: 24.7 us -> 26.9 us  [exchanged(): lax.all_to_all(chunks, 'lon', split_axis=0, concat_axis=0, tiled=True)]
    all_to_all x2, waiting for transfers between devices: 7.37 us -> 5.22 us  [exchanged(): lax.all_to_all(chunks, 'lon', split_axis=0, concat_axis=0, tiled=True)]
    all_to_all x2, starting transfers between devices: 14.6 us -> 13 us  [exchanged(): lax.all_to_all(chunks, 'lon', split_axis=0, concat_axis=0, tiled=True)]
    ppermute x3, waiting for transfers between devices: 2.25 us -> 1.03 us  [next_to_pole(): return lax.ppermute(value, ('lat', 'lon'), pairs)]
  transfers between devices with their start and end apart: 6 -> 6, of which waited for: 4 -> 3; matrix products, arithmetic and copies ran while one was open for 0% -> 0% of each run, Pallas kernels for 4% -> 9%
where the time goes in v1:
time: 78.5 us; the launch traced here: 77.7 us
  blocking collectives  26.9 us (34%)
  starting transfers between devices  21.8 us (28%)
  Pallas kernels  18.8 us (24%)
  waiting for transfers between devices  8.99 us (11%)
  local copies, waits for them, and re-layouts  1 us (1%)
    all_to_all x2, blocking collectives, exchanged(): lax.all_to_all(chunks, 'lon', split_axis=0, concat_axis=0, tiled=True)  26.9 us
    pallas_call x7, Pallas kernels, launch(): pl.pallas_call(kernel, in_specs=[pl.BlockSpec(memory_space=pltpu.HBM)] *...  18.8 us
    all_to_all x2, starting transfers between devices, exchanged(): lax.all_to_all(chunks, 'lon', split_axis=0, concat_axis=0, tiled=True)  13 us
    all_to_all x2, waiting for transfers between devices, exchanged(): lax.all_to_all(chunks, 'lon', split_axis=0, concat_axis=0, tiled=True)  5.22 us
    ppermute x1, starting transfers between devices, moved(): return lax.ppermute(value, ('lat', 'lon'), pairs)  4.92 us
    ppermute x3, starting transfers between devices, next_to_pole(): return lax.ppermute(value, ('lat', 'lon'), pairs)  3.89 us
    ppermute x1, waiting for transfers between devices, moved(): return lax.ppermute(value, ('lat', 'lon'), pairs)  2.74 us
  transfers between devices with their start and end apart: 6, of which 3 were waited for; matrix products, arithmetic and copies ran while one was open for 0% of the time, Pallas kernels for 9%

profile of v1, /device:TPU:8, one launch (start us, length us, event | category | flops | bytes accessed | tf_op | source)
XLA Modules:
  0.0 77.7 jit_solution(4383041831980277659)
XLA Ops:
  0.0 19.2 %conditional.5 = (f32[16,8,640]{2,1,0:T(8,128)}, f32[2,8,128]{2,1,0:T(8,128)S(1)}, f32[36,360]{1,0:T(8,128)S(1)}, f32[2,8,128]{2,1,0:T(8,128)}, f32[3,36,360]{2,...) conditional(s32[]{:T(128)} %convert_element_type.2, ...), branch_computations={%region_0.0_spmd, %region_1.0_spmd} | conditional | flops 4096 | bytes 31715800 | solution.py:650
  0.0 2.8 %branch_1_fun.6 = (f32[16,8,640]{2,1,0:T(8,128)}, f32[3,36,360]{2,1,0:T(8,128)S(1)}, f32[3,36,360]{2,1,0:T(8,128)S(1)}, f32[3,36,360]{2,1,0:T(8,128)S(1)}, f32[2,16,128]{2,1,0:T(8,128)S(1)}) custom-call(f32[3,12,16,360]{3,2,1,0:T(8,128)} %get-tuple-element.101.refs_0_, f32[3,5,12,16,360]{4,3,2,1,0:T(8,128)} %get-tuple-element.102.refs_1_.coeff_in, ...), custom_call_target="tpu_custom_call" | custom-call | bytes 8933056 | tf_op jit(solution)/shard_map/cond/branch_1_fun/pallas_call | solution.py:77
  2.9 0.0 copy-start.6
  2.9 7.4 %all-to-all-start = ((f32[16,8,640]{2,1,0:T(8,128)}), f32[16,8,640]{2,1,0:T(8,128)S(1)}, u32[]{:S(2)}, u32[]{:S(2)}) async-start(f32[16,8,640]{2,1,0:T(8,128)} %get-tuple-element.105), calls=%async_computation | async-start | bytes 655360 | tf_op jit(solution)/shard_map/cond/branch_1_fun/all_to_all | solution.py:568
  10.3 2.1 %branch_1_fun.7 = (f32[36,360]{1,0:T(8,128)S(1)}, f32[2,8,128]{2,1,0:T(8,128)}) custom-call(f32[3,5,12,16,360]{4,3,2,1,0:T(8,128)} %get-tuple-element.102.refs_1_.coeff_in), custom_call_target="tpu_custom_call" | custom-call | bytes 4207232 | tf_op jit(solution)/shard_map/cond/branch_1_fun/pallas_call | solution.py:77
  12.3 5.2 %all-to-all-done.received_in = f32[16,8,640]{2,1,0:T(8,128)S(1)} async-done(((f32[16,8,640]{2,1,0:T(8,128)}), f32[16,8,640]{2,1,0:T(8,128)S(1)}, u32[]{:S(2)}, u32[]{:S(2)}) %all-to-all-start) | async-done | bytes 327712 | tf_op jit(solution)/shard_map/cond/branch_1_fun/all_to_all | solution.py:568
  17.6 0.0 copy-done.6
  17.6 1.7 %branch_1_fun.8 = (f32[16,8,640]{2,1,0:T(8,128)}, f32[2,8,128]{2,1,0:T(8,128)S(1)}) custom-call(f32[16,8,640]{2,1,0:T(8,128)S(1)} %all-to-all-done.received_in, s32[16]{0:T(128)S(1)} %copy-done.6, f32[2,8,128]{2,1,0:T(8,128)} %get-tuple-element.212.tiles_in), custom_call_target="tpu_custom_call" | custom-call | bytes 671808 | tf_op jit(solution)/shard_map/cond/branch_1_fun/pallas_call | solution.py:77
  19.3 1.3 %collective-permute-start.7 = (f32[3,36,360]{2,1,0:T(8,128)S(1)}, f32[3,36,360]{2,1,0:T(8,128)S(1)}, u32[]{:S(2)}, u32[]{:S(2)}) collective-permute-start(f32[3,36,360]{2,1,0:T(8,128)S(1)} %get-tuple-element.184), channel_id=1, source_target_pairs={{16,0},{224,240},{17,1},{225,241},{18,2},{226,242},{19,3},{227,243... | collective-permute-start | bytes 466568 | tf_op jit(solution)/shard_map/ppermute | solution.py:584
  20.6 13.3 %conditional.6 = (f32[16,8,640]{2,1,0:T(8,128)}, f32[36,360]{1,0:T(8,128)}, f32[3,36,360]{2,1,0:T(8,128)S(1)}, f32[3,36,360]{2,1,0:T(8,128)S(1)}) conditional(s32[]{:T(128)} %convert_element_type.2, (f32[3,36,360]{2,1,0:T(8,128)S(1)}, f32[3,36,360]{2,1,0:T(8,128)S(1)}) %tuple.44, (f32[16,8,640]{2,1,0:T(8,128)}, f32[36,360]{1,0:T(8,128)S(1)}, ...), branch_computations={%region_2.0_spmd, %region_3.0_spmd} | conditional | bytes 1812584 | solution.py:665
  20.6 5.6 %all-to-all-start.1 = ((f32[16,8,640]{2,1,0:T(8,128)}), f32[16,8,640]{2,1,0:T(8,128)}, u32[]{:S(2)}, u32[]{:S(2)}) async-start(f32[16,8,640]{2,1,0:T(8,128)} %get-tuple-element.117), calls=%async_computation.1 | async-start | bytes 655360 | tf_op jit(solution)/shard_map/cond/branch_1_fun/all_to_all | solution.py:568
  26.1 4.9 %collective-permute-start.2 = (f32[36,360]{1,0:T(8,128)S(1)}, f32[36,360]{1,0:T(8,128)}, u32[]{:S(2)}, u32[]{:S(2)}) collective-permute-start(f32[36,360]{1,0:T(8,128)S(1)} %get-tuple-element.118), channel_id=1, source_target_pairs={{0,8},{1,9},{2,10},{3,11},{4,12},{5,13},{6,14},{7,15},{8,0},{9,1},... | collective-permute-start | bytes 155528 | tf_op jit(solution)/shard_map/cond/branch_1_fun/ppermute | solution.py:575
  31.1 2.7 %collective-permute-done.2 = f32[36,360]{1,0:T(8,128)} collective-permute-done((f32[36,360]{1,0:T(8,128)S(1)}, f32[36,360]{1,0:T(8,128)}, u32[]{:S(2)}, u32[]{:S(2)}) %collective-permute-start.2) | collective-permute-done | bytes 51872 | tf_op jit(solution)/shard_map/cond/branch_1_fun/ppermute | solution.py:575
  33.9 0.0 all-to-all-done.1
  33.9 0.0 collective-permute-done.7
  33.9 0.0 copy-start.5
  33.9 6.1 %conditional.7 = ((f32[16,8,640]{2,1,0:T(8,128)S(1)}, f32[3,36,360]{2,1,0:T(8,128)S(1)}, f32[36,360]{1,0:T(8,128)S(1)}, f32[2,16,128]{2,1,0:T(8,128)S(1)}, f32[3,12,16,360]{3,2,1,0:T(8,128)S(1)})) conditional(s32[]{:T(128)} %convert_element_type.2, () %tuple.46, (f32[16,8,640]{2,1,0:T(8,128)}, f32[16,128,384]{2,1,0:T(8,128)}, s32[16]{0:T(128)}, ...), branch_computations={%region_4.0_spmd, %region_5.0_spmd} | conditional | bytes 10875976 | solution.py:681
  33.9 6.1 %branch_1_fun.9 = (f32[16,8,640]{2,1,0:T(8,128)S(1)}, f32[3,36,360]{2,1,0:T(8,128)S(1)}, f32[36,360]{1,0:T(8,128)S(1)}, f32[2,16,128]{2,1,0:T(8,128)S(1)}, f32[3,12,16,360]{3,2,1,0:T(8,128)S(1)}) custom-call(f32[16,8,640]{2,1,0:T(8,128)} %get-tuple-element.121.waves_in, f32[16,128,384]{2,1,0:T(8,128)} %get-tuple-element.122.table_in, ...), custom_call_target="tpu_custom_call" | custom-call | bytes 10875968 | tf_op jit(solution)/shard_map/cond/branch_1_fun/pallas_call | solution.py:77
  40.0 1.3 %collective-permute-start.8 = (f32[3,36,360]{2,1,0:T(8,128)S(1)}, f32[3,36,360]{2,1,0:T(8,128)S(1)}, u32[]{:S(2)}, u32[]{:S(2)}) collective-permute-start(f32[3,36,360]{2,1,0:T(8,128)S(1)} %get-tuple-element.186), channel_id=1, source_target_pairs={{0,16},{240,224},{1,17},{241,225},{2,18},{242,226},{3,19},{243,227... | collective-permute-start | bytes 466568 | tf_op jit(solution)/shard_map/ppermute | solution.py:584
  41.3 1.0 %collective-permute-done.8.polar_in = f32[3,36,360]{2,1,0:T(8,128)S(1)} collective-permute-done((f32[3,36,360]{2,1,0:T(8,128)S(1)}, f32[3,36,360]{2,1,0:T(8,128)S(1)}, u32[]{:S(2)}, u32[]{:S(2)}) %collective-permute-start.8) | collective-permute-done | bytes 155552 | tf_op jit(solution)/shard_map/ppermute | solution.py:584
  42.3 0.0 copy-done.5
  42.3 0.0 copy-start.4
  42.3 27.9 %conditional.8 = (f32[16,8,640]{2,1,0:T(8,128)}, f32[2,8,128]{2,1,0:T(8,128)S(1)}, f32[3,12,16,360]{3,2,1,0:T(8,128)S(1)}) conditional(s32[]{:T(128)} %convert_element_type.2, (f32[2,16,128]{2,1,0:T(8,128)S(1)}, f32[3,12,16,360]{3,2,1,0:T(8,128)}, f32[3,12,16,360]{3,2,1,0:T(8,128)}, f32[3,5,12,16,360]{4,3,2,1,0:T(8,128)}, ...), branch_computations={%region_6.0_spmd, %region_7.0_spmd} | conditional | bytes 30220556 | solution.py:712
  42.3 14.5 %all_to_all.16.received_in = f32[16,8,640]{2,1,0:T(8,128)S(1)} all-to-all(f32[16,8,640]{2,1,0:T(8,128)S(1)} %get-tuple-element.140), channel_id=1, replica_groups=mesh['lat'=16,'lon'=16] {'lon'}, dimensions={0} | all-to-all | bytes 655360 | tf_op jit(solution)/shard_map/cond/branch_1_fun/all_to_all | solution.py:568
  56.8 1.0 %branch_1_fun.10 = (f32[16,8,640]{2,1,0:T(8,128)S(1)}, f32[2,8,128]{2,1,0:T(8,128)S(1)}) custom-call(f32[16,8,640]{2,1,0:T(8,128)S(1)} %all_to_all.16.received_in, s32[16]{0:T(128)S(1)} %get-tuple-element.141.cutoff_in, f32[2,8,128]{2,1,0:T(8,128)} %get-tuple-element.142.tiles_in), custom_call_target="tpu_custom_call" | custom-call | bytes 671808 | tf_op jit(solution)/shard_map/cond/branch_1_fun/pallas_call | solution.py:77
  57.8 12.4 %all_to_all.17 = f32[16,8,640]{2,1,0:T(8,128)} all-to-all(f32[16,8,640]{2,1,0:T(8,128)S(1)} %get-tuple-element.143), channel_id=1, replica_groups=mesh['lat'=16,'lon'=16] {'lon'}, dimensions={0} | all-to-all | bytes 655360 | tf_op jit(solution)/shard_map/cond/branch_1_fun/all_to_all | solution.py:568
  70.2 1.3 %collective-permute-start.9 = (f32[16,8,640]{2,1,0:T(8,128)}, f32[16,8,640]{2,1,0:T(8,128)S(1)}, u32[]{:S(2)}, u32[]{:S(2)}) collective-permute-start(f32[16,8,640]{2,1,0:T(8,128)} %get-tuple-element.191), channel_id=1, source_target_pairs={{0,16},{240,224},{1,17},{241,225},{2,18},{242,226},{3,19},{243,227... | collective-permute-start | bytes 983048 | tf_op jit(solution)/shard_map/ppermute | solution.py:584
  71.5 0.0 copy-done.4
  71.5 5.2 %conditional.9 = (f32[3,12,16,360]{3,2,1,0:T(8,128)S(1)}) conditional(s32[]{:T(128)} %convert_element_type.2, f32[3,12,16,360]{3,2,1,0:T(8,128)S(1)} %get-tuple-element.190, (f32[16,8,640]{2,1,0:T(8,128)}, f32[16,128,384]{2,1,0:T(8,128)}, s32[16]{0:T(128)S(1)}, f32[3,12,16,360]{3,2,1,0:T(8,128)S(1)}, f32[3,5,12,16,360]{4,3,2,1,0:T(8,128)}, ...), branch_computations={%region_8.0_spmd, %region_9.0_spmd} | conditional | bytes 11066696 | solution.py:727
  71.5 0.1 copy.52.middle_in
  71.6 5.2 %branch_1_fun.11 = f32[3,12,16,360]{3,2,1,0:T(8,128)S(1)} custom-call(f32[16,8,640]{2,1,0:T(8,128)} %get-tuple-element.146.waves_in, f32[16,128,384]{2,1,0:T(8,128)} %get-tuple-element.147.table_in, s32[16]{0:T(128)S(1)} %get-tuple-element.148.mask_in, f32[3,12,16,360]{3,2,1,0:T(8,128)S(1)} %copy.52.middle_in, ...), custom_call_target="tpu_custom_call" | custom-call | bytes 9407808 | tf_op jit(solution)/shard_map/cond/branch_1_fun/pallas_call | solution.py:77
  76.8 0.0 copy-start.3
  76.8 0.0 collective-permute-done.9.waves_in
  76.8 0.9 %copy-done.3 = f32[3,12,16,360]{3,2,1,0:T(8,128)} copy-done((f32[3,12,16,360]{3,2,1,0:T(8,128)}, f32[3,12,16,360]{3,2,1,0:T(8,128)S(1)}, u32[]{:S(2)}) %copy-start.3) | copy-done | bytes 829464
  (3 shorter events, 0.1 us)
Async XLA Ops:
  2.9 14.7 %copy-start.6 = (s32[16]{0:T(128)S(1)}, s32[16]{0:T(128)}, u32[]{:S(2)}) copy-start(s32[16]{0:T(128)} %get-tuple-element.106.cutoff_in) | copy-start | bytes 196 | tf_op jit(solution)/shard_map/cond
  2.9 14.7 %all-to-all-start = ((f32[16,8,640]{2,1,0:T(8,128)}), f32[16,8,640]{2,1,0:T(8,128)S(1)}, u32[]{:S(2)}, u32[]{:S(2)}) async-start(f32[16,8,640]{2,1,0:T(8,128)} %get-tuple-element.105), calls=%async_computation | async-start | bytes 655360 | tf_op jit(solution)/shard_map/cond/branch_1_fun/all_to_all | solution.py:568
  19.3 14.6 %collective-permute-start.7 = (f32[3,36,360]{2,1,0:T(8,128)S(1)}, f32[3,36,360]{2,1,0:T(8,128)S(1)}, u32[]{:S(2)}, u32[]{:S(2)}) collective-permute-start(f32[3,36,360]{2,1,0:T(8,128)S(1)} %get-tuple-element.184), channel_id=1, source_target_pairs={{16,0},{224,240},{17,1},{225,241},{18,2},{226,242},{19,3},{227,243... | collective-permute-start | bytes 466568 | tf_op jit(solution)/shard_map/ppermute | solution.py:584
  20.6 13.3 %all-to-all-start.1 = ((f32[16,8,640]{2,1,0:T(8,128)}), f32[16,8,640]{2,1,0:T(8,128)}, u32[]{:S(2)}, u32[]{:S(2)}) async-start(f32[16,8,640]{2,1,0:T(8,128)} %get-tuple-element.117), calls=%async_computation.1 | async-start | bytes 655360 | tf_op jit(solution)/shard_map/cond/branch_1_fun/all_to_all | solution.py:568
  26.1 7.7 %collective-permute-start.2 = (f32[36,360]{1,0:T(8,128)S(1)}, f32[36,360]{1,0:T(8,128)}, u32[]{:S(2)}, u32[]{:S(2)}) collective-permute-start(f32[36,360]{1,0:T(8,128)S(1)} %get-tuple-element.118), channel_id=1, source_target_pairs={{0,8},{1,9},{2,10},{3,11},{4,12},{5,13},{6,14},{7,15},{8,0},{9,1},... | collective-permute-start | bytes 155528 | tf_op jit(solution)/shard_map/cond/branch_1_fun/ppermute | solution.py:575
  33.9 8.5 %copy-start.5 = (s32[16]{0:T(128)S(1)}, s32[16]{0:T(128)}, u32[]{:S(2)}) copy-start(s32[16]{0:T(128)} %param.20) | copy-start | bytes 196
  40.0 2.3 %collective-permute-start.8 = (f32[3,36,360]{2,1,0:T(8,128)S(1)}, f32[3,36,360]{2,1,0:T(8,128)S(1)}, u32[]{:S(2)}, u32[]{:S(2)}) collective-permute-start(f32[3,36,360]{2,1,0:T(8,128)S(1)} %get-tuple-element.186), channel_id=1, source_target_pairs={{0,16},{240,224},{1,17},{241,225},{2,18},{242,226},{3,19},{243,227... | collective-permute-start | bytes 466568 | tf_op jit(solution)/shard_map/ppermute | solution.py:584
  42.3 29.2 %copy-start.4 = (s32[16]{0:T(128)S(1)}, s32[16]{0:T(128)}, u32[]{:S(2)}) copy-start(s32[16]{0:T(128)} %param.19) | copy-start | bytes 196
  70.2 6.6 %collective-permute-start.9 = (f32[16,8,640]{2,1,0:T(8,128)}, f32[16,8,640]{2,1,0:T(8,128)S(1)}, u32[]{:S(2)}, u32[]{:S(2)}) collective-permute-start(f32[16,8,640]{2,1,0:T(8,128)} %get-tuple-element.191), channel_id=1, source_target_pairs={{0,16},{240,224},{1,17},{241,225},{2,18},{242,226},{3,19},{243,227... | collective-permute-start | bytes 983048 | tf_op jit(solution)/shard_map/ppermute | solution.py:584
  76.8 0.9 %copy-start.3 = (f32[3,12,16,360]{3,2,1,0:T(8,128)}, f32[3,12,16,360]{3,2,1,0:T(8,128)S(1)}, u32[]{:S(2)}) copy-start(f32[3,12,16,360]{3,2,1,0:T(8,128)S(1)} %get-tuple-element.242.result_in) | copy-start | bytes 2488324

commit v2 on v1

--- a/solution.py
+++ b/solution.py
@@ -28,8 +28,12 @@
 FIELD = (FIELDS, LEV, BAND, WIDTH)
 HALF_FIELD = (FIELDS, LEV, HALF, WIDTH)
 COEFF = (FIELDS, 5, LEV, BAND, WIDTH)
-CHUNKS = (LON_DEV, SHARE, ROWS + 64)
+MORE = ROWS + 64
+CHUNKS = (LON_DEV, SHARE, MORE)
+FIRST_CHUNKS = (LON_DEV, SHARE, MORE + 128)
+LAST_TILE = (LON_DEV, SHARE, 128)
 LINE = (SLABS, WIDTH)
+ACROSS = (40, WIDE)
 LINES = (3, SLABS, WIDTH)
 TILES = (2, HALF, 128)
 EDGES = (2, BAND, 128)
@@ -70,16 +74,19 @@
     return pltpu.VMEM(shape, jnp.float32)
 
 
-def launch(kernel, operands, outs, far_outs=(), scratch=(), copies=0, aliases=None):
+def launch(kernel, operands, outs, far_outs=(), scratch=(), copies=0, aliases=None, near=0, pinned=False):
     shapes = [*outs, *far_outs]
     nbytes = sum(4 * math.prod(shape) for shape in shapes)
     nbytes += sum(4 * math.prod(operand.shape) for operand in operands)
     return pl.pallas_call(
         kernel,
-        in_specs=[pl.BlockSpec(memory_space=pltpu.HBM)] * len(operands),
+        in_specs=[pl.BlockSpec(memory_space=pltpu.VMEM)] * near
+        + [pl.BlockSpec(memory_space=pltpu.HBM)] * (len(operands) - near),
         out_specs=[pl.BlockSpec(memory_space=pltpu.VMEM)] * len(outs)
         + [pl.BlockSpec(memory_space=pltpu.HBM)] * len(far_outs),
-        out_shape=[jax.ShapeDtypeStruct(shape, jnp.float32) for shape in shapes],
+        out_shape=[
+            (pltpu.HBM if pinned else jax.ShapeDtypeStruct)(shape, jnp.float32) for shape in shapes
+        ],
         scratch_shapes=[*scratch, pltpu.SemaphoreType.DMA((copies,))],
         input_output_aliases=aliases or {},
         compiler_params=pltpu.CompilerParams(vmem_limit_bytes=24 * 2**20),
@@ -144,12 +151,24 @@
     return weight
 
 
+TILED = ACROSS[0] // 8 * (WIDE // 128)
+
+
+def tile_place(index):
+    row, column = index // (WIDE // 128), index % (WIDE // 128)
+    return slice(8 * row, 8 * row + 8), slice(128 * column, 128 * column + 128)
+
+
 def forward_kernel(
-    field_in, coeff_in, table_in, mask_in, send, field, table, to_east, to_west, mask, sems
+    field_in, coeff_in, table_in, mask_in,
+    send,
+    field, table, to_east, to_west, pole, across, mask, sems,
 ):
     lon, lat = place()
+    top = lat == TOP
     first = open_row(lat)
     rows = pl.ds(first, HALF)
+    closed = pl.ds(pl.multiple_of(HALF - first, HALF), HALF)
     field_copy, table_copy, *rest = begin(
         sems,
         (field_in, field),
@@ -157,7 +176,9 @@
         (coeff_in.at[:, 3, :, rows], to_east),
         (coeff_in.at[:, 4, :, rows], to_west),
         (mask_in, mask),
-    )
+        (coeff_in.at[:, jnp.where(top, 1, 2), :, closed], pole),
+    )
+    across[...] = jnp.zeros(ACROSS, jnp.float32)
     finish(field_copy, table_copy)
     waves = dot(table[:, :WIDTH], field[...].reshape(ROWS, WIDTH), 1, 1)
     send[:, :, :ROWS] = waves.reshape(LON_DEV, SHARE, ROWS)
@@ -171,19 +192,22 @@
         east = with_lane(east, slab, jnp.where(filtered, coeff, coeff * value[:, WIDTH - 1 :]))
         coeff = to_west[at][:, 0:1]
         west = with_lane(west, slab, jnp.where(filtered, coeff, coeff * value[:, 0:1]))
+        sign = 1.0 if at[0] == FIELDS - 1 else -1.0
+        lines = pole[at]
+        line = jnp.where(top, lines[HALF - 1 :], lines[0:1])
+        across[slab : slab + 1, :WIDTH] = sign * line
     for target in range(LON_DEV):
-        send[target, :, ROWS:] = jnp.where(target == (lon + 1) % LON_DEV, east, west)[:, :64]
-
-
-def across_kernel(coeff_in, across, tiles, pole, to_east, to_west, sems):
-    lon, lat = place()
-    top = lat == TOP
+        tile = jnp.where(target == (lon + 1) % LON_DEV, east, west)
+        send[target, :, ROWS:MORE] = tile[:, :64]
+        send[target, :, MORE:] = across[tile_place(target)] if target < TILED else tile
+
+
+def closed_kernel(coeff_in, tiles, to_east, to_west, sems):
+    _, lat = place()
     closed = pl.ds(pl.multiple_of(HALF - open_row(lat), HALF), HALF)
-    term = jnp.where(top, 1, 2)
     finish(
         *begin(
             sems,
-            (coeff_in.at[:, term, :, closed], pole),
             (coeff_in.at[:, 3, :, closed], to_east),
             (coeff_in.at[:, 4, :, closed], to_west),
         )
@@ -191,21 +215,14 @@
     east = west = jnp.zeros((HALF, 128), jnp.float32)
     for slab in range(SLABS):
         at = slab // LEV, slab % LEV
-        sign = 1.0 if at[0] == FIELDS - 1 else -1.0
-        lines = pole[at]
-        across[slab : slab + 1] = sign * jnp.where(top, lines[HALF - 1 :], lines[0:1])
         east = with_lane(east, slab, to_east[at][:, WIDTH - 1 :])
         west = with_lane(west, slab, to_west[at][:, 0:1])
     tiles[0] = east
     tiles[1] = west
 
 
-def respond_kernel(received_in, cutoff_in, tiles_in, send, edges, received, cutoff, tiles, sems):
+def responded(received, cutoff, edges):
     lon, _ = place()
-    main, *rest = begin(
-        sems, (received_in, received), (cutoff_in, cutoff), (tiles_in, tiles)
-    )
-    finish(*rest)
     shape = (SHARE, ROWS)
     wave = (lon * SHARE + iota(shape, 0)) % KMAX
     row = iota(shape, 1) % BAND
@@ -215,20 +232,36 @@
     ratio = limit.astype(jnp.float32) / jnp.maximum(wave, 1).astype(jnp.float32)
     response = jnp.where(wave <= limit, 1.0, ratio * ratio)
     response = response * jnp.where(wave == 0, 1.0 / NLON, 2.0 / NLON)
-    finish(main)
     total = received[0, :, :ROWS]
     for source in range(1, LON_DEV):
         total = total + received[source, :, :ROWS]
-    total = total * response
+    blank = jnp.zeros((HALF, 64), jnp.float32)
+    west = received[(lon + LON_DEV - 1) % LON_DEV, :, ROWS:MORE]
+    east = received[(lon + 1) % LON_DEV, :, ROWS:MORE]
+    edges[0] = jnp.concatenate([west, blank], axis=1)
+    edges[1] = jnp.concatenate([east, blank], axis=1)
+    return total * response
+
+
+def first_respond_kernel(received, cutoff_in, tiles_in, send, edges, cutoff, tiles, sems):
+    lon, _ = place()
+    finish(*begin(sems, (cutoff_in, cutoff), (tiles_in, tiles)))
+    total = responded(received, cutoff, edges)
     for target in range(LON_DEV):
         send[target, :, :ROWS] = total
         tile = jnp.where(target == (lon + 1) % LON_DEV, tiles[0], tiles[1])
-        send[target, :, ROWS:] = tile[:, :64]
-    blank = jnp.zeros((HALF, 64), jnp.float32)
-    west = received[(lon + LON_DEV - 1) % LON_DEV, :, ROWS:]
-    east = received[(lon + 1) % LON_DEV, :, ROWS:]
-    edges[0] = jnp.concatenate([west, blank], axis=1)
-    edges[1] = jnp.concatenate([east, blank], axis=1)
+        send[target, :, ROWS:MORE] = tile[:, :64]
+        send[target, :, MORE:] = received[(target + LON_DEV // 2) % LON_DEV, :, MORE:]
+
+
+def second_respond_kernel(received, cutoff_in, send, edges, cutoff, sems):
+    _, lat = place()
+    finish(*begin(sems, (cutoff_in, cutoff)))
+    total = responded(received, cutoff, edges)
+    near = row_waves(total, jnp.where(lat == TOP, 0, BAND - 1))
+    for target in range(LON_DEV):
+        send[target, :, :ROWS] = total
+        send[target, :, ROWS:] = near[:, :64]
 
 
 def gather_terms(value, coeff, south_line, north_line, west_edge, east_edge):
@@ -245,13 +278,16 @@
     return [coeff[field, term, level] for term in range(5)]
 
 
-def one_row(waves, table, row, opposite):
+def row_waves(waves, row):
     picked = iota((ROWS, 128), 0) == iota((ROWS, 128), 1) * BAND + row
     picked = picked.astype(jnp.float32).astype(jnp.bfloat16)
     high, low = split(waves)
-    chosen = pair_dot(high, picked, 1, 0) + pair_dot(low, picked, 1, 0)
-    if opposite:
-        chosen = jnp.where(iota((WAVES, 128), 0) % 2 == 1, -chosen, chosen)
+    return pair_dot(high, picked, 1, 0) + pair_dot(low, picked, 1, 0)
+
+
+def across_pole(waves, table, row):
+    chosen = row_waves(waves, row)
+    chosen = jnp.where(iota((WAVES, 128), 0) % 2 == 1, -chosen, chosen)
     return dot(chosen, table, 0, 0)
 
 
@@ -262,34 +298,34 @@
 
 
 def middle_kernel(
-    waves_in, table_in, mask_in, state_in, extra_in, coeff_in, opened_in, beyond_in, across_in,
-    send, to_next, next_line, edges, middle_out,
-    waves, table, mask, state, extra, coeff_ref, opened, beyond, across, middle,
+    waves, table_in, mask_in, state_in, extra_in, coeff_in, opened_in, beyond_in,
+    send, to_next, next_line, edges, across, middle_out,
+    table, mask, state, extra, coeff_ref, opened, beyond, middle,
     filtered, opposite, sems,
 ):
     lon, lat = place()
     top = lat == TOP
-    waves_copy, table_copy, *rest = begin(
+    table_copy, *rest = begin(
         sems,
-        (waves_in, waves),
         (table_in.at[lon], table),
         (mask_in, mask),
         (opened_in, opened),
         (beyond_in, beyond),
-        (across_in, across),
         *by_field((state_in, state), (extra_in, extra), (coeff_in, coeff_ref)),
     )
-    rest, fields = rest[:4], rest[4:]
-    finish(waves_copy, table_copy)
+    rest, fields = rest[:3], rest[3:]
+    for tile in range(TILED):
+        across[tile_place(tile)] = waves[tile, :, MORE:]
+    finish(table_copy)
     flat = waves[:, :, :ROWS].reshape(WAVES, ROWS)
     filtered[...] = dot(flat, table[...], 0, 0)
     polar_row = jnp.where(top, BAND - 1, 0)
-    opposite[...] = one_row(flat, table[...], polar_row, True)
+    opposite[...] = across_pole(flat, table[...], polar_row)
     finish(*rest)
     blank = jnp.zeros((HALF, 64), jnp.float32)
     sides = (lon + LON_DEV - 1) % LON_DEV, (lon + 1) % LON_DEV
     for side in range(2):
-        closed = jnp.concatenate([waves[sides[side], :, ROWS:], blank], axis=1)
+        closed = jnp.concatenate([waves[sides[side], :, ROWS:MORE], blank], axis=1)
         edges[side] = whole_band(closed, opened[side], top)
     weight = row_weight(mask, 0, (BAND, WIDTH))
     is_filtered = weight[:, 0:1] > 0.5
@@ -312,7 +348,7 @@
         total, north, south = gather_terms(
             value, coeff, jnp.where(top, halo, 0.0), jnp.where(top, 0.0, halo), west, east
         )
-        pole = across[here] * opposite[here][:, :WIDTH]
+        pole = (across[here] * opposite[here])[:, :WIDTH]
         total = total + jnp.where(row == polar_row, pole, 0.0) + extra[field, level]
         middle[field, level] = total
         product = jnp.where(top, south[0:1], north[BAND - 1 :])
@@ -344,16 +380,15 @@
 
 
 def final_kernel(
-    waves_in, table_in, mask_in, middle_in, coeff_in, edges_in, opened_in, line_in, across_in,
+    waves, table_in, mask_in, middle_in, coeff_in, edges_in, opened_in, line_in, across_in,
     out,
-    waves, table, mask, middle, coeff_ref, edges, opened, next_line, across, result,
+    table, mask, middle, coeff_ref, edges, opened, next_line, across, result,
     filtered, opposite, sems,
 ):
     lon, lat = place()
     top = lat == TOP
-    waves_copy, table_copy, *rest = begin(
+    table_copy, *rest = begin(
         sems,
-        (waves_in, waves),
         (table_in.at[lon], table),
         (mask_in, mask),
         (edges_in, edges),
@@ -363,11 +398,11 @@
         *by_field((middle_in, middle), (coeff_in, coeff_ref)),
     )
     rest, fields = rest[:5], rest[5:]
-    finish(waves_copy, table_copy)
+    finish(table_copy)
     flat = waves[:, :, :ROWS].reshape(WAVES, ROWS)
     filtered[...] = dot(flat, table[...], 0, 0)
     polar_row = jnp.where(top, BAND - 1, 0)
-    opposite[...] = one_row(flat, table[...], polar_row, True)
+    opposite[...] = across_pole(flat, table[...], polar_row)
     finish(*rest)
     weight = row_weight(mask, 0, (BAND, WIDTH))
     is_filtered = weight[:, 0:1] > 0.5
@@ -391,7 +426,7 @@
         total, _, _ = gather_terms(
             value, coeff, jnp.where(top, halo, 0.0), jnp.where(top, 0.0, halo), west, east
         )
-        pole = across[here] * opposite[here][:, :WIDTH]
+        pole = (across[here] * opposite[here])[:, :WIDTH]
         result[field, level] = total + jnp.where(row == polar_row, pole, 0.0)
         return carry
 
@@ -553,9 +588,8 @@
                 (polar_in, polar),
             )
         )
-        flat = waves[:, :, :ROWS].reshape(WAVES, ROWS)
-        smooth = one_row(flat, table[...], jnp.where(bottom, BAND - 1, 0), False)
-        line = polar[1] + polar[2] * smooth[:SLABS, :WIDTH]
+        smooth = dot(waves[...].reshape(WAVES, 128), table[...], 0, 0)
+        line = polar[1] + polar[2] * smooth[64 : 64 + SLABS, :WIDTH]
         row = iota((HALF, WIDTH), 0)
         mine = row == jnp.where(bottom, 0, HALF - 1)
         for slab in range(SLABS):
@@ -597,32 +631,28 @@
     def blanks(*shapes):
         return tuple(jnp.zeros(shape, jnp.float32) for shape in shapes)
 
-    def respond(received, tiles):
-        return launch(
-            respond_kernel,
-            [received, wave_cutoff, tiles],
-            [CHUNKS, TILES],
-            (),
-            [in_vmem(CHUNKS), small, in_vmem(TILES)],
-            copies=3,
-        )
-
     def polar_first():
         half = in_vmem(HALF_FIELD)
         send, to_polar, to_north, to_south, edge = launch(
             forward_kernel_with_blanks,
             [adjoint_state, coefficients, table, polar_mask],
-            [CHUNKS],
+            [FIRST_CHUNKS],
             [LINES, LINES, LINES, (2, *one_edge)],
-            [in_vmem(FIELD), table_scratch, half, half, small],
-            copies=5,
+            [in_vmem(FIELD), table_scratch, half, half, half, in_vmem(ACROSS), small],
+            copies=6,
         )
         received = exchanged(send)
-        cross, tiles = launch(
-            across_kernel, [coefficients], [LINE, TILES], (), [half, half, half], copies=3
-        )
-        send, opened = respond(received, tiles)
-        return send, opened, cross, tiles, to_polar, to_north, to_south, edge
+        (tiles,) = launch(closed_kernel, [coefficients], [TILES], (), [half, half], copies=2)
+        send, opened = launch(
+            first_respond_kernel,
+            [received, wave_cutoff, tiles],
+            [FIRST_CHUNKS, TILES],
+            (),
+            [small, in_vmem(TILES)],
+            copies=2,
+            near=1,
+        )
+        return send, opened, to_polar, to_north, to_south, edge
 
     def plain_first():
         (edges,) = launch(
@@ -643,48 +673,53 @@
             [in_vmem(FIELD), in_vmem(FIELD), in_vmem(COEFF), in_vmem(one_edge), in_vmem(one_edge)],
             copies=5,
         )
-        send, opened, cross, tiles = blanks(CHUNKS, TILES, LINE, TILES)
-        edge = jnp.stack([west, east])
-        return send, opened, cross, tiles, to_polar, to_north, to_south, edge
-
-    send, opened, cross, tiles, to_polar, to_north, to_south, edge = lax.cond(
-        polar, polar_first, plain_first
-    )
+        send, opened = blanks(FIRST_CHUNKS, TILES)
+        return send, opened, to_polar, to_north, to_south, jnp.stack([west, east])
+
+    send, opened, to_polar, to_north, to_south, edge = lax.cond(polar, polar_first, plain_first)
     beyond = next_to_pole(to_polar, False)
 
     def polar_second():
-        waves = exchanged(send)
-        across = moved(cross, (0, TOP), 0, LON_DEV // 2)
-        return waves, across, to_north, to_south
+        return exchanged(send), to_north, to_south
 
     def plain_second():
         below = moved(to_north, range(1, TOP - 1), 1, 0)
         above = moved(to_south, range(2, TOP), -1, 0)
-        return *blanks(CHUNKS, LINE), below, above
-
-    waves, across, below, above = lax.cond(polar, polar_second, plain_second)
+        return *blanks(FIRST_CHUNKS), below, above
+
+    waves, below, above = lax.cond(polar, polar_second, plain_second)
 
     def polar_third():
         return tuple(launch(
             middle_kernel,
-            [waves, table, polar_mask, adjoint_state, innovation, coefficients, opened, beyond, across],
-            [CHUNKS, LINES, LINE, EDGES],
+            [waves, table, polar_mask, adjoint_state, innovation, coefficients, opened, beyond],
+            [CHUNKS, LINES, LINE, EDGES, ACROSS],
             [FIELD],
-            [in_vmem(CHUNKS), table_scratch, small, in_vmem(FIELD), in_vmem(FIELD), in_vmem(COEFF)]
-            + [in_vmem(TILES), in_vmem(LINES), in_vmem(LINE), in_vmem(FIELD), *wave_scratch],
-            copies=15,
+            [table_scratch, small, in_vmem(FIELD), in_vmem(FIELD), in_vmem(COEFF)]
+            + [in_vmem(TILES), in_vmem(LINES), in_vmem(FIELD), *wave_scratch],
+            copies=13,
+            near=1,
         ))
 
     def plain_third():
-        return blanks(CHUNKS, LINES, LINE, EDGES, FIELD)
-
-    send, to_next, next_line, edges, middle = lax.cond(polar, polar_third, plain_third)
+        return blanks(CHUNKS, LINES, LINE, EDGES, ACROSS, FIELD)
+
+    send, to_next, next_line, edges, across, middle = lax.cond(polar, polar_third, plain_third)
     reached = next_to_pole(to_next, True)
 
     def polar_fourth():
         received = exchanged(send)
-        again, opened = respond(received, tiles)
-        return exchanged(again), opened, middle
+        again, opened = launch(
+            second_respond_kernel,
+            [received, wave_cutoff],
+            [CHUNKS, TILES],
+            (),
+            [small],
+            copies=1,
+            near=1,
+        )
+        waves = exchanged(again)
+        return waves, lax.slice_in_dim(waves, MORE - 128, MORE, axis=2), opened, middle
 
     def plain_fourth():
         west, east = edge[0], edge[1]
@@ -707,10 +742,10 @@
             [in_vmem(FIELD), in_vmem(COEFF), in_vmem(one_edge), in_vmem(one_edge), in_vmem((2, *LINE))],
             copies=5,
         )
-        return *blanks(CHUNKS, TILES), result
-
-    waves, opened, result = lax.cond(polar, polar_fourth, plain_fourth)
-    waves_beyond = next_to_pole(waves, True)
+        return *blanks(CHUNKS, LAST_TILE, TILES), result
+
+    waves, near_waves, opened, result = lax.cond(polar, polar_fourth, plain_fourth)
+    waves_beyond = next_to_pole(near_waves, True)
 
     def polar_fifth():
         (out,) = launch(
@@ -718,9 +753,11 @@
             [waves, table, polar_mask, result, coefficients, edges, opened, next_line, across],
             (),
             [FIELD],
-            [in_vmem(CHUNKS), table_scratch, small, in_vmem(FIELD), in_vmem(COEFF), in_vmem(EDGES)]
-            + [in_vmem(TILES), in_vmem(LINE), in_vmem(LINE), in_vmem(FIELD), *wave_scratch],
-            copies=13,
+            [table_scratch, small, in_vmem(FIELD), in_vmem(COEFF), in_vmem(EDGES)]
+            + [in_vmem(TILES), in_vmem(LINE), in_vmem(ACROSS), in_vmem(FIELD), *wave_scratch],
+            copies=12,
+            near=1,
+            pinned=True,
         )
         return out
 
@@ -730,9 +767,10 @@
         [result, waves_beyond, table, reached],
         (),
         [FIELD],
-        [in_vmem(HALF_FIELD), in_vmem(CHUNKS), table_scratch, in_vmem(LINES)],
+        [in_vmem(HALF_FIELD), in_vmem(LAST_TILE), table_scratch, in_vmem(LINES)],
         copies=4,
         aliases={0: 0},
+        pinned=True,
     )
     return out
 

time: 78.5 us -> 79.4 us (1.011)
  waiting for transfers between devices: 8.99 us -> 14.9 us
  starting transfers between devices: 21.8 us -> 16.9 us
  blocking collectives: 26.9 us -> 24.9 us
  Pallas kernels: 18.8 us -> 19.9 us
  local copies, waits for them, and re-layouts: 1 us -> 2.06 us
    all_to_all x2, waiting for transfers between devices: 5.22 us -> 13.9 us  [exchanged(): lax.all_to_all(chunks, 'lon', split_axis=0, concat_axis=0, tiled=True)]
    ppermute x1 -> x0, starting transfers between devices: 4.92 us -> none  [moved(): return lax.ppermute(value, ('lat', 'lon'), pairs)]
    ppermute x1 -> x0, waiting for transfers between devices: 2.74 us -> none  [moved(): return lax.ppermute(value, ('lat', 'lon'), pairs)]
    all_to_all x2, blocking collectives: 26.9 us -> 24.9 us  [exchanged(): lax.all_to_all(chunks, 'lon', split_axis=0, concat_axis=0, tiled=True)]
    cond x5, local copies, waits for them, and re-layouts: 0.1 us -> 1.2 us
    pallas_call x7, Pallas kernels: 18.8 us -> 19.9 us  [launch(): pl.pallas_call(kernel, in_specs=[pl.BlockSpec(memory_space=pltpu.VMEM)] *...]
    unnamed x6 -> x4, local copies, waits for them, and re-layouts: 0.9 us -> 0.01 us
    slice x0 -> x1, local copies, waits for them, and re-layouts: none -> 0.84 us  [polar_fourth(): lax.slice_in_dim(waves, MORE - 128, MORE, axis=2)]
  transfers between devices with their start and end apart: 6 -> 5, of which waited for: 3 -> 3; matrix products, arithmetic and copies ran while one was open for 0% -> 2% of each run, Pallas kernels for 9% -> 10%
where the time goes in v2:
time: 79.4 us; the launch traced here: 78.9 us
  blocking collectives  24.9 us (31%)
  Pallas kernels  19.9 us (25%)
  starting transfers between devices  16.9 us (21%)
  waiting for transfers between devices  14.9 us (19%)
  local copies, waits for them, and re-layouts  2.06 us (3%)
    all_to_all x2, blocking collectives, exchanged(): lax.all_to_all(chunks, 'lon', split_axis=0, concat_axis=0, tiled=True)  24.9 us
    pallas_call x7, Pallas kernels, launch(): pl.pallas_call(kernel, in_specs=[pl.BlockSpec(memory_space=pltpu.VMEM)] *...  19.9 us
    all_to_all x2, waiting for transfers between devices, exchanged(): lax.all_to_all(chunks, 'lon', split_axis=0, concat_axis=0, tiled=True)  13.9 us
    all_to_all x2, starting transfers between devices, exchanged(): lax.all_to_all(chunks, 'lon', split_axis=0, concat_axis=0, tiled=True)  13 us
    ppermute x3, starting transfers between devices, next_to_pole(): return lax.ppermute(value, ('lat', 'lon'), pairs)  3.87 us
  transfers between devices with their start and end apart: 5, of which 3 were waited for; matrix products, arithmetic and copies ran while one was open for 2% of the time, Pallas kernels for 10%

profile of v2, /device:TPU:8, one launch (start us, length us, event | category | flops | bytes accessed | tf_op | source)
XLA Modules:
  0.0 78.9 jit_solution(6255740829607410061)
XLA Ops:
  0.0 19.2 %conditional.5 = (f32[16,8,768]{2,1,0:T(8,128)}, f32[2,8,128]{2,1,0:T(8,128)S(1)}, f32[3,36,360]{2,1,0:T(8,128)S(1)}, f32[3,36,360]{2,1,0:T(8,128)S(1)}, f32[3,3...) conditional(s32[]{:T(128)} %convert_element_type.2, (f32[3,12,16,360]{3,2,1,0:T(8,128)}, ...), branch_computations={%region_0.0_spmd, %region_1.0_spmd} | conditional | flops 4096 | bytes 31721280 | solution.py:679
  0.0 2.9 %branch_1_fun.6 = (f32[16,8,768]{2,1,0:T(8,128)}, f32[3,36,360]{2,1,0:T(8,128)S(1)}, f32[3,36,360]{2,1,0:T(8,128)S(1)}, f32[3,36,360]{2,1,0:T(8,128)S(1)}, f32[2,16,128]{2,1,0:T(8,128)S(1)}) custom-call(f32[3,12,16,360]{3,2,1,0:T(8,128)} %get-tuple-element.95.refs_0_, f32[3,5,12,16,360]{4,3,2,1,0:T(8,128)} %get-tuple-element.96.refs_1_.coeff_in, ...), custom_call_target="tpu_custom_call" | custom-call | bytes 8998592 | tf_op jit(solution)/shard_map/cond/branch_1_fun/pallas_call | solution.py:81
  2.9 0.0 copy-start.5
  2.9 7.4 %all-to-all-start = ((f32[16,8,768]{2,1,0:T(8,128)}), f32[16,8,768]{2,1,0:T(8,128)S(1)}, u32[]{:S(2)}, u32[]{:S(2)}) async-start(f32[16,8,768]{2,1,0:T(8,128)} %get-tuple-element.99), calls=%async_computation | async-start | bytes 786432 | tf_op jit(solution)/shard_map/cond/branch_1_fun/all_to_all | solution.py:602
  10.3 1.3 %branch_1_fun.7.tiles_in = f32[2,8,128]{2,1,0:T(8,128)S(1)} custom-call(f32[3,5,12,16,360]{4,3,2,1,0:T(8,128)} %get-tuple-element.96.refs_1_.coeff_in), custom_call_target="tpu_custom_call" | custom-call | bytes 4155392 | tf_op jit(solution)/shard_map/cond/branch_1_fun/pallas_call | solution.py:81
  11.6 6.2 %all-to-all-done.received = f32[16,8,768]{2,1,0:T(8,128)S(1)} async-done(((f32[16,8,768]{2,1,0:T(8,128)}), f32[16,8,768]{2,1,0:T(8,128)S(1)}, u32[]{:S(2)}, u32[]{:S(2)}) %all-to-all-start) | async-done | bytes 393248 | tf_op jit(solution)/shard_map/cond/branch_1_fun/all_to_all | solution.py:602
  17.8 0.0 copy-done.5
  17.8 1.4 %branch_1_fun.8 = (f32[16,8,768]{2,1,0:T(8,128)}, f32[2,8,128]{2,1,0:T(8,128)S(1)}) custom-call(f32[16,8,768]{2,1,0:T(8,128)S(1)} %all-to-all-done.received, s32[16]{0:T(128)S(1)} %copy-done.5, f32[2,8,128]{2,1,0:T(8,128)S(1)} %branch_1_fun.7.tiles_in), custom_call_target="tpu_custom_call" | custom-call | bytes 802880 | tf_op jit(solution)/shard_map/cond/branch_1_fun/pallas_call | solution.py:81
  19.2 1.3 %collective-permute-start.6 = (f32[3,36,360]{2,1,0:T(8,128)S(1)}, f32[3,36,360]{2,1,0:T(8,128)S(1)}, u32[]{:S(2)}, u32[]{:S(2)}) collective-permute-start(f32[3,36,360]{2,1,0:T(8,128)S(1)} %get-tuple-element.171), channel_id=1, source_target_pairs={{16,0},{224,240},{17,1},{225,241},{18,2},{226,242},{19,3},{227,243... | collective-permute-start | bytes 466568 | tf_op jit(solution)/shard_map/ppermute | solution.py:618
  20.5 13.4 %conditional.6 = (f32[16,8,768]{2,1,0:T(8,128)}, f32[3,36,360]{2,1,0:T(8,128)S(1)}, f32[3,36,360]{2,1,0:T(8,128)S(1)}) conditional(s32[]{:T(128)} %convert_element_type.2, (f32[3,36,360]{2,1,0:T(8,128)S(1)}, f32[3,36,360]{2,1,0:T(8,128)S(1)}) %tuple.44, (f32[16,8,768]{2,1,0:T(8,128)}, f32[3,36,360]{2,1,0:T(8,128)S(1)}, ...), branch_computations={%region_2.0_spmd, %region_3.0_spmd} | conditional | bytes 1801784 | solution.py:690
  20.6 5.6 %all-to-all-start.1 = ((f32[16,8,768]{2,1,0:T(8,128)}), f32[16,8,768]{2,1,0:T(8,128)}, u32[]{:S(2)}, u32[]{:S(2)}) async-start(f32[16,8,768]{2,1,0:T(8,128)} %get-tuple-element.109), calls=%async_computation.1 | async-start | bytes 786432 | tf_op jit(solution)/shard_map/cond/branch_1_fun/all_to_all | solution.py:602
  26.3 7.7 %all-to-all-done.1 = f32[16,8,768]{2,1,0:T(8,128)} async-done(((f32[16,8,768]{2,1,0:T(8,128)}), f32[16,8,768]{2,1,0:T(8,128)}, u32[]{:S(2)}, u32[]{:S(2)}) %all-to-all-start.1) | async-done | bytes 393248 | tf_op jit(solution)/shard_map/cond/branch_1_fun/all_to_all | solution.py:602
  33.9 0.0 collective-permute-done.6
  33.9 0.0 copy-start.4
  33.9 6.8 %conditional.7 = ((f32[16,8,640]{2,1,0:T(8,128)S(1)}, f32[3,36,360]{2,1,0:T(8,128)S(1)}, f32[36,360]{1,0:T(8,128)S(1)}, f32[2,16,128]{2,1,0:T(8,128)S(1)}, f32[4...) conditional(s32[]{:T(128)} %convert_element_type.2, () %tuple.46, (f32[16,8,768]{2,1,0:T(8,128)}, ...), branch_computations={%region_4.0_spmd, %region_5.0_spmd} | conditional | bytes 10951112 | solution.py:707
  33.9 6.8 %branch_1_fun.9 = (f32[16,8,640]{2,1,0:T(8,128)S(1)}, f32[3,36,360]{2,1,0:T(8,128)S(1)}, f32[36,360]{1,0:T(8,128)S(1)}, f32[2,16,128]{2,1,0:T(8,128)S(1)}, f32[4...) custom-call(f32[16,8,768]{2,1,0:T(8,128)} %get-tuple-element.112.waves, f32[16,128,384]{2,1,0:T(8,128)} %get-tuple-element.113.table_in, ...), custom_call_target="tpu_custom_call" | custom-call | bytes 10951104 | tf_op jit(solution)/shard_map/cond/branch_1_fun/pallas_call | solution.py:81
  40.8 1.3 %collective-permute-start.7 = (f32[3,36,360]{2,1,0:T(8,128)S(1)}, f32[3,36,360]{2,1,0:T(8,128)S(1)}, u32[]{:S(2)}, u32[]{:S(2)}) collective-permute-start(f32[3,36,360]{2,1,0:T(8,128)S(1)} %get-tuple-element.172), channel_id=1, source_target_pairs={{0,16},{240,224},{1,17},{241,225},{2,18},{242,226},{3,19},{243,227... | collective-permute-start | bytes 466568 | tf_op jit(solution)/shard_map/ppermute | solution.py:618
  42.1 1.0 %collective-permute-done.7.polar_in = f32[3,36,360]{2,1,0:T(8,128)S(1)} collective-permute-done((f32[3,36,360]{2,1,0:T(8,128)S(1)}, f32[3,36,360]{2,1,0:T(8,128)S(1)}, u32[]{:S(2)}, u32[]{:S(2)}) %collective-permute-start.7) | collective-permute-done | bytes 155552 | tf_op jit(solution)/shard_map/ppermute | solution.py:618
  43.1 0.0 copy-done.4
  43.1 0.0 copy-start.3
  43.1 26.6 %conditional.8 = (f32[16,8,640]{2,1,0:T(8,128)}, f32[16,8,128]{2,1,0:T(8,128)S(1)}, f32[2,8,128]{2,1,0:T(8,128)S(1)}, f32[3,12,16,360]{3,2,1,0:T(8,128)}) conditional(s32[]{:T(128)} %convert_element_type.2, (f32[2,16,128]{2,1,0:T(8,128)S(1)}, f32[3,12,16,360]{3,2,1,0:T(8,128)}, f32[3,12,16,360]{3,2,1,0:T(8,128)}, f32[3,5,12,16,360]{4,3,2,1,0:T(8,128)}, ...), branch_computations={%region_6.0_spmd, %region_7.0_spmd} | conditional | bytes 30286104 | solution.py:747
  43.1 12.5 %all_to_all.16.received = f32[16,8,640]{2,1,0:T(8,128)S(1)} all-to-all(f32[16,8,640]{2,1,0:T(8,128)S(1)} %get-tuple-element.130), channel_id=1, replica_groups=mesh['lat'=16,'lon'=16] {'lon'}, dimensions={0} | all-to-all | bytes 655360 | tf_op jit(solution)/shard_map/cond/branch_1_fun/all_to_all | solution.py:602
  55.6 0.8 %branch_1_fun.10 = (f32[16,8,640]{2,1,0:T(8,128)S(1)}, f32[2,8,128]{2,1,0:T(8,128)S(1)}) custom-call(f32[16,8,640]{2,1,0:T(8,128)S(1)} %all_to_all.16.received, s32[16]{0:T(128)S(1)} %get-tuple-element.131.cutoff_in), custom_call_target="tpu_custom_call" | custom-call | bytes 663616 | tf_op jit(solution)/shard_map/cond/branch_1_fun/pallas_call | solution.py:81
  56.5 12.4 %all_to_all.17 = f32[16,8,640]{2,1,0:T(8,128)} all-to-all(f32[16,8,640]{2,1,0:T(8,128)S(1)} %get-tuple-element.132), channel_id=1, replica_groups=mesh['lat'=16,'lon'=16] {'lon'}, dimensions={0} | all-to-all | bytes 655360 | tf_op jit(solution)/shard_map/cond/branch_1_fun/all_to_all | solution.py:602
  68.9 0.8 %slice.23 = f32[16,8,128]{2,1,0:T(8,128)S(1)} slice(f32[16,8,640]{2,1,0:T(8,128)} %all_to_all.17), slice={[0:16], [0:8], [512:640]} | slice | bytes 131072 | tf_op jit(solution)/shard_map/cond/branch_1_fun/slice | solution.py:722
  69.7 1.3 %collective-permute-start.8 = (f32[16,8,128]{2,1,0:T(8,128)S(1)}, f32[16,8,128]{2,1,0:T(8,128)S(1)}, u32[]{:S(2)}, u32[]{:S(2)}) collective-permute-start(f32[16,8,128]{2,1,0:T(8,128)S(1)} %get-tuple-element.181), channel_id=1, source_target_pairs={{0,16},{240,224},{1,17},{241,225},{2,18},{242,226},{3,19},{243,227... | collective-permute-start | bytes 196616 | tf_op jit(solution)/shard_map/ppermute | solution.py:618
  71.0 0.0 copy-done.3
  71.0 7.7 %conditional.9 = (f32[3,12,16,360]{3,2,1,0:T(8,128)}) conditional(s32[]{:T(128)} %convert_element_type.2, f32[3,12,16,360]{3,2,1,0:T(8,128)} %get-tuple-element.175, (f32[16,8,640]{2,1,0:T(8,128)}, f32[16,128,384]{2,1,0:T(8,128)}, s32[16]{0:T(128)S(1)}, f32[3,12,16,360]{3,2,1,0:T(8,128)}, f32[3,5,12,16,360]{4,3,2,1,0:T(8,128)}, ...), branch_computations={%region_8.0_spmd, %region_9.0_spmd} | conditional | bytes 11076296 | solution.py:764
  71.1 1.2 %copy.50.middle_in = f32[3,12,16,360]{3,2,1,0:T(8,128)S(1)} copy(f32[3,12,16,360]{3,2,1,0:T(8,128)} %get-tuple-element.138) | data formatting | bytes 1658880 | tf_op jit(solution)/shard_map/cond
  72.2 6.5 %branch_1_fun.11 = f32[3,12,16,360]{3,2,1,0:T(8,128)} custom-call(f32[16,8,640]{2,1,0:T(8,128)} %get-tuple-element.135.waves, f32[16,128,384]{2,1,0:T(8,128)} %get-tuple-element.136.table_in, s32[16]{0:T(128)S(1)} %get-tuple-element.137.mask_in, f32[3,12,16,360]{3,2,1,0:T(8,128)S(1)} %copy.50.middle_in, f32[3,5,12,16,360]{4,3,2,1,0:T(8,128)} %get-tuple-element.139.coeff_in, ...), custom_call_target="tpu_custom_call" | custom-call | bytes 9417408 | tf_op jit(solution)/shard_map/cond/branch_1_fun/pallas_call | solution.py:81
  78.8 0.0 collective-permute-done.8.waves_in
  78.8 0.1 shard_map.64
  (2 shorter events, 0.0 us)
Async XLA Ops:
  2.9 14.9 %copy-start.5 = (s32[16]{0:T(128)S(1)}, s32[16]{0:T(128)}, u32[]{:S(2)}) copy-start(s32[16]{0:T(128)} %get-tuple-element.100.cutoff_in) | copy-start | bytes 196 | tf_op jit(solution)/shard_map/cond
  2.9 14.9 %all-to-all-start = ((f32[16,8,768]{2,1,0:T(8,128)}), f32[16,8,768]{2,1,0:T(8,128)S(1)}, u32[]{:S(2)}, u32[]{:S(2)}) async-start(f32[16,8,768]{2,1,0:T(8,128)} %get-tuple-element.99), calls=%async_computation | async-start | bytes 786432 | tf_op jit(solution)/shard_map/cond/branch_1_fun/all_to_all | solution.py:602
  19.2 14.7 %collective-permute-start.6 = (f32[3,36,360]{2,1,0:T(8,128)S(1)}, f32[3,36,360]{2,1,0:T(8,128)S(1)}, u32[]{:S(2)}, u32[]{:S(2)}) collective-permute-start(f32[3,36,360]{2,1,0:T(8,128)S(1)} %get-tuple-element.171), channel_id=1, source_target_pairs={{16,0},{224,240},{17,1},{225,241},{18,2},{226,242},{19,3},{227,243... | collective-permute-start | bytes 466568 | tf_op jit(solution)/shard_map/ppermute | solution.py:618
  20.6 13.4 %all-to-all-start.1 = ((f32[16,8,768]{2,1,0:T(8,128)}), f32[16,8,768]{2,1,0:T(8,128)}, u32[]{:S(2)}, u32[]{:S(2)}) async-start(f32[16,8,768]{2,1,0:T(8,128)} %get-tuple-element.109), calls=%async_computation.1 | async-start | bytes 786432 | tf_op jit(solution)/shard_map/cond/branch_1_fun/all_to_all | solution.py:602
  33.9 9.2 %copy-start.4 = (s32[16]{0:T(128)S(1)}, s32[16]{0:T(128)}, u32[]{:S(2)}) copy-start(s32[16]{0:T(128)} %param.20) | copy-start | bytes 196
  40.8 2.3 %collective-permute-start.7 = (f32[3,36,360]{2,1,0:T(8,128)S(1)}, f32[3,36,360]{2,1,0:T(8,128)S(1)}, u32[]{:S(2)}, u32[]{:S(2)}) collective-permute-start(f32[3,36,360]{2,1,0:T(8,128)S(1)} %get-tuple-element.172), channel_id=1, source_target_pairs={{0,16},{240,224},{1,17},{241,225},{2,18},{242,226},{3,19},{243,227... | collective-permute-start | bytes 466568 | tf_op jit(solution)/shard_map/ppermute | solution.py:618
  43.1 27.9 %copy-start.3 = (s32[16]{0:T(128)S(1)}, s32[16]{0:T(128)}, u32[]{:S(2)}) copy-start(s32[16]{0:T(128)} %param.19) | copy-start | bytes 196
  69.7 9.0 %collective-permute-start.8 = (f32[16,8,128]{2,1,0:T(8,128)S(1)}, f32[16,8,128]{2,1,0:T(8,128)S(1)}, u32[]{:S(2)}, u32[]{:S(2)}) collective-permute-start(f32[16,8,128]{2,1,0:T(8,128)S(1)} %get-tuple-element.181), channel_id=1, source_target_pairs={{0,16},{240,224},{1,17},{241,225},{2,18},{242,226},{3,19},{243,227... | collective-permute-start | bytes 196616 | tf_op jit(solution)/shard_map/ppermute | solution.py:618

commit v3 on v2

--- a/solution.py
+++ b/solution.py
@@ -20,10 +20,11 @@
 TOP = LAT_DEV - 1
 WIDTH = NLON // LON_DEV
 WIDE = 384
+LAST = (WIDTH - 1) // 128 * 128
 SLABS = FIELDS * LEV
 ROWS = SLABS * BAND
 SHARE = WAVES // LON_DEV
-UNROLL = 4
+UNROLL = 6
 
 FIELD = (FIELDS, LEV, BAND, WIDTH)
 HALF_FIELD = (FIELDS, LEV, HALF, WIDTH)
@@ -135,6 +136,37 @@
     return jnp.where(iota(tile.shape, 1) == slab, column, tile)
 
 
+def exact_dot(value, chosen, left_dim=1, right_dim=0):
+    high, low = split(value)
+    chosen = chosen.astype(jnp.float32).astype(jnp.bfloat16)
+    return pair_dot(high, chosen, left_dim, right_dim) + pair_dot(low, chosen, left_dim, right_dim)
+
+
+def every_lane(values, lane):
+    return exact_dot(values, iota((values.shape[1], 128), 0) == lane)
+
+
+def own_lane(rows):
+    shape = (SLABS * rows, 128)
+    return iota(shape, 0) // rows == iota(shape, 1)
+
+
+def tile_of(values, lane, rows, first):
+    spread = jnp.where(own_lane(rows), every_lane(values, lane), 0.0)
+    shape = (HALF, SLABS * rows)
+    picked = iota(shape, 1) % rows == iota(shape, 0) + first
+    picked = picked.astype(jnp.float32).astype(jnp.bfloat16)
+    high, low = split(spread)
+    return pair_dot(picked, high, 1, 0) + pair_dot(picked, low, 1, 0)
+
+
+def halo_of(tile, wave_lanes, lane, weight):
+    tall = jnp.concatenate([tile] * SLABS, axis=0)
+    spread = exact_dot(jnp.where(own_lane(BAND), tall, 0.0), iota((128, 128), 0) >= 0)
+    filtered = jnp.concatenate([weight] * SLABS, axis=0) > 0.5
+    return spread * jnp.where(filtered, every_lane(wave_lanes, lane), 1.0)
+
+
 def place():
     return lax.axis_index("lon"), lax.axis_index("lat")
 
@@ -183,15 +215,16 @@
     waves = dot(table[:, :WIDTH], field[...].reshape(ROWS, WIDTH), 1, 1)
     send[:, :, :ROWS] = waves.reshape(LON_DEV, SHARE, ROWS)
     finish(*rest)
-    filtered = row_weight(mask, first, (HALF, 1)) > 0.5
-    east = west = jnp.zeros((HALF, 128), jnp.float32)
+    filtered = row_weight(mask, first, (HALF, 128)) > 0.5
+    filtered = jnp.concatenate([filtered.astype(jnp.float32)] * SLABS, axis=0) > 0.5
+    flat = SLABS * HALF, 128
+    coeff, value = to_west[:, :, :, :128].reshape(flat), field[:, :, rows, :128].reshape(flat)
+    west = tile_of(jnp.where(filtered, coeff, coeff * value), 0, HALF, 0)
+    flat, filtered = (flat[0], WIDTH - LAST), filtered[:, : WIDTH - LAST]
+    coeff, value = to_east[:, :, :, LAST:].reshape(flat), field[:, :, rows, LAST:].reshape(flat)
+    east = tile_of(jnp.where(filtered, coeff, coeff * value), WIDTH - LAST - 1, HALF, 0)
     for slab in range(SLABS):
         at = slab // LEV, slab % LEV
-        value = field[*at, rows]
-        coeff = to_east[at][:, WIDTH - 1 :]
-        east = with_lane(east, slab, jnp.where(filtered, coeff, coeff * value[:, WIDTH - 1 :]))
-        coeff = to_west[at][:, 0:1]
-        west = with_lane(west, slab, jnp.where(filtered, coeff, coeff * value[:, 0:1]))
         sign = 1.0 if at[0] == FIELDS - 1 else -1.0
         lines = pole[at]
         line = jnp.where(top, lines[HALF - 1 :], lines[0:1])
@@ -298,15 +331,16 @@
 
 
 def middle_kernel(
-    waves, table_in, mask_in, state_in, extra_in, coeff_in, opened_in, beyond_in,
+    waves_in, table_in, mask_in, state_in, extra_in, coeff_in, opened_in, beyond_in,
     send, to_next, next_line, edges, across, middle_out,
-    table, mask, state, extra, coeff_ref, opened, beyond, middle,
-    filtered, opposite, sems,
+    waves, table, mask, state, extra, coeff_ref, opened, beyond, middle,
+    filtered, opposite, halos, ends, sems,
 ):
     lon, lat = place()
     top = lat == TOP
-    table_copy, *rest = begin(
+    waves_copy, table_copy, *rest = begin(
         sems,
+        (waves_in, waves),
         (table_in.at[lon], table),
         (mask_in, mask),
         (opened_in, opened),
@@ -314,9 +348,9 @@
         *by_field((state_in, state), (extra_in, extra), (coeff_in, coeff_ref)),
     )
     rest, fields = rest[:3], rest[3:]
+    finish(waves_copy, table_copy)
     for tile in range(TILED):
         across[tile_place(tile)] = waves[tile, :, MORE:]
-    finish(table_copy)
     flat = waves[:, :, :ROWS].reshape(WAVES, ROWS)
     filtered[...] = dot(flat, table[...], 0, 0)
     polar_row = jnp.where(top, BAND - 1, 0)
@@ -328,22 +362,21 @@
         closed = jnp.concatenate([waves[sides[side], :, ROWS:MORE], blank], axis=1)
         edges[side] = whole_band(closed, opened[side], top)
     weight = row_weight(mask, 0, (BAND, WIDTH))
-    is_filtered = weight[:, 0:1] > 0.5
+    narrow = row_weight(mask, 0, (BAND, 128))
+    for side, lane in enumerate((WIDTH + 1 - LAST, WIDTH - LAST)):
+        halos[side] = halo_of(edges[side], filtered[:, LAST:], lane, narrow)
     next_weight = jnp.where(top, weight[0:1], weight[BAND - 1 :])
     row = iota((BAND, WIDTH), 0)
 
     def one(field, level, carry):
-        east_tile, west_tile = carry
         slab = field * LEV + level
         here = pl.ds(slab, 1)
         value = state[field, level]
         smooth = filtered[pl.ds(slab * BAND, BAND)]
         value = value + weight * (smooth[:, :WIDTH] - value)
         coeff = load_coeff(coeff_ref, field, level)
-        west = lane_of(edges[0], slab)
-        west = jnp.where(is_filtered, west * smooth[:, WIDTH + 1 : WIDTH + 2], west)
-        east = lane_of(edges[1], slab)
-        east = jnp.where(is_filtered, east * smooth[:, WIDTH : WIDTH + 1], east)
+        band = pl.ds(slab * BAND, BAND)
+        west, east = halos[0, band, 0:1], halos[1, band, 0:1]
         halo = beyond[2, here]
         total, north, south = gather_terms(
             value, coeff, jnp.where(top, halo, 0.0), jnp.where(top, 0.0, halo), west, east
@@ -358,21 +391,19 @@
         to_next[1, here] = (1.0 - next_weight) * near_coeff * near
         to_next[2, here] = next_weight * near_coeff
         next_line[here] = beyond[1, here] * (beyond[0, here] + product)
-        column = (coeff[3] * total)[:, WIDTH - 1 :]
-        east_tile = with_lane(east_tile, slab, jnp.where(top, column[:HALF], column[HALF:]))
-        column = (coeff[4] * total)[:, 0:1]
-        west_tile = with_lane(west_tile, slab, jnp.where(top, column[:HALF], column[HALF:]))
-        return east_tile, west_tile
-
-    none = jnp.zeros((HALF, 128), jnp.float32)
-    carry, stored = (none, none), []
+        ends[0, band, : WIDTH - LAST] = (coeff[3] * total)[:, LAST:]
+        ends[1, band] = (coeff[4] * total)[:, :128]
+        return carry
+
+    stored = []
     for field in range(FIELDS):
         finish(*fields[3 * field : 3 * field + 3])
-        carry = for_levels(field, one, carry)
+        for_levels(field, one)
         stored += begin(sems.at[field : field + 1], (middle.at[field], middle_out.at[field]))
-    east_tile, west_tile = carry
     sums = dot(table[:, :WIDTH], middle[...].reshape(ROWS, WIDTH), 1, 1)
     send[:, :, :ROWS] = sums.reshape(LON_DEV, SHARE, ROWS)
+    east_tile = tile_of(ends[0, :, : WIDTH - LAST], WIDTH - LAST - 1, BAND, open_row(lat))
+    west_tile = tile_of(ends[1], 0, BAND, open_row(lat))
     for target in range(LON_DEV):
         tile = jnp.where(target == (lon + 1) % LON_DEV, east_tile, west_tile)
         send[target, :, ROWS:] = tile[:, :64]
@@ -380,15 +411,16 @@
 
 
 def final_kernel(
-    waves, table_in, mask_in, middle_in, coeff_in, edges_in, opened_in, line_in, across_in,
+    waves_in, table_in, mask_in, middle_in, coeff_in, edges_in, opened_in, line_in, across_in,
     out,
-    table, mask, middle, coeff_ref, edges, opened, next_line, across, result,
-    filtered, opposite, sems,
+    waves, table, mask, middle, coeff_ref, edges, opened, next_line, across, result,
+    filtered, opposite, halos, sems,
 ):
     lon, lat = place()
     top = lat == TOP
-    table_copy, *rest = begin(
+    waves_copy, table_copy, *rest = begin(
         sems,
+        (waves_in, waves),
         (table_in.at[lon], table),
         (mask_in, mask),
         (edges_in, edges),
@@ -398,18 +430,19 @@
         *by_field((middle_in, middle), (coeff_in, coeff_ref)),
     )
     rest, fields = rest[:5], rest[5:]
-    finish(table_copy)
+    finish(waves_copy, table_copy)
     flat = waves[:, :, :ROWS].reshape(WAVES, ROWS)
     filtered[...] = dot(flat, table[...], 0, 0)
     polar_row = jnp.where(top, BAND - 1, 0)
     opposite[...] = across_pole(flat, table[...], polar_row)
     finish(*rest)
     weight = row_weight(mask, 0, (BAND, WIDTH))
-    is_filtered = weight[:, 0:1] > 0.5
     row = iota((BAND, WIDTH), 0)
     none = jnp.zeros((HALF, 128), jnp.float32)
-    west_band = whole_band(none, opened[0], top)
-    east_band = whole_band(none, opened[1], top)
+    narrow = row_weight(mask, 0, (BAND, 128))
+    for side, lane in enumerate((WIDTH + 1 - LAST, WIDTH - LAST)):
+        tile = jnp.where(narrow > 0.5, edges[side], whole_band(none, opened[side], top))
+        halos[side] = halo_of(tile, filtered[:, LAST:], lane, narrow)
 
     def one(field, level, carry):
         slab = field * LEV + level
@@ -418,10 +451,8 @@
         smooth = filtered[pl.ds(slab * BAND, BAND)]
         value = value + weight * (smooth[:, :WIDTH] - value)
         coeff = load_coeff(coeff_ref, field, level)
-        west = lane_of(edges[0], slab) * smooth[:, WIDTH + 1 : WIDTH + 2]
-        west = jnp.where(is_filtered, west, lane_of(west_band, slab))
-        east = lane_of(edges[1], slab) * smooth[:, WIDTH : WIDTH + 1]
-        east = jnp.where(is_filtered, east, lane_of(east_band, slab))
+        band = pl.ds(slab * BAND, BAND)
+        west, east = halos[0, band, 0:1], halos[1, band, 0:1]
         halo = next_line[here]
         total, _, _ = gather_terms(
             value, coeff, jnp.where(top, halo, 0.0), jnp.where(top, 0.0, halo), west, east
@@ -625,7 +656,8 @@
     small = pltpu.SMEM((BAND,), jnp.int32)
     plain = range(1, TOP)
     table_scratch = in_vmem((WAVES, WIDE))
-    wave_scratch = [in_vmem((ROWS, WIDE)), in_vmem((128, WIDE))]
+    halo_scratch = in_vmem((2, ROWS, 128))
+    wave_scratch = [in_vmem((ROWS, WIDE)), in_vmem((128, WIDE)), halo_scratch]
     one_edge = (BAND, 128)
 
     def blanks(*shapes):
@@ -695,10 +727,9 @@
             [waves, table, polar_mask, adjoint_state, innovation, coefficients, opened, beyond],
             [CHUNKS, LINES, LINE, EDGES, ACROSS],
             [FIELD],
-            [table_scratch, small, in_vmem(FIELD), in_vmem(FIELD), in_vmem(COEFF)]
-            + [in_vmem(TILES), in_vmem(LINES), in_vmem(FIELD), *wave_scratch],
-            copies=13,
-            near=1,
+            [in_vmem(FIRST_CHUNKS), table_scratch, small, in_vmem(FIELD), in_vmem(FIELD), in_vmem(COEFF)]
+            + [in_vmem(TILES), in_vmem(LINES), in_vmem(FIELD), *wave_scratch, halo_scratch],
+            copies=14,
         ))
 
     def plain_third():
@@ -709,17 +740,17 @@
 
     def polar_fourth():
         received = exchanged(send)
-        again, opened = launch(
-            second_respond_kernel,
+        again, opened, result = launch(
+            second_respond_kernel_with_blank,
             [received, wave_cutoff],
             [CHUNKS, TILES],
-            (),
+            [FIELD],
             [small],
             copies=1,
             near=1,
         )
         waves = exchanged(again)
-        return waves, lax.slice_in_dim(waves, MORE - 128, MORE, axis=2), opened, middle
+        return waves, lax.slice_in_dim(waves, MORE - 128, MORE, axis=2), opened, result
 
     def plain_fourth():
         west, east = edge[0], edge[1]
@@ -750,13 +781,12 @@
     def polar_fifth():
         (out,) = launch(
             final_kernel,
-            [waves, table, polar_mask, result, coefficients, edges, opened, next_line, across],
+            [waves, table, polar_mask, middle, coefficients, edges, opened, next_line, across],
             (),
             [FIELD],
-            [table_scratch, small, in_vmem(FIELD), in_vmem(COEFF), in_vmem(EDGES)]
+            [in_vmem(CHUNKS), table_scratch, small, in_vmem(FIELD), in_vmem(COEFF), in_vmem(EDGES)]
             + [in_vmem(TILES), in_vmem(LINE), in_vmem(ACROSS), in_vmem(FIELD), *wave_scratch],
-            copies=12,
-            near=1,
+            copies=13,
             pinned=True,
         )
         return out
@@ -777,6 +807,10 @@
 
 def forward_kernel_with_blanks(*refs):
     forward_kernel(*refs[:5], *refs[9:])
+
+
+def second_respond_kernel_with_blank(*refs):
+    second_respond_kernel(*refs[:4], *refs[5:])
 
 
 def solution(mesh):

time: 79.4 us -> 76 us (0.957)
  the two profiles are of different devices: /device:TPU:8 before, /device:TPU:1 now
where the time goes in v3:
time: 76 us; the launch traced here: 75.5 us
  waiting for transfers between devices  30.6 us (40%)
  starting transfers between devices  25.1 us (33%)
  Pallas kernels  17.1 us (23%)
  local copies, waits for them, and re-layouts  2.46 us (3%)
    ppermute x6, starting transfers between devices, moved(): return lax.ppermute(value, ('lat', 'lon'), pairs)  19.9 us
    ppermute x6, waiting for transfers between devices, moved(): return lax.ppermute(value, ('lat', 'lon'), pairs)  17.2 us
    pallas_call x5, Pallas kernels, launch(): pl.pallas_call(kernel, in_specs=[pl.BlockSpec(memory_space=pltpu.VMEM)] *...  17.1 us
    ppermute x3, waiting for transfers between devices, next_to_pole(): return lax.ppermute(value, ('lat', 'lon'), pairs)  13.4 us
    ppermute x3, starting transfers between devices, next_to_pole(): return lax.ppermute(value, ('lat', 'lon'), pairs)  5.21 us
    another operation x12, local copies, waits for them, and re-layouts  2.43 us
  transfers between devices with their start and end apart: 9, of which 6 were waited for; matrix products, arithmetic and copies ran while one was open for 1% of the time, Pallas kernels for 0%

profile of v3, /device:TPU:1, one launch (start us, length us, event | category | flops | bytes accessed | tf_op | source)
XLA Modules:
  0.0 75.5 jit_solution(17933452194363951474)
XLA Ops:
  0.0 21.7 %conditional.5 = (f32[16,8,768]{2,1,0:T(8,128)}, f32[2,8,128]{2,1,0:T(8,128)S(1)}, f32[3,36,360]{2,1,0:T(8,128)S(1)}, f32[3,36,360]{2,1,0:T(8,128)S(1)}, f32[3,3...) conditional(s32[]{:T(128)} %convert_element_type.2, (f32[3,12,16,360]{3,2,1,0:T(8,128)}, ...), branch_computations={%region_0.0_spmd, %region_1.0_spmd} | conditional | flops 4096 | bytes 31721280 | solution.py:711
  0.0 0.0 copy-start
  0.0 0.0 copy-start.2
  0.0 2.2 %branch_0_fun.4 = f32[2,16,128]{2,1,0:T(8,128)S(1)} custom-call(f32[3,12,16,360]{3,2,1,0:T(8,128)} %get-tuple-element.88.field_in, f32[3,5,12,16,360]{4,3,2,1,0:T(8,128)} %get-tuple-element.90.coeff_in), custom_call_target="tpu_custom_call" | custom-call | bytes 4993024 | tf_op jit(solution)/shard_map/cond/branch_0_fun/pallas_call | solution.py:82
  2.2 7.8 %collective-permute-start.3 = (f32[16,128]{1,0:T(8,128)S(1)}, f32[16,128]{1,0:T(8,128)S(1)}, u32[]{:S(2)}, u32[]{:S(2)}) collective-permute-start(f32[16,128]{1,0:T(8,128)S(1)} %get-tuple-element.181), channel_id=1, source_target_pairs={{16,31},{17,16},{18,17},{19,18},{20,19},{21,20},{22,21},{23,22},{2... | collective-permute-start | bytes 24584 | tf_op jit(solution)/shard_map/cond/branch_0_fun/ppermute | solution.py:640
  10.0 1.9 %collective-permute-start.2 = (f32[16,128]{1,0:T(8,128)S(1)}, f32[16,128]{1,0:T(8,128)S(1)}, u32[]{:S(2)}, u32[]{:S(2)}) collective-permute-start(f32[16,128]{1,0:T(8,128)S(1)} %get-tuple-element.182), channel_id=1, source_target_pairs={{16,17},{17,18},{18,19},{19,20},{20,21},{21,22},{22,23},{23,24},{2... | collective-permute-start | bytes 24584 | tf_op jit(solution)/shard_map/cond/branch_0_fun/ppermute | solution.py:640
  11.9 0.0 collective-permute-done.3.east_in
  11.9 5.8 %collective-permute-done.2.west_in = f32[16,128]{1,0:T(8,128)S(1)} collective-permute-done((f32[16,128]{1,0:T(8,128)S(1)}, f32[16,128]{1,0:T(8,128)S(1)}, u32[]{:S(2)}, u32[]{:S(2)}) %collective-permute-start.2) | collective-permute-done | bytes 8224 | tf_op jit(solution)/shard_map/cond/branch_0_fun/ppermute | solution.py:640
  17.7 0.0 copy-done
  17.7 0.0 copy-done.2
  17.7 3.2 %branch_0_fun.5 = (f32[3,36,360]{2,1,0:T(8,128)S(1)}, f32[3,36,360]{2,1,0:T(8,128)S(1)}, f32[3,36,360]{2,1,0:T(8,128)S(1)}) custom-call(f32[3,12,16,360]{3,2,1,0:T(8,128)S(1)} %copy-done.2, f32[3,12,16,360]{3,2,1,0:T(8,128)} %get-tuple-element.89.extra_in, f32[3,5,12,16,360]{4,3,2,1,0:T(8,128)S(1)} %copy-done, f32[16,128]{1,0:T(8,128)S(1)} %collective-permute-done.2.west_in, ...), custom_call_target="tpu_custom_call" | custom-call | bytes 6289024 | tf_op jit(solution)/shard_map/cond/branch_0_fun/pallas_call | solution.py:82
  20.9 0.8 %broadcast.24 = f32[16,8,768]{2,1,0:T(8,128)} broadcast(f32[]{:T(128)} %constant.3.clone), dimensions={} | broadcast | bytes 393220 | tf_op jit(solution)/shard_map/broadcast.3
  21.7 2.6 %collective-permute-start.6 = (f32[3,36,360]{2,1,0:T(8,128)S(1)}, f32[3,36,360]{2,1,0:T(8,128)S(1)}, u32[]{:S(2)}, u32[]{:S(2)}) collective-permute-start(f32[3,36,360]{2,1,0:T(8,128)S(1)} %get-tuple-element.170), channel_id=1, source_target_pairs={{16,0},{224,240},{17,1},{225,241},{18,2},{226,242},{19,3},{227,243... | collective-permute-start | bytes 466568 | tf_op jit(solution)/shard_map/ppermute | solution.py:649
  24.3 11.6 %conditional.6 = (f32[16,8,768]{2,1,0:T(8,128)}, f32[3,36,360]{2,1,0:T(8,128)S(1)}, f32[3,36,360]{2,1,0:T(8,128)S(1)}) conditional(s32[]{:T(128)} %convert_element_type.2, (f32[3,36,360]{2,1,0:T(8,128)S(1)}, f32[3,36,360]{2,1,0:T(8,128)S(1)}) %tuple.48, (f32[16,8,768]{2,1,0:T(8,128)}, f32[3,36,360]{2,1,0:T(8,128)S(1)}, ...), branch_computations={%region_2.0_spmd, %region_3.0_spmd} | conditional | bytes 1801784 | solution.py:722
  24.3 3.6 %collective-permute-start = (f32[3,36,360]{2,1,0:T(8,128)S(1)}, f32[3,36,360]{2,1,0:T(8,128)S(1)}, u32[]{:S(2)}, u32[]{:S(2)}) collective-permute-start(f32[3,36,360]{2,1,0:T(8,128)S(1)} %get-tuple-element.106), channel_id=1, source_target_pairs={{16,32},{17,33},{18,34},{19,35},{20,36},{21,37},{22,38},{23,39},{2... | collective-permute-start | bytes 466568 | tf_op jit(solution)/shard_map/cond/branch_0_fun/ppermute | solution.py:640
  27.9 1.3 %collective-permute-start.1 = (f32[3,36,360]{2,1,0:T(8,128)S(1)}, f32[3,36,360]{2,1,0:T(8,128)S(1)}, u32[]{:S(2)}, u32[]{:S(2)}) collective-permute-start(f32[3,36,360]{2,1,0:T(8,128)S(1)} %get-tuple-element.107), channel_id=1, source_target_pairs={{32,16},{33,17},{34,18},{35,19},{36,20},{37,21},{38,22},{39,23},{4... | collective-permute-start | bytes 466568 | tf_op jit(solution)/shard_map/cond/branch_0_fun/ppermute | solution.py:640
  29.2 1.2 %collective-permute-done = f32[3,36,360]{2,1,0:T(8,128)S(1)} collective-permute-done((f32[3,36,360]{2,1,0:T(8,128)S(1)}, f32[3,36,360]{2,1,0:T(8,128)S(1)}, u32[]{:S(2)}, u32[]{:S(2)}) %collective-permute-start) | collective-permute-done | bytes 155552 | tf_op jit(solution)/shard_map/cond/branch_0_fun/ppermute | solution.py:640
  30.4 4.8 %collective-permute-done.1 = f32[3,36,360]{2,1,0:T(8,128)S(1)} collective-permute-done((f32[3,36,360]{2,1,0:T(8,128)S(1)}, f32[3,36,360]{2,1,0:T(8,128)S(1)}, u32[]{:S(2)}, u32[]{:S(2)}) %collective-permute-start.1) | collective-permute-done | bytes 155552 | tf_op jit(solution)/shard_map/cond/branch_0_fun/ppermute | solution.py:640
  35.2 0.8 %broadcast.26 = f32[16,8,768]{2,1,0:T(8,128)} broadcast(f32[]{:T(128)} %constant.8.clone), dimensions={} | broadcast | bytes 393220 | tf_op jit(solution)/shard_map/broadcast.5
  36.0 0.0 collective-permute-done.6
  36.0 0.0 copy-start.4
  36.0 0.2 conditional.7
  36.0 0.1 broadcast.32
  36.1 1.3 %collective-permute-start.7 = (f32[3,36,360]{2,1,0:T(8,128)S(1)}, f32[3,36,360]{2,1,0:T(8,128)S(1)}, u32[]{:S(2)}, u32[]{:S(2)}) collective-permute-start(f32[3,36,360]{2,1,0:T(8,128)S(1)} %get-tuple-element.171), channel_id=1, source_target_pairs={{0,16},{240,224},{1,17},{241,225},{2,18},{242,226},{3,19},{243,227... | collective-permute-start | bytes 466568 | tf_op jit(solution)/shard_map/ppermute | solution.py:649
  37.4 7.2 %collective-permute-done.7.polar_in = f32[3,36,360]{2,1,0:T(8,128)S(1)} collective-permute-done((f32[3,36,360]{2,1,0:T(8,128)S(1)}, f32[3,36,360]{2,1,0:T(8,128)S(1)}, u32[]{:S(2)}, u32[]{:S(2)}) %collective-permute-start.7) | collective-permute-done | bytes 155552 | tf_op jit(solution)/shard_map/ppermute | solution.py:649
  44.6 0.0 copy-done.4
  44.6 0.0 copy-start.3
  44.6 21.2 %conditional.8 = (f32[16,8,640]{2,1,0:T(8,128)}, f32[16,8,128]{2,1,0:T(8,128)S(1)}, f32[2,8,128]{2,1,0:T(8,128)S(1)}, f32[3,12,16,360]{3,2,1,0:T(8,128)}) conditional(s32[]{:T(128)} %convert_element_type.2, (f32[2,16,128]{2,1,0:T(8,128)S(1)}, f32[3,12,16,360]{3,2,1,0:T(8,128)}, f32[3,12,16,360]{3,2,1,0:T(8,128)}, f32[3,5,12,16,360]{4,3,2,1,0:T(8,128)}, ...), branch_computations={%region_6.0_spmd, %region_7.0_spmd} | conditional | bytes 30286104 | solution.py:778
  44.6 0.0 copy-start.1
  44.6 6.1 %branch_0_fun.6 = (f32[2,16,128]{2,1,0:T(8,128)S(1)}, f32[2,36,360]{2,1,0:T(8,128)S(1)}, f32[3,12,16,360]{3,2,1,0:T(8,128)S(1)}) custom-call(f32[3,12,16,360]{3,2,1,0:T(8,128)} %get-tuple-element.119.state_in, f32[3,12,16,360]{3,2,1,0:T(8,128)} %get-tuple-element.120.extra_in, f32[3,5,12,16,360]{4,3,2,1,0:T(8,128)} %get-tuple-element.121.coeff_in, ...), custom_call_target="tpu_custom_call" | custom-call | bytes 7238528 | tf_op jit(solution)/shard_map/cond/branch_0_fun/pallas_call | solution.py:82
  50.7 3.0 %collective-permute-start.5 = (f32[16,128]{1,0:T(8,128)S(1)}, f32[16,128]{1,0:T(8,128)S(1)}, u32[]{:S(2)}, u32[]{:S(2)}) collective-permute-start(f32[16,128]{1,0:T(8,128)S(1)} %get-tuple-element.183), channel_id=1, source_target_pairs={{16,31},{17,16},{18,17},{19,18},{20,19},{21,20},{22,21},{23,22},{2... | collective-permute-start | bytes 24584 | tf_op jit(solution)/shard_map/cond/branch_0_fun/ppermute | solution.py:640
  53.7 2.3 %collective-permute-start.4 = (f32[16,128]{1,0:T(8,128)S(1)}, f32[16,128]{1,0:T(8,128)S(1)}, u32[]{:S(2)}, u32[]{:S(2)}) collective-permute-start(f32[16,128]{1,0:T(8,128)S(1)} %get-tuple-element.184), channel_id=1, source_target_pairs={{16,17},{17,18},{18,19},{19,20},{20,21},{21,22},{22,23},{23,24},{2... | collective-permute-start | bytes 24584 | tf_op jit(solution)/shard_map/cond/branch_0_fun/ppermute | solution.py:640
  56.0 0.0 collective-permute-done.5.east_in
  56.0 5.4 %collective-permute-done.4.west_in = f32[16,128]{1,0:T(8,128)S(1)} collective-permute-done((f32[16,128]{1,0:T(8,128)S(1)}, f32[16,128]{1,0:T(8,128)S(1)}, u32[]{:S(2)}, u32[]{:S(2)}) %collective-permute-start.4) | collective-permute-done | bytes 8224 | tf_op jit(solution)/shard_map/cond/branch_0_fun/ppermute | solution.py:640
  61.4 0.0 copy-done.1
  61.4 3.6 %branch_0_fun.7 = f32[3,12,16,360]{3,2,1,0:T(8,128)} custom-call(f32[3,12,16,360]{3,2,1,0:T(8,128)S(1)} %get-tuple-element.126.middle_in, f32[3,5,12,16,360]{4,3,2,1,0:T(8,128)S(1)} %copy-done.1, f32[16,128]{1,0:T(8,128)S(1)} %collective-permute-done.4.west_in, f32[16,128]{1,0:T(8,128)S(1)} %collective-permute-done.5.east_in, ...), custom_call_target="tpu_custom_call" | custom-call | bytes 5926144 | tf_op jit(solution)/shard_map/cond/branch_0_fun/pallas_call | solution.py:82
  65.0 0.7 broadcast.33
  65.8 1.3 %collective-permute-start.8 = (f32[16,8,128]{2,1,0:T(8,128)S(1)}, f32[16,8,128]{2,1,0:T(8,128)S(1)}, u32[]{:S(2)}, u32[]{:S(2)}) collective-permute-start(f32[16,8,128]{2,1,0:T(8,128)S(1)} %get-tuple-element.180), channel_id=1, source_target_pairs={{0,16},{240,224},{1,17},{241,225},{2,18},{242,226},{3,19},{243,227... | collective-permute-start | bytes 196616 | tf_op jit(solution)/shard_map/ppermute | solution.py:649
  67.1 0.0 copy-done.3
  67.1 6.3 %collective-permute-done.8.waves_in = f32[16,8,128]{2,1,0:T(8,128)S(1)} collective-permute-done((f32[16,8,128]{2,1,0:T(8,128)S(1)}, f32[16,8,128]{2,1,0:T(8,128)S(1)}, u32[]{:S(2)}, u32[]{:S(2)}) %collective-permute-start.8) | collective-permute-done | bytes 65568 | tf_op jit(solution)/shard_map/ppermute | solution.py:649
  73.3 2.2 %shard_map.64 = f32[3,12,16,360]{3,2,1,0:T(8,128)} custom-call(f32[3,12,16,360]{3,2,1,0:T(8,128)} %get-tuple-element.226.result_in, f32[16,8,128]{2,1,0:T(8,128)S(1)} %collective-permute-done.8.waves_in, f32[16,128,384]{2,1,0:T(8,128)} %constant.5.clone.table_in, f32[3,36,360]{2,1,0:T(8,128)S(1)} %collective-permute-done.7.polar_in), custom_call_target="tpu_custom_call", output_to_operand_aliasing={{}: (0, {})} | custom-call | bytes 5025664 | tf_op jit(solution)/shard_map/pallas_call | solution.py:82
  (13 shorter events, 0.1 us)
Async XLA Ops:
  0.0 17.7 %copy-start = (f32[3,5,12,16,360]{4,3,2,1,0:T(8,128)S(1)}, f32[3,5,12,16,360]{4,3,2,1,0:T(8,128)}, u32[]{:S(2)}) copy-start(f32[3,5,12,16,360]{4,3,2,1,0:T(8,128)} %get-tuple-element.90.coeff_in) | copy-start | bytes 12441604 | tf_op jit(solution)/shard_map/cond
  0.0 17.7 %copy-start.2 = (f32[3,12,16,360]{3,2,1,0:T(8,128)S(1)}, f32[3,12,16,360]{3,2,1,0:T(8,128)}, u32[]{:S(2)}) copy-start(f32[3,12,16,360]{3,2,1,0:T(8,128)} %get-tuple-element.88.field_in) | copy-start | bytes 2488324 | tf_op jit(solution)/shard_map/cond
  2.2 9.7 %collective-permute-start.3 = (f32[16,128]{1,0:T(8,128)S(1)}, f32[16,128]{1,0:T(8,128)S(1)}, u32[]{:S(2)}, u32[]{:S(2)}) collective-permute-start(f32[16,128]{1,0:T(8,128)S(1)} %get-tuple-element.181), channel_id=1, source_target_pairs={{16,31},{17,16},{18,17},{19,18},{20,19},{21,20},{22,21},{23,22},{2... | collective-permute-start | bytes 24584 | tf_op jit(solution)/shard_map/cond/branch_0_fun/ppermute | solution.py:640
  10.0 7.7 %collective-permute-start.2 = (f32[16,128]{1,0:T(8,128)S(1)}, f32[16,128]{1,0:T(8,128)S(1)}, u32[]{:S(2)}, u32[]{:S(2)}) collective-permute-start(f32[16,128]{1,0:T(8,128)S(1)} %get-tuple-element.182), channel_id=1, source_target_pairs={{16,17},{17,18},{18,19},{19,20},{20,21},{21,22},{22,23},{23,24},{2... | collective-permute-start | bytes 24584 | tf_op jit(solution)/shard_map/cond/branch_0_fun/ppermute | solution.py:640
  21.7 14.3 %collective-permute-start.6 = (f32[3,36,360]{2,1,0:T(8,128)S(1)}, f32[3,36,360]{2,1,0:T(8,128)S(1)}, u32[]{:S(2)}, u32[]{:S(2)}) collective-permute-start(f32[3,36,360]{2,1,0:T(8,128)S(1)} %get-tuple-element.170), channel_id=1, source_target_pairs={{16,0},{224,240},{17,1},{225,241},{18,2},{226,242},{19,3},{227,243... | collective-permute-start | bytes 466568 | tf_op jit(solution)/shard_map/ppermute | solution.py:649
  24.3 6.0 %collective-permute-start = (f32[3,36,360]{2,1,0:T(8,128)S(1)}, f32[3,36,360]{2,1,0:T(8,128)S(1)}, u32[]{:S(2)}, u32[]{:S(2)}) collective-permute-start(f32[3,36,360]{2,1,0:T(8,128)S(1)} %get-tuple-element.106), channel_id=1, source_target_pairs={{16,32},{17,33},{18,34},{19,35},{20,36},{21,37},{22,38},{23,39},{2... | collective-permute-start | bytes 466568 | tf_op jit(solution)/shard_map/cond/branch_0_fun/ppermute | solution.py:640
  27.9 7.3 %collective-permute-start.1 = (f32[3,36,360]{2,1,0:T(8,128)S(1)}, f32[3,36,360]{2,1,0:T(8,128)S(1)}, u32[]{:S(2)}, u32[]{:S(2)}) collective-permute-start(f32[3,36,360]{2,1,0:T(8,128)S(1)} %get-tuple-element.107), channel_id=1, source_target_pairs={{32,16},{33,17},{34,18},{35,19},{36,20},{37,21},{38,22},{39,23},{4... | collective-permute-start | bytes 466568 | tf_op jit(solution)/shard_map/cond/branch_0_fun/ppermute | solution.py:640
  36.0 8.6 %copy-start.4 = (s32[16]{0:T(128)S(1)}, s32[16]{0:T(128)}, u32[]{:S(2)}) copy-start(s32[16]{0:T(128)} %param.20) | copy-start | bytes 196
  36.1 8.5 %collective-permute-start.7 = (f32[3,36,360]{2,1,0:T(8,128)S(1)}, f32[3,36,360]{2,1,0:T(8,128)S(1)}, u32[]{:S(2)}, u32[]{:S(2)}) collective-permute-start(f32[3,36,360]{2,1,0:T(8,128)S(1)} %get-tuple-element.171), channel_id=1, source_target_pairs={{0,16},{240,224},{1,17},{241,225},{2,18},{242,226},{3,19},{243,227... | collective-permute-start | bytes 466568 | tf_op jit(solution)/shard_map/ppermute | solution.py:649
  44.6 22.5 %copy-start.3 = (s32[16]{0:T(128)S(1)}, s32[16]{0:T(128)}, u32[]{:S(2)}) copy-start(s32[16]{0:T(128)} %param.19) | copy-start | bytes 196
  44.6 16.8 %copy-start.1 = (f32[3,5,12,16,360]{4,3,2,1,0:T(8,128)S(1)}, f32[3,5,12,16,360]{4,3,2,1,0:T(8,128)}, u32[]{:S(2)}) copy-start(f32[3,5,12,16,360]{4,3,2,1,0:T(8,128)} %get-tuple-element.121.coeff_in) | copy-start | bytes 12441604 | tf_op jit(solution)/shard_map/cond
  50.7 5.3 %collective-permute-start.5 = (f32[16,128]{1,0:T(8,128)S(1)}, f32[16,128]{1,0:T(8,128)S(1)}, u32[]{:S(2)}, u32[]{:S(2)}) collective-permute-start(f32[16,128]{1,0:T(8,128)S(1)} %get-tuple-element.183), channel_id=1, source_target_pairs={{16,31},{17,16},{18,17},{19,18},{20,19},{21,20},{22,21},{23,22},{2... | collective-permute-start | bytes 24584 | tf_op jit(solution)/shard_map/cond/branch_0_fun/ppermute | solution.py:640
  53.7 7.7 %collective-permute-start.4 = (f32[16,128]{1,0:T(8,128)S(1)}, f32[16,128]{1,0:T(8,128)S(1)}, u32[]{:S(2)}, u32[]{:S(2)}) collective-permute-start(f32[16,128]{1,0:T(8,128)S(1)} %get-tuple-element.184), channel_id=1, source_target_pairs={{16,17},{17,18},{18,19},{19,20},{20,21},{21,22},{22,23},{23,24},{2... | collective-permute-start | bytes 24584 | tf_op jit(solution)/shard_map/cond/branch_0_fun/ppermute | solution.py:640
  65.8 7.6 %collective-permute-start.8 = (f32[16,8,128]{2,1,0:T(8,128)S(1)}, f32[16,8,128]{2,1,0:T(8,128)S(1)}, u32[]{:S(2)}, u32[]{:S(2)}) collective-permute-start(f32[16,8,128]{2,1,0:T(8,128)S(1)} %get-tuple-element.180), channel_id=1, source_target_pairs={{0,16},{240,224},{1,17},{241,225},{2,18},{242,226},{3,19},{243,227... | collective-permute-start | bytes 196616 | tf_op jit(solution)/shard_map/ppermute | solution.py:649

commit v4 on v3

--- a/solution.py
+++ b/solution.py
@@ -215,16 +215,15 @@
     waves = dot(table[:, :WIDTH], field[...].reshape(ROWS, WIDTH), 1, 1)
     send[:, :, :ROWS] = waves.reshape(LON_DEV, SHARE, ROWS)
     finish(*rest)
-    filtered = row_weight(mask, first, (HALF, 128)) > 0.5
-    filtered = jnp.concatenate([filtered.astype(jnp.float32)] * SLABS, axis=0) > 0.5
-    flat = SLABS * HALF, 128
-    coeff, value = to_west[:, :, :, :128].reshape(flat), field[:, :, rows, :128].reshape(flat)
-    west = tile_of(jnp.where(filtered, coeff, coeff * value), 0, HALF, 0)
-    flat, filtered = (flat[0], WIDTH - LAST), filtered[:, : WIDTH - LAST]
-    coeff, value = to_east[:, :, :, LAST:].reshape(flat), field[:, :, rows, LAST:].reshape(flat)
-    east = tile_of(jnp.where(filtered, coeff, coeff * value), WIDTH - LAST - 1, HALF, 0)
+    filtered = row_weight(mask, first, (HALF, 1)) > 0.5
+    east = west = jnp.zeros((HALF, 128), jnp.float32)
     for slab in range(SLABS):
         at = slab // LEV, slab % LEV
+        value = field[*at, rows]
+        coeff = to_east[at][:, WIDTH - 1 :]
+        east = with_lane(east, slab, jnp.where(filtered, coeff, coeff * value[:, WIDTH - 1 :]))
+        coeff = to_west[at][:, 0:1]
+        west = with_lane(west, slab, jnp.where(filtered, coeff, coeff * value[:, 0:1]))
         sign = 1.0 if at[0] == FIELDS - 1 else -1.0
         lines = pole[at]
         line = jnp.where(top, lines[HALF - 1 :], lines[0:1])
@@ -276,9 +275,9 @@
     return total * response
 
 
-def first_respond_kernel(received, cutoff_in, tiles_in, send, edges, cutoff, tiles, sems):
+def first_respond_kernel(received, tiles, cutoff_in, send, edges, cutoff, sems):
     lon, _ = place()
-    finish(*begin(sems, (cutoff_in, cutoff), (tiles_in, tiles)))
+    finish(*begin(sems, (cutoff_in, cutoff)))
     total = responded(received, cutoff, edges)
     for target in range(LON_DEV):
         send[target, :, :ROWS] = total
@@ -287,11 +286,13 @@
         send[target, :, MORE:] = received[(target + LON_DEV // 2) % LON_DEV, :, MORE:]
 
 
-def second_respond_kernel(received, cutoff_in, send, edges, cutoff, sems):
+def second_respond_kernel(received, cutoff_in, mask_in, send, edges, cutoff, mask, sems):
     _, lat = place()
-    finish(*begin(sems, (cutoff_in, cutoff)))
+    finish(*begin(sems, (cutoff_in, cutoff), (mask_in, mask)))
     total = responded(received, cutoff, edges)
-    near = row_waves(total, jnp.where(lat == TOP, 0, BAND - 1))
+    near_row = jnp.where(lat == TOP, 0, BAND - 1)
+    near = row_waves(total, near_row)
+    near = with_lane(near, SLABS, mask[near_row].astype(jnp.float32))
     for target in range(LON_DEV):
         send[target, :, :ROWS] = total
         send[target, :, ROWS:] = near[:, :64]
@@ -388,8 +389,7 @@
         near = jnp.where(top, total[0:1], total[BAND - 1 :])
         near_coeff = jnp.where(top, coeff[2][0:1], coeff[1][BAND - 1 :])
         to_next[0, here] = product
-        to_next[1, here] = (1.0 - next_weight) * near_coeff * near
-        to_next[2, here] = next_weight * near_coeff
+        to_next[1, here] = jnp.where(next_weight > 0.5, near_coeff, near_coeff * near)
         next_line[here] = beyond[1, here] * (beyond[0, here] + product)
         ends[0, band, : WIDTH - LAST] = (coeff[3] * total)[:, LAST:]
         ends[1, band] = (coeff[4] * total)[:, :128]
@@ -575,10 +575,11 @@
 
 
 def plain_final_kernel(
-    middle_in, coeff_in, west_in, east_in, lines_in,
-    out,
+    middle_in, coeff_in, west_in, east_in, lines_in, table_in,
+    out, part, table,
     middle, coeff_ref, west_edge, east_edge, lines, sems,
 ):
+    lon, lat = place()
     finish(
         *begin(
             sems,
@@ -587,6 +588,7 @@
             (west_in, west_edge),
             (east_in, east_edge),
             (lines_in, lines),
+            (table_in.at[lon], table),
         )
     )
 
@@ -596,37 +598,31 @@
         coeff = load_coeff(coeff_ref, field, level)
         west, east = lane_of(west_edge[...], slab), lane_of(east_edge[...], slab)
         value = middle[field, level]
-        out[field, level] = gather_terms(value, coeff, lines[0, here], lines[1, here], west, east)[0]
+        total = gather_terms(value, coeff, lines[0, here], lines[1, here], west, east)[0]
+        out[field, level] = total
+        part[field, level] = jnp.where(lat == 1, total[:HALF], total[HALF:])
         return carry
 
     for_slabs(one)
 
 
-def reach_kernel(result_in, waves_in, table_in, polar_in, result_out, part, waves, table, polar, sems):
-    lon, lat = place()
-    next_to = (lat == 1) | (lat == TOP - 1)
+def reach_kernel(part, waves, table, polar, result_in, result_out, changed, sems):
+    _, lat = place()
     bottom = lat == 1
     rows = pl.ds(pl.multiple_of(jnp.where(bottom, 0, HALF), HALF), HALF)
 
-    @pl.when(next_to)
+    @pl.when(bottom | (lat == TOP - 1))
     def _():
-        finish(
-            *begin(
-                sems,
-                (result_in.at[:, :, rows], part),
-                (waves_in, waves),
-                (table_in.at[lon], table),
-                (polar_in, polar),
-            )
-        )
-        smooth = dot(waves[...].reshape(WAVES, 128), table[...], 0, 0)
-        line = polar[1] + polar[2] * smooth[64 : 64 + SLABS, :WIDTH]
+        flat = waves[...].reshape(WAVES, 128)
+        smooth = dot(flat, table[...], 0, 0)[64 : 64 + SLABS, :WIDTH]
+        masked = flat[0:1, 64 + SLABS : 65 + SLABS] > 0.5
+        line = polar[1] * jnp.where(masked, smooth, 1.0)
         row = iota((HALF, WIDTH), 0)
         mine = row == jnp.where(bottom, 0, HALF - 1)
         for slab in range(SLABS):
             at = slab // LEV, slab % LEV
-            part[at] = part[at] + jnp.where(mine, line[slab : slab + 1], 0.0)
-        finish(*begin(sems, (part, result_out.at[:, :, rows])))
+            changed[at] = part[at] + jnp.where(mine, line[slab : slab + 1], 0.0)
+        finish(*begin(sems, (changed, result_out.at[:, :, rows])))
 
 
 def exchanged(chunks):
@@ -677,12 +673,12 @@
         (tiles,) = launch(closed_kernel, [coefficients], [TILES], (), [half, half], copies=2)
         send, opened = launch(
             first_respond_kernel,
-            [received, wave_cutoff, tiles],
+            [received, tiles, wave_cutoff],
             [FIRST_CHUNKS, TILES],
             (),
-            [small, in_vmem(TILES)],
-            copies=2,
-            near=1,
+            [small],
+            copies=1,
+            near=2,
         )
         return send, opened, to_polar, to_north, to_south, edge
 
@@ -725,7 +721,7 @@
         return tuple(launch(
             middle_kernel,
             [waves, table, polar_mask, adjoint_state, innovation, coefficients, opened, beyond],
-            [CHUNKS, LINES, LINE, EDGES, ACROSS],
+            [CHUNKS, (2, *LINE), LINE, EDGES, ACROSS],
             [FIELD],
             [in_vmem(FIRST_CHUNKS), table_scratch, small, in_vmem(FIELD), in_vmem(FIELD), in_vmem(COEFF)]
             + [in_vmem(TILES), in_vmem(LINES), in_vmem(FIELD), *wave_scratch, halo_scratch],
@@ -733,24 +729,24 @@
         ))
 
     def plain_third():
-        return blanks(CHUNKS, LINES, LINE, EDGES, ACROSS, FIELD)
+        return blanks(CHUNKS, (2, *LINE), LINE, EDGES, ACROSS, FIELD)
 
     send, to_next, next_line, edges, across, middle = lax.cond(polar, polar_third, plain_third)
     reached = next_to_pole(to_next, True)
 
     def polar_fourth():
         received = exchanged(send)
-        again, opened, result = launch(
+        again, opened, result, part, own_table = launch(
             second_respond_kernel_with_blank,
-            [received, wave_cutoff],
+            [received, wave_cutoff, polar_mask],
             [CHUNKS, TILES],
-            [FIELD],
-            [small],
-            copies=1,
+            [FIELD, HALF_FIELD, (WAVES, WIDE)],
+            [small, small],
+            copies=2,
             near=1,
         )
         waves = exchanged(again)
-        return waves, lax.slice_in_dim(waves, MORE - 128, MORE, axis=2), opened, result
+        return waves, lax.slice_in_dim(waves, MORE - 128, MORE, axis=2), opened, result, part, own_table
 
     def plain_fourth():
         west, east = edge[0], edge[1]
@@ -760,22 +756,22 @@
             [(2, *one_edge), (2, *LINE)],
             [FIELD],
             [in_vmem(FIELD), in_vmem(FIELD), in_vmem(COEFF), in_vmem(one_edge), in_vmem(one_edge)]
-            + [in_vmem(LINES), in_vmem(LINES), in_vmem(LINES), in_vmem(FIELD)],
+            + [in_vmem(LINES), in_vmem(LINES), in_vmem((2, *LINE)), in_vmem(FIELD)],
             copies=8,
         )
         west = moved(second[0], plain, 0, 1)
         east = moved(second[1], plain, 0, -1)
-        (result,) = launch(
+        result, part, own_table = launch(
             plain_final_kernel,
-            [middle, coefficients, west, east, lines],
-            [FIELD],
+            [middle, coefficients, west, east, lines, table],
+            [FIELD, HALF_FIELD, (WAVES, WIDE)],
             (),
             [in_vmem(FIELD), in_vmem(COEFF), in_vmem(one_edge), in_vmem(one_edge), in_vmem((2, *LINE))],
-            copies=5,
-        )
-        return *blanks(CHUNKS, LAST_TILE, TILES), result
-
-    waves, near_waves, opened, result = lax.cond(polar, polar_fourth, plain_fourth)
+            copies=6,
+        )
+        return *blanks(CHUNKS, LAST_TILE, TILES), result, part, own_table
+
+    waves, near_waves, opened, result, part, own_table = lax.cond(polar, polar_fourth, plain_fourth)
     waves_beyond = next_to_pole(near_waves, True)
 
     def polar_fifth():
@@ -794,12 +790,13 @@
     result = lax.cond(polar, polar_fifth, lambda kept=result: kept)
     (out,) = launch(
         reach_kernel,
-        [result, waves_beyond, table, reached],
+        [part, waves_beyond, own_table, reached, result],
         (),
         [FIELD],
-        [in_vmem(HALF_FIELD), in_vmem(LAST_TILE), table_scratch, in_vmem(LINES)],
-        copies=4,
-        aliases={0: 0},
+        [in_vmem(HALF_FIELD)],
+        copies=1,
+        aliases={4: 0},
+        near=4,
         pinned=True,
     )
     return out
@@ -810,7 +807,7 @@
 
 
 def second_respond_kernel_with_blank(*refs):
-    second_respond_kernel(*refs[:4], *refs[5:])
+    second_respond_kernel(*refs[:5], *refs[8:])
 
 
 def solution(mesh):

time: 76 us -> 74.4 us (0.979)
  the two profiles are of different devices: /device:TPU:1 before, /device:TPU:8 now
where the time goes in v4:
time: 74.4 us; the launch traced here: 73.7 us
  blocking collectives  24.8 us (33%)
  starting transfers between devices  16.9 us (23%)
  Pallas kernels  16.1 us (22%)
  waiting for transfers between devices  14.8 us (20%)
  local copies, waits for them, and re-layouts  0.88 us (1%)
    all_to_all x2, blocking collectives, exchanged(): lax.all_to_all(chunks, 'lon', split_axis=0, concat_axis=0, tiled=True)  24.8 us
    pallas_call x7, Pallas kernels, launch(): pl.pallas_call(kernel, in_specs=[pl.BlockSpec(memory_space=pltpu.VMEM)] *...  16.1 us
    all_to_all x2, waiting for transfers between devices, exchanged(): lax.all_to_all(chunks, 'lon', split_axis=0, concat_axis=0, tiled=True)  13.9 us
    all_to_all x2, starting transfers between devices, exchanged(): lax.all_to_all(chunks, 'lon', split_axis=0, concat_axis=0, tiled=True)  13 us
    ppermute x3, starting transfers between devices, next_to_pole(): return lax.ppermute(value, ('lat', 'lon'), pairs)  3.87 us
  transfers between devices with their start and end apart: 5, of which 3 were waited for; matrix products, arithmetic and copies ran while one was open for 0% of the time, Pallas kernels for 8%

profile of v4, /device:TPU:8, one launch (start us, length us, event | category | flops | bytes accessed | tf_op | source)
XLA Modules:
  0.0 73.7 jit_solution(10719882146617635409)
XLA Ops:
  0.0 19.2 %conditional.5 = (f32[16,8,768]{2,1,0:T(8,128)}, f32[2,8,128]{2,1,0:T(8,128)S(1)}, f32[3,36,360]{2,1,0:T(8,128)S(1)}, f32[3,36,360]{2,1,0:T(8,128)S(1)}, f32[3,3...) conditional(s32[]{:T(128)} %convert_element_type.2, (f32[3,12,16,360]{3,2,1,0:T(8,128)}, ...), branch_computations={%region_0.0_spmd, %region_1.0_spmd} | conditional | flops 4096 | bytes 31721280 | solution.py:707
  0.0 2.9 %branch_1_fun.6 = (f32[16,8,768]{2,1,0:T(8,128)}, f32[3,36,360]{2,1,0:T(8,128)S(1)}, f32[3,36,360]{2,1,0:T(8,128)S(1)}, f32[3,36,360]{2,1,0:T(8,128)S(1)}, f32[2,16,128]{2,1,0:T(8,128)S(1)}) custom-call(f32[3,12,16,360]{3,2,1,0:T(8,128)} %get-tuple-element.97.refs_0_, f32[3,5,12,16,360]{4,3,2,1,0:T(8,128)} %get-tuple-element.98.refs_1_.coeff_in, ...), custom_call_target="tpu_custom_call" | custom-call | bytes 8998592 | tf_op jit(solution)/shard_map/cond/branch_1_fun/pallas_call | solution.py:82
  2.9 0.0 copy-start.4
  2.9 7.4 %all-to-all-start = ((f32[16,8,768]{2,1,0:T(8,128)}), f32[16,8,768]{2,1,0:T(8,128)S(1)}, u32[]{:S(2)}, u32[]{:S(2)}) async-start(f32[16,8,768]{2,1,0:T(8,128)} %get-tuple-element.101), calls=%async_computation | async-start | bytes 786432 | tf_op jit(solution)/shard_map/cond/branch_1_fun/all_to_all | solution.py:629
  10.3 1.3 %branch_1_fun.7.tiles = f32[2,8,128]{2,1,0:T(8,128)S(1)} custom-call(f32[3,5,12,16,360]{4,3,2,1,0:T(8,128)} %get-tuple-element.98.refs_1_.coeff_in), custom_call_target="tpu_custom_call" | custom-call | bytes 4155392 | tf_op jit(solution)/shard_map/cond/branch_1_fun/pallas_call | solution.py:82
  11.6 6.2 %all-to-all-done.received = f32[16,8,768]{2,1,0:T(8,128)S(1)} async-done(((f32[16,8,768]{2,1,0:T(8,128)}), f32[16,8,768]{2,1,0:T(8,128)S(1)}, u32[]{:S(2)}, u32[]{:S(2)}) %all-to-all-start) | async-done | bytes 393248 | tf_op jit(solution)/shard_map/cond/branch_1_fun/all_to_all | solution.py:629
  17.8 0.0 copy-done.4
  17.8 1.4 %branch_1_fun.8 = (f32[16,8,768]{2,1,0:T(8,128)}, f32[2,8,128]{2,1,0:T(8,128)S(1)}) custom-call(f32[16,8,768]{2,1,0:T(8,128)S(1)} %all-to-all-done.received, f32[2,8,128]{2,1,0:T(8,128)S(1)} %branch_1_fun.7.tiles, s32[16]{0:T(128)S(1)} %copy-done.4), custom_call_target="tpu_custom_call" | custom-call | bytes 802880 | tf_op jit(solution)/shard_map/cond/branch_1_fun/pallas_call | solution.py:82
  19.2 1.3 %collective-permute-start.6 = (f32[3,36,360]{2,1,0:T(8,128)S(1)}, f32[3,36,360]{2,1,0:T(8,128)S(1)}, u32[]{:S(2)}, u32[]{:S(2)}) collective-permute-start(f32[3,36,360]{2,1,0:T(8,128)S(1)} %get-tuple-element.182), channel_id=1, source_target_pairs={{16,0},{224,240},{17,1},{225,241},{18,2},{226,242},{19,3},{227,243... | collective-permute-start | bytes 466568 | tf_op jit(solution)/shard_map/ppermute | solution.py:645
  20.5 13.4 %conditional.6 = (f32[16,8,768]{2,1,0:T(8,128)}, f32[3,36,360]{2,1,0:T(8,128)S(1)}, f32[3,36,360]{2,1,0:T(8,128)S(1)}) conditional(s32[]{:T(128)} %convert_element_type.2, (f32[3,36,360]{2,1,0:T(8,128)S(1)}, f32[3,36,360]{2,1,0:T(8,128)S(1)}) %tuple.44, (f32[16,8,768]{2,1,0:T(8,128)}, f32[3,36,360]{2,1,0:T(8,128)S(1)}, ...), branch_computations={%region_2.0_spmd, %region_3.0_spmd} | conditional | bytes 1801784 | solution.py:718
  20.6 5.6 %all-to-all-start.1 = ((f32[16,8,768]{2,1,0:T(8,128)}), f32[16,8,768]{2,1,0:T(8,128)}, u32[]{:S(2)}, u32[]{:S(2)}) async-start(f32[16,8,768]{2,1,0:T(8,128)} %get-tuple-element.111), calls=%async_computation.1 | async-start | bytes 786432 | tf_op jit(solution)/shard_map/cond/branch_1_fun/all_to_all | solution.py:629
  26.2 7.7 %all-to-all-done.1 = f32[16,8,768]{2,1,0:T(8,128)} async-done(((f32[16,8,768]{2,1,0:T(8,128)}), f32[16,8,768]{2,1,0:T(8,128)}, u32[]{:S(2)}, u32[]{:S(2)}) %all-to-all-start.1) | async-done | bytes 393248 | tf_op jit(solution)/shard_map/cond/branch_1_fun/all_to_all | solution.py:629
  33.9 0.0 collective-permute-done.6
  33.9 0.0 copy-start.3
  33.9 5.3 %conditional.7 = ((f32[16,8,640]{2,1,0:T(8,128)S(1)}, f32[2,36,360]{2,1,0:T(8,128)S(1)}, f32[36,360]{1,0:T(8,128)S(1)}, f32[2,16,128]{2,1,0:T(8,128)S(1)}, f32[4...) conditional(s32[]{:T(128)} %convert_element_type.2, () %tuple.46, (f32[16,8,768]{2,1,0:T(8,128)}, ...), branch_computations={%region_4.0_spmd, %region_5.0_spmd} | conditional | bytes 10899272 | solution.py:734
  33.9 5.3 %branch_1_fun.9 = (f32[16,8,640]{2,1,0:T(8,128)S(1)}, f32[2,36,360]{2,1,0:T(8,128)S(1)}, f32[36,360]{1,0:T(8,128)S(1)}, f32[2,16,128]{2,1,0:T(8,128)S(1)}, f32[4...) custom-call(f32[16,8,768]{2,1,0:T(8,128)} %get-tuple-element.114.waves_in, f32[16,128,384]{2,1,0:T(8,128)} %get-tuple-element.115.table_in, ...), custom_call_target="tpu_custom_call" | custom-call | bytes 10899264 | tf_op jit(solution)/shard_map/cond/branch_1_fun/pallas_call | solution.py:82
  39.2 1.3 %collective-permute-start.7 = (f32[2,36,360]{2,1,0:T(8,128)S(1)}, f32[2,36,360]{2,1,0:T(8,128)S(1)}, u32[]{:S(2)}, u32[]{:S(2)}) collective-permute-start(f32[2,36,360]{2,1,0:T(8,128)S(1)} %get-tuple-element.183), channel_id=1, source_target_pairs={{0,16},{240,224},{1,17},{241,225},{2,18},{242,226},{3,19},{243,227... | collective-permute-start | bytes 311048 | tf_op jit(solution)/shard_map/ppermute | solution.py:645
  40.5 1.0 %collective-permute-done.7.polar = f32[2,36,360]{2,1,0:T(8,128)S(1)} collective-permute-done((f32[2,36,360]{2,1,0:T(8,128)S(1)}, f32[2,36,360]{2,1,0:T(8,128)S(1)}, u32[]{:S(2)}, u32[]{:S(2)}) %collective-permute-start.7) | collective-permute-done | bytes 103712 | tf_op jit(solution)/shard_map/ppermute | solution.py:645
  41.5 0.0 copy-done.3
  41.5 26.7 %conditional.8 = (f32[16,8,640]{2,1,0:T(8,128)}, f32[16,8,128]{2,1,0:T(8,128)S(1)}, f32[2,8,128]{2,1,0:T(8,128)S(1)}, f32[3,12,16,360]{3,2,1,0:T(8,128)}, f32[3,...) conditional(s32[]{:T(128)} %convert_element_type.2, (f32[2,16,128]{2,1,0:T(8,128)S(1)}, ...), branch_computations={%region_6.0_spmd, %region_7.0_spmd} | conditional | bytes 33991336 | solution.py:774
  41.5 12.4 %all_to_all.16.refs_0_ = f32[16,8,640]{2,1,0:T(8,128)S(1)} all-to-all(f32[16,8,640]{2,1,0:T(8,128)S(1)} %get-tuple-element.136), channel_id=1, replica_groups=mesh['lat'=16,'lon'=16] {'lon'}, dimensions={0} | all-to-all | bytes 655360 | tf_op jit(solution)/shard_map/cond/branch_1_fun/all_to_all | solution.py:629
  53.9 1.0 %branch_1_fun.10 = (f32[16,8,640]{2,1,0:T(8,128)S(1)}, f32[2,8,128]{2,1,0:T(8,128)S(1)}, f32[3,12,16,360]{3,2,1,0:T(8,128)}, f32[3,12,8,360]{3,2,1,0:T(8,128)S(1)}, f32[128,384]{1,0:T(8,128)S(1)}) custom-call(f32[16,8,640]{2,1,0:T(8,128)S(1)} %all_to_all.16.refs_0_, s32[16]{0:T(128)S(1)} %get-tuple-element.137.refs_1_, s32[16]{0:T(128)} %get-tuple-element.138.refs_2_), custom_call_target="tpu_custom_call" | custom-call | bytes 2104448 | tf_op jit(solution)/shard_map/cond/branch_1_fun/pallas_call | solution.py:82
  54.9 12.4 %all_to_all.17 = f32[16,8,640]{2,1,0:T(8,128)} all-to-all(f32[16,8,640]{2,1,0:T(8,128)S(1)} %get-tuple-element.139), channel_id=1, replica_groups=mesh['lat'=16,'lon'=16] {'lon'}, dimensions={0} | all-to-all | bytes 655360 | tf_op jit(solution)/shard_map/cond/branch_1_fun/all_to_all | solution.py:629
  67.3 0.8 %slice.23 = f32[16,8,128]{2,1,0:T(8,128)S(1)} slice(f32[16,8,640]{2,1,0:T(8,128)} %all_to_all.17), slice={[0:16], [0:8], [512:640]} | slice | bytes 131072 | tf_op jit(solution)/shard_map/cond/branch_1_fun/slice | solution.py:749
  68.1 1.3 %collective-permute-start.8 = (f32[16,8,128]{2,1,0:T(8,128)S(1)}, f32[16,8,128]{2,1,0:T(8,128)S(1)}, u32[]{:S(2)}, u32[]{:S(2)}) collective-permute-start(f32[16,8,128]{2,1,0:T(8,128)S(1)} %get-tuple-element.186), channel_id=1, source_target_pairs={{0,16},{240,224},{1,17},{241,225},{2,18},{242,226},{3,19},{243,227... | collective-permute-start | bytes 196616 | tf_op jit(solution)/shard_map/ppermute | solution.py:645
  69.4 4.3 %conditional.9 = (f32[3,12,16,360]{3,2,1,0:T(8,128)}) conditional(s32[]{:T(128)} %convert_element_type.2, f32[3,12,16,360]{3,2,1,0:T(8,128)} %get-tuple-element.188, (f32[16,8,640]{2,1,0:T(8,128)}, f32[16,128,384]{2,1,0:T(8,128)}, s32[16]{0:T(128)}, f32[3,12,16,360]{3,2,1,0:T(8,128)S(1)}, f32[3,5,12,16,360]{4,3,2,1,0:T(8,128)}, ...), branch_computations={%region_8.0_spmd, %region_9.0_spmd} | conditional | bytes 9417416 | solution.py:790
  69.4 4.2 %branch_1_fun.11 = f32[3,12,16,360]{3,2,1,0:T(8,128)} custom-call(f32[16,8,640]{2,1,0:T(8,128)} %get-tuple-element.144.waves_in, f32[16,128,384]{2,1,0:T(8,128)} %get-tuple-element.145.table_in, s32[16]{0:T(128)} %get-tuple-element.146.mask_in, f32[3,12,16,360]{3,2,1,0:T(8,128)S(1)} %get-tuple-element.147.middle_in, ...), custom_call_target="tpu_custom_call" | custom-call | bytes 9417408 | tf_op jit(solution)/shard_map/cond/branch_1_fun/pallas_call | solution.py:82
  73.7 0.0 collective-permute-done.8.waves
  (3 shorter events, 0.1 us)
Async XLA Ops:
  2.9 14.9 %copy-start.4 = (s32[16]{0:T(128)S(1)}, s32[16]{0:T(128)}, u32[]{:S(2)}) copy-start(s32[16]{0:T(128)} %get-tuple-element.102.cutoff_in) | copy-start | bytes 196 | tf_op jit(solution)/shard_map/cond
  2.9 14.9 %all-to-all-start = ((f32[16,8,768]{2,1,0:T(8,128)}), f32[16,8,768]{2,1,0:T(8,128)S(1)}, u32[]{:S(2)}, u32[]{:S(2)}) async-start(f32[16,8,768]{2,1,0:T(8,128)} %get-tuple-element.101), calls=%async_computation | async-start | bytes 786432 | tf_op jit(solution)/shard_map/cond/branch_1_fun/all_to_all | solution.py:629
  19.2 14.7 %collective-permute-start.6 = (f32[3,36,360]{2,1,0:T(8,128)S(1)}, f32[3,36,360]{2,1,0:T(8,128)S(1)}, u32[]{:S(2)}, u32[]{:S(2)}) collective-permute-start(f32[3,36,360]{2,1,0:T(8,128)S(1)} %get-tuple-element.182), channel_id=1, source_target_pairs={{16,0},{224,240},{17,1},{225,241},{18,2},{226,242},{19,3},{227,243... | collective-permute-start | bytes 466568 | tf_op jit(solution)/shard_map/ppermute | solution.py:645
  20.6 13.4 %all-to-all-start.1 = ((f32[16,8,768]{2,1,0:T(8,128)}), f32[16,8,768]{2,1,0:T(8,128)}, u32[]{:S(2)}, u32[]{:S(2)}) async-start(f32[16,8,768]{2,1,0:T(8,128)} %get-tuple-element.111), calls=%async_computation.1 | async-start | bytes 786432 | tf_op jit(solution)/shard_map/cond/branch_1_fun/all_to_all | solution.py:629
  33.9 7.6 %copy-start.3 = (s32[16]{0:T(128)S(1)}, s32[16]{0:T(128)}, u32[]{:S(2)}) copy-start(s32[16]{0:T(128)} %param.20) | copy-start | bytes 196
  39.2 2.3 %collective-permute-start.7 = (f32[2,36,360]{2,1,0:T(8,128)S(1)}, f32[2,36,360]{2,1,0:T(8,128)S(1)}, u32[]{:S(2)}, u32[]{:S(2)}) collective-permute-start(f32[2,36,360]{2,1,0:T(8,128)S(1)} %get-tuple-element.183), channel_id=1, source_target_pairs={{0,16},{240,224},{1,17},{241,225},{2,18},{242,226},{3,19},{243,227... | collective-permute-start | bytes 311048 | tf_op jit(solution)/shard_map/ppermute | solution.py:645
  68.1 5.6 %collective-permute-start.8 = (f32[16,8,128]{2,1,0:T(8,128)S(1)}, f32[16,8,128]{2,1,0:T(8,128)S(1)}, u32[]{:S(2)}, u32[]{:S(2)}) collective-permute-start(f32[16,8,128]{2,1,0:T(8,128)S(1)} %get-tuple-element.186), channel_id=1, source_target_pairs={{0,16},{240,224},{1,17},{241,225},{2,18},{242,226},{3,19},{243,227... | collective-permute-start | bytes 196616 | tf_op jit(solution)/shard_map/ppermute | solution.py:645

commit v5 on v4

--- a/solution.py
+++ b/solution.py
@@ -32,12 +32,11 @@
 MORE = ROWS + 64
 CHUNKS = (LON_DEV, SHARE, MORE)
 FIRST_CHUNKS = (LON_DEV, SHARE, MORE + 128)
-LAST_TILE = (LON_DEV, SHARE, 128)
 LINE = (SLABS, WIDTH)
 ACROSS = (40, WIDE)
 LINES = (3, SLABS, WIDTH)
 TILES = (2, HALF, 128)
-EDGES = (2, BAND, 128)
+EDGES = (3, BAND, 128)
 
 
 def wave_tables():
@@ -364,6 +363,7 @@
         edges[side] = whole_band(closed, opened[side], top)
     weight = row_weight(mask, 0, (BAND, WIDTH))
     narrow = row_weight(mask, 0, (BAND, 128))
+    edges[2] = narrow
     for side, lane in enumerate((WIDTH + 1 - LAST, WIDTH - LAST)):
         halos[side] = halo_of(edges[side], filtered[:, LAST:], lane, narrow)
     next_weight = jnp.where(top, weight[0:1], weight[BAND - 1 :])
@@ -411,9 +411,9 @@
 
 
 def final_kernel(
-    waves_in, table_in, mask_in, middle_in, coeff_in, edges_in, opened_in, line_in, across_in,
+    waves_in, table_in, middle_in, coeff_in, edges_in, opened_in, line_in, across_in,
     out,
-    waves, table, mask, middle, coeff_ref, edges, opened, next_line, across, result,
+    waves, table, middle, coeff_ref, edges, opened, next_line, across, result,
     filtered, opposite, halos, sems,
 ):
     lon, lat = place()
@@ -422,24 +422,23 @@
         sems,
         (waves_in, waves),
         (table_in.at[lon], table),
-        (mask_in, mask),
         (edges_in, edges),
         (opened_in, opened),
         (line_in, next_line),
         (across_in, across),
         *by_field((middle_in, middle), (coeff_in, coeff_ref)),
     )
-    rest, fields = rest[:5], rest[5:]
+    rest, fields = rest[:4], rest[4:]
     finish(waves_copy, table_copy)
     flat = waves[:, :, :ROWS].reshape(WAVES, ROWS)
     filtered[...] = dot(flat, table[...], 0, 0)
     polar_row = jnp.where(top, BAND - 1, 0)
     opposite[...] = across_pole(flat, table[...], polar_row)
     finish(*rest)
-    weight = row_weight(mask, 0, (BAND, WIDTH))
+    narrow = edges[2]
+    weight = jnp.concatenate([narrow] * (WIDE // 128), axis=1)[:, :WIDTH]
     row = iota((BAND, WIDTH), 0)
     none = jnp.zeros((HALF, 128), jnp.float32)
-    narrow = row_weight(mask, 0, (BAND, 128))
     for side, lane in enumerate((WIDTH + 1 - LAST, WIDTH - LAST)):
         tile = jnp.where(narrow > 0.5, edges[side], whole_band(none, opened[side], top))
         halos[side] = halo_of(tile, filtered[:, LAST:], lane, narrow)
@@ -613,7 +612,7 @@
 
     @pl.when(bottom | (lat == TOP - 1))
     def _():
-        flat = waves[...].reshape(WAVES, 128)
+        flat = waves[:, :, MORE - 128 :].reshape(WAVES, 128)
         smooth = dot(flat, table[...], 0, 0)[64 : 64 + SLABS, :WIDTH]
         masked = flat[0:1, 64 + SLABS : 65 + SLABS] > 0.5
         line = polar[1] * jnp.where(masked, smooth, 1.0)
@@ -736,17 +735,22 @@
 
     def polar_fourth():
         received = exchanged(send)
-        again, opened, result, part, own_table = launch(
-            second_respond_kernel_with_blank,
+        again, opened = launch(
+            second_respond_kernel,
             [received, wave_cutoff, polar_mask],
             [CHUNKS, TILES],
-            [FIELD, HALF_FIELD, (WAVES, WIDE)],
+            (),
             [small, small],
             copies=2,
             near=1,
         )
-        waves = exchanged(again)
-        return waves, lax.slice_in_dim(waves, MORE - 128, MORE, axis=2), opened, result, part, own_table
+        return exchanged(again), opened
+
+    waves, opened = lax.cond(polar, polar_fourth, lambda: blanks(CHUNKS, TILES))
+    reached, waves = lax.optimization_barrier((reached, waves))
+
+    def polar_wait():
+        return tuple(launch(lambda *_: None, [], (), [FIELD, HALF_FIELD, (WAVES, WIDE)], copies=1))
 
     def plain_fourth():
         west, east = edge[0], edge[1]
@@ -769,20 +773,20 @@
             [in_vmem(FIELD), in_vmem(COEFF), in_vmem(one_edge), in_vmem(one_edge), in_vmem((2, *LINE))],
             copies=6,
         )
-        return *blanks(CHUNKS, LAST_TILE, TILES), result, part, own_table
-
-    waves, near_waves, opened, result, part, own_table = lax.cond(polar, polar_fourth, plain_fourth)
-    waves_beyond = next_to_pole(near_waves, True)
+        return result, part, own_table
+
+    result, part, own_table = lax.cond(polar, polar_wait, plain_fourth)
+    waves_beyond = next_to_pole(waves, True)
 
     def polar_fifth():
         (out,) = launch(
             final_kernel,
-            [waves, table, polar_mask, middle, coefficients, edges, opened, next_line, across],
+            [waves, table, middle, coefficients, edges, opened, next_line, across],
             (),
             [FIELD],
-            [in_vmem(CHUNKS), table_scratch, small, in_vmem(FIELD), in_vmem(COEFF), in_vmem(EDGES)]
+            [in_vmem(CHUNKS), table_scratch, in_vmem(FIELD), in_vmem(COEFF), in_vmem(EDGES)]
             + [in_vmem(TILES), in_vmem(LINE), in_vmem(ACROSS), in_vmem(FIELD), *wave_scratch],
-            copies=13,
+            copies=12,
             pinned=True,
         )
         return out
@@ -804,10 +808,6 @@
 
 def forward_kernel_with_blanks(*refs):
     forward_kernel(*refs[:5], *refs[9:])
-
-
-def second_respond_kernel_with_blank(*refs):
-    second_respond_kernel(*refs[:5], *refs[8:])
 
 
 def solution(mesh):

time: 74.4 us -> 73.2 us (0.984)
  waiting for transfers between devices: 14.8 us -> 13.9 us
  local copies, waits for them, and re-layouts: 0.88 us -> 0.04 us
    ppermute x3, waiting for transfers between devices: 0.96 us -> 0.01 us  [next_to_pole(): return lax.ppermute(value, ('lat', 'lon'), pairs)]
    slice x1 -> x0, local copies, waits for them, and re-layouts: 0.84 us -> none  [polar_fourth(): lax.slice_in_dim(waves, MORE - 128, MORE, axis=2)]
    pallas_call x7 -> x8, Pallas kernels: 16.1 us -> 16.1 us  [launch(): pl.pallas_call(kernel, in_specs=[pl.BlockSpec(memory_space=pltpu.VMEM)] *...]
  transfers between devices with their start and end apart: 5 -> 5, of which waited for: 3 -> 2; matrix products, arithmetic and copies ran while one was open for 0% -> 0% of each run, Pallas kernels for 8% -> 9%
where the time goes in v5:
time: 73.2 us; the launch traced here: 72 us
  blocking collectives  24.8 us (34%)
  starting transfers between devices  16.9 us (23%)
  Pallas kernels  16.1 us (22%)
  waiting for transfers between devices  13.9 us (19%)
    all_to_all x2, blocking collectives, exchanged(): lax.all_to_all(chunks, 'lon', split_axis=0, concat_axis=0, tiled=True)  24.8 us
    pallas_call x8, Pallas kernels, launch(): pl.pallas_call(kernel, in_specs=[pl.BlockSpec(memory_space=pltpu.VMEM)] *...  16.1 us
    all_to_all x2, waiting for transfers between devices, exchanged(): lax.all_to_all(chunks, 'lon', split_axis=0, concat_axis=0, tiled=True)  13.9 us
    all_to_all x2, starting transfers between devices, exchanged(): lax.all_to_all(chunks, 'lon', split_axis=0, concat_axis=0, tiled=True)  13.1 us
    ppermute x3, starting transfers between devices, next_to_pole(): return lax.ppermute(value, ('lat', 'lon'), pairs)  3.89 us
  transfers between devices with their start and end apart: 5, of which 2 were waited for; matrix products, arithmetic and copies ran while one was open for 0% of the time, Pallas kernels for 9%

profile of v5, /device:TPU:8, one launch (start us, length us, event | category | flops | bytes accessed | tf_op | source)
XLA Modules:
  0.0 72.0 jit_solution(13861204483513426595)
XLA Ops:
  0.0 19.2 %conditional.6 = (f32[16,8,768]{2,1,0:T(8,128)}, f32[2,8,128]{2,1,0:T(8,128)S(1)}, f32[3,36,360]{2,1,0:T(8,128)S(1)}, f32[3,36,360]{2,1,0:T(8,128)S(1)}, f32[3,3...) conditional(s32[]{:T(128)} %convert_element_type.2, (f32[3,12,16,360]{3,2,1,0:T(8,128)}, ...), branch_computations={%region_0.0_spmd, %region_1.0_spmd} | conditional | flops 4096 | bytes 31721280 | solution.py:706
  0.0 2.9 %branch_1_fun.7 = (f32[16,8,768]{2,1,0:T(8,128)}, f32[3,36,360]{2,1,0:T(8,128)S(1)}, f32[3,36,360]{2,1,0:T(8,128)S(1)}, f32[3,36,360]{2,1,0:T(8,128)S(1)}, f32[2,16,128]{2,1,0:T(8,128)S(1)}) custom-call(f32[3,12,16,360]{3,2,1,0:T(8,128)} %get-tuple-element.102.refs_0_, f32[3,5,12,16,360]{4,3,2,1,0:T(8,128)} %get-tuple-element.103.refs_1_.coeff_in, ...), custom_call_target="tpu_custom_call" | custom-call | bytes 8998592 | tf_op jit(solution)/shard_map/cond/branch_1_fun/pallas_call | solution.py:81
  2.9 0.0 copy-start.4
  2.9 7.4 %all-to-all-start = ((f32[16,8,768]{2,1,0:T(8,128)}), f32[16,8,768]{2,1,0:T(8,128)S(1)}, u32[]{:S(2)}, u32[]{:S(2)}) async-start(f32[16,8,768]{2,1,0:T(8,128)} %get-tuple-element.106), calls=%async_computation | async-start | bytes 786432 | tf_op jit(solution)/shard_map/cond/branch_1_fun/all_to_all | solution.py:628
  10.3 1.3 %branch_1_fun.8.tiles = f32[2,8,128]{2,1,0:T(8,128)S(1)} custom-call(f32[3,5,12,16,360]{4,3,2,1,0:T(8,128)} %get-tuple-element.103.refs_1_.coeff_in), custom_call_target="tpu_custom_call" | custom-call | bytes 4155392 | tf_op jit(solution)/shard_map/cond/branch_1_fun/pallas_call | solution.py:81
  11.6 6.2 %all-to-all-done.received = f32[16,8,768]{2,1,0:T(8,128)S(1)} async-done(((f32[16,8,768]{2,1,0:T(8,128)}), f32[16,8,768]{2,1,0:T(8,128)S(1)}, u32[]{:S(2)}, u32[]{:S(2)}) %all-to-all-start) | async-done | bytes 393248 | tf_op jit(solution)/shard_map/cond/branch_1_fun/all_to_all | solution.py:628
  17.8 0.0 copy-done.4
  17.8 1.4 %branch_1_fun.9 = (f32[16,8,768]{2,1,0:T(8,128)}, f32[2,8,128]{2,1,0:T(8,128)S(1)}) custom-call(f32[16,8,768]{2,1,0:T(8,128)S(1)} %all-to-all-done.received, f32[2,8,128]{2,1,0:T(8,128)S(1)} %branch_1_fun.8.tiles, s32[16]{0:T(128)S(1)} %copy-done.4), custom_call_target="tpu_custom_call" | custom-call | bytes 802880 | tf_op jit(solution)/shard_map/cond/branch_1_fun/pallas_call | solution.py:81
  19.2 1.3 %collective-permute-start.6 = (f32[3,36,360]{2,1,0:T(8,128)S(1)}, f32[3,36,360]{2,1,0:T(8,128)S(1)}, u32[]{:S(2)}, u32[]{:S(2)}) collective-permute-start(f32[3,36,360]{2,1,0:T(8,128)S(1)} %get-tuple-element.187), channel_id=1, source_target_pairs={{16,0},{224,240},{17,1},{225,241},{18,2},{226,242},{19,3},{227,243... | collective-permute-start | bytes 466568 | tf_op jit(solution)/shard_map/ppermute | solution.py:644
  20.5 13.4 %conditional.7 = (f32[16,8,768]{2,1,0:T(8,128)}, f32[3,36,360]{2,1,0:T(8,128)S(1)}, f32[3,36,360]{2,1,0:T(8,128)S(1)}) conditional(s32[]{:T(128)} %convert_element_type.2, (f32[3,36,360]{2,1,0:T(8,128)S(1)}, f32[3,36,360]{2,1,0:T(8,128)S(1)}) %tuple.57, (f32[16,8,768]{2,1,0:T(8,128)}, f32[3,36,360]{2,1,0:T(8,128)S(1)}, ...), branch_computations={%region_2.0_spmd, %region_3.0_spmd} | conditional | bytes 1801784 | solution.py:717
  20.6 5.7 %all-to-all-start.1 = ((f32[16,8,768]{2,1,0:T(8,128)}), f32[16,8,768]{2,1,0:T(8,128)}, u32[]{:S(2)}, u32[]{:S(2)}) async-start(f32[16,8,768]{2,1,0:T(8,128)} %get-tuple-element.116), calls=%async_computation.1 | async-start | bytes 786432 | tf_op jit(solution)/shard_map/cond/branch_1_fun/all_to_all | solution.py:628
  26.3 7.7 %all-to-all-done.1 = f32[16,8,768]{2,1,0:T(8,128)} async-done(((f32[16,8,768]{2,1,0:T(8,128)}), f32[16,8,768]{2,1,0:T(8,128)}, u32[]{:S(2)}, u32[]{:S(2)}) %all-to-all-start.1) | async-done | bytes 393248 | tf_op jit(solution)/shard_map/cond/branch_1_fun/all_to_all | solution.py:628
  33.9 0.0 collective-permute-done.6
  33.9 0.0 copy-start.3
  33.9 5.3 %conditional.8 = ((f32[16,8,640]{2,1,0:T(8,128)S(1)}, f32[2,36,360]{2,1,0:T(8,128)S(1)}, f32[36,360]{1,0:T(8,128)S(1)}, f32[3,16,128]{2,1,0:T(8,128)S(1)}, f32[4...) conditional(s32[]{:T(128)} %convert_element_type.2, () %tuple.59, (f32[16,8,768]{2,1,0:T(8,128)}, ...), branch_computations={%region_4.0_spmd, %region_5.0_spmd} | conditional | bytes 10907464 | solution.py:733
  33.9 5.3 %branch_1_fun.10 = (f32[16,8,640]{2,1,0:T(8,128)S(1)}, f32[2,36,360]{2,1,0:T(8,128)S(1)}, f32[36,360]{1,0:T(8,128)S(1)}, f32[3,16,128]{2,1,0:T(8,128)S(1)}, f32[...) custom-call(f32[16,8,768]{2,1,0:T(8,128)} %get-tuple-element.119.waves_in, ...), custom_call_target="tpu_custom_call" | custom-call | bytes 10907456 | tf_op jit(solution)/shard_map/cond/branch_1_fun/pallas_call | solution.py:81
  39.2 1.3 %collective-permute-start.7 = (f32[2,36,360]{2,1,0:T(8,128)S(1)}, f32[2,36,360]{2,1,0:T(8,128)S(1)}, u32[]{:S(2)}, u32[]{:S(2)}) collective-permute-start(f32[2,36,360]{2,1,0:T(8,128)S(1)} %get-tuple-element.188), channel_id=1, source_target_pairs={{0,16},{240,224},{1,17},{241,225},{2,18},{242,226},{3,19},{243,227... | collective-permute-start | bytes 311048 | tf_op jit(solution)/shard_map/ppermute | solution.py:644
  40.5 0.0 copy-done.3
  40.5 25.8 %conditional.9 = (f32[16,8,640]{2,1,0:T(8,128)}, f32[2,8,128]{2,1,0:T(8,128)S(1)}) conditional(s32[]{:T(128)} %convert_element_type.2, () %tuple.61, (f32[16,8,640]{2,1,0:T(8,128)S(1)}, s32[16]{0:T(128)S(1)}, s32[16]{0:T(128)}) %tuple.84), branch_computations={%region_6.0_spmd, %region_7.0_spmd} | conditional | bytes 1974416 | solution.py:749
  40.6 12.4 %all_to_all.16.received = f32[16,8,640]{2,1,0:T(8,128)S(1)} all-to-all(f32[16,8,640]{2,1,0:T(8,128)S(1)} %get-tuple-element.127), channel_id=1, replica_groups=mesh['lat'=16,'lon'=16] {'lon'}, dimensions={0} | all-to-all | bytes 655360 | tf_op jit(solution)/shard_map/cond/branch_1_fun/all_to_all | solution.py:628
  53.0 1.0 %branch_1_fun.11 = (f32[16,8,640]{2,1,0:T(8,128)S(1)}, f32[2,8,128]{2,1,0:T(8,128)S(1)}) custom-call(f32[16,8,640]{2,1,0:T(8,128)S(1)} %all_to_all.16.received, s32[16]{0:T(128)S(1)} %get-tuple-element.128.cutoff_in, s32[16]{0:T(128)} %get-tuple-element.129.mask_in), custom_call_target="tpu_custom_call" | custom-call | bytes 663680 | tf_op jit(solution)/shard_map/cond/branch_1_fun/pallas_call | solution.py:81
  54.0 12.4 %all_to_all.17 = f32[16,8,640]{2,1,0:T(8,128)} all-to-all(f32[16,8,640]{2,1,0:T(8,128)S(1)} %get-tuple-element.130), channel_id=1, replica_groups=mesh['lat'=16,'lon'=16] {'lon'}, dimensions={0} | all-to-all | bytes 655360 | tf_op jit(solution)/shard_map/cond/branch_1_fun/all_to_all | solution.py:628
  66.4 0.0 collective-permute-done.7.polar
  66.4 1.3 %collective-permute-start.8 = (f32[16,8,640]{2,1,0:T(8,128)}, f32[16,8,640]{2,1,0:T(8,128)S(1)}, u32[]{:S(2)}, u32[]{:S(2)}) collective-permute-start(f32[16,8,640]{2,1,0:T(8,128)} %get-tuple-element.193), channel_id=1, source_target_pairs={{0,16},{240,224},{1,17},{241,225},{2,18},{242,226},{3,19},{243,227... | collective-permute-start | bytes 983048 | tf_op jit(solution)/shard_map/ppermute | solution.py:644
  67.7 4.2 %conditional.11 = (f32[3,12,16,360]{3,2,1,0:T(8,128)}) conditional(s32[]{:T(128)} %convert_element_type.2, f32[3,12,16,360]{3,2,1,0:T(8,128)} %get-tuple-element.195, (f32[16,8,640]{2,1,0:T(8,128)}, f32[16,128,384]{2,1,0:T(8,128)}, f32[3,12,16,360]{3,2,1,0:T(8,128)S(1)}, f32[3,5,12,16,360]{4,3,2,1,0:T(8,128)}, f32[3,16,128]{2,1,0:T(8,128)S(1)}, ...), branch_computations={%region_10.0_spmd, %region_11.0_spmd} | conditional | bytes 9425544 | solution.py:794
  67.7 4.2 %branch_1_fun.13 = f32[3,12,16,360]{3,2,1,0:T(8,128)} custom-call(f32[16,8,640]{2,1,0:T(8,128)} %get-tuple-element.149.waves_in, f32[16,128,384]{2,1,0:T(8,128)} %get-tuple-element.150.table_in, f32[3,12,16,360]{3,2,1,0:T(8,128)S(1)} %get-tuple-element.151.middle_in, f32[3,5,12,16,360]{4,3,2,1,0:T(8,128)} %get-tuple-element.152.coeff_in, ...), custom_call_target="tpu_custom_call" | custom-call | bytes 9425536 | tf_op jit(solution)/shard_map/cond/branch_1_fun/pallas_call | solution.py:81
  72.0 0.0 collective-permute-done.8.waves
  (5 shorter events, 0.1 us)
Async XLA Ops:
  2.9 14.9 %copy-start.4 = (s32[16]{0:T(128)S(1)}, s32[16]{0:T(128)}, u32[]{:S(2)}) copy-start(s32[16]{0:T(128)} %get-tuple-element.107.cutoff_in) | copy-start | bytes 196 | tf_op jit(solution)/shard_map/cond
  2.9 14.9 %all-to-all-start = ((f32[16,8,768]{2,1,0:T(8,128)}), f32[16,8,768]{2,1,0:T(8,128)S(1)}, u32[]{:S(2)}, u32[]{:S(2)}) async-start(f32[16,8,768]{2,1,0:T(8,128)} %get-tuple-element.106), calls=%async_computation | async-start | bytes 786432 | tf_op jit(solution)/shard_map/cond/branch_1_fun/all_to_all | solution.py:628
  19.2 14.7 %collective-permute-start.6 = (f32[3,36,360]{2,1,0:T(8,128)S(1)}, f32[3,36,360]{2,1,0:T(8,128)S(1)}, u32[]{:S(2)}, u32[]{:S(2)}) collective-permute-start(f32[3,36,360]{2,1,0:T(8,128)S(1)} %get-tuple-element.187), channel_id=1, source_target_pairs={{16,0},{224,240},{17,1},{225,241},{18,2},{226,242},{19,3},{227,243... | collective-permute-start | bytes 466568 | tf_op jit(solution)/shard_map/ppermute | solution.py:644
  20.6 13.4 %all-to-all-start.1 = ((f32[16,8,768]{2,1,0:T(8,128)}), f32[16,8,768]{2,1,0:T(8,128)}, u32[]{:S(2)}, u32[]{:S(2)}) async-start(f32[16,8,768]{2,1,0:T(8,128)} %get-tuple-element.116), calls=%async_computation.1 | async-start | bytes 786432 | tf_op jit(solution)/shard_map/cond/branch_1_fun/all_to_all | solution.py:628
  33.9 6.6 %copy-start.3 = (s32[16]{0:T(128)S(1)}, s32[16]{0:T(128)}, u32[]{:S(2)}) copy-start(s32[16]{0:T(128)} %param.22) | copy-start | bytes 196
  39.2 27.2 %collective-permute-start.7 = (f32[2,36,360]{2,1,0:T(8,128)S(1)}, f32[2,36,360]{2,1,0:T(8,128)S(1)}, u32[]{:S(2)}, u32[]{:S(2)}) collective-permute-start(f32[2,36,360]{2,1,0:T(8,128)S(1)} %get-tuple-element.188), channel_id=1, source_target_pairs={{0,16},{240,224},{1,17},{241,225},{2,18},{242,226},{3,19},{243,227... | collective-permute-start | bytes 311048 | tf_op jit(solution)/shard_map/ppermute | solution.py:644
  66.4 5.6 %collective-permute-start.8 = (f32[16,8,640]{2,1,0:T(8,128)}, f32[16,8,640]{2,1,0:T(8,128)S(1)}, u32[]{:S(2)}, u32[]{:S(2)}) collective-permute-start(f32[16,8,640]{2,1,0:T(8,128)} %get-tuple-element.193), channel_id=1, source_target_pairs={{0,16},{240,224},{1,17},{241,225},{2,18},{242,226},{3,19},{243,227... | collective-permute-start | bytes 983048 | tf_op jit(solution)/shard_map/ppermute | solution.py:644

commit v6 on v5

--- a/solution.py
+++ b/solution.py
@@ -24,7 +24,7 @@
 SLABS = FIELDS * LEV
 ROWS = SLABS * BAND
 SHARE = WAVES // LON_DEV
-UNROLL = 6
+UNROLL = 12
 
 FIELD = (FIELDS, LEV, BAND, WIDTH)
 HALF_FIELD = (FIELDS, LEV, HALF, WIDTH)

time: 73.2 us -> 73 us (level)
  no operation moved by 1% of the time
where the time goes in v6:
time: 73 us; the launch traced here: 71.5 us
  blocking collectives  24.8 us (34%)
  starting transfers between devices  16.9 us (23%)
  Pallas kernels  15.6 us (21%)
  waiting for transfers between devices  13.9 us (19%)
    all_to_all x2, blocking collectives, exchanged(): lax.all_to_all(chunks, 'lon', split_axis=0, concat_axis=0, tiled=True)  24.8 us
    pallas_call x8, Pallas kernels, launch(): pl.pallas_call(kernel, in_specs=[pl.BlockSpec(memory_space=pltpu.VMEM)] *...  15.6 us
    all_to_all x2, waiting for transfers between devices, exchanged(): lax.all_to_all(chunks, 'lon', split_axis=0, concat_axis=0, tiled=True)  13.9 us
    all_to_all x2, starting transfers between devices, exchanged(): lax.all_to_all(chunks, 'lon', split_axis=0, concat_axis=0, tiled=True)  13.1 us
    ppermute x3, starting transfers between devices, next_to_pole(): return lax.ppermute(value, ('lat', 'lon'), pairs)  3.89 us
  transfers between devices with their start and end apart: 5, of which 2 were waited for; matrix products, arithmetic and copies ran while one was open for 0% of the time, Pallas kernels for 9%

profile of v6, /device:TPU:8, one launch (start us, length us, event | category | flops | bytes accessed | tf_op | source)
XLA Modules:
  0.0 71.5 jit_solution(7698196004823466537)
XLA Ops:
  0.0 19.2 %conditional.6 = (f32[16,8,768]{2,1,0:T(8,128)}, f32[2,8,128]{2,1,0:T(8,128)S(1)}, f32[3,36,360]{2,1,0:T(8,128)S(1)}, f32[3,36,360]{2,1,0:T(8,128)S(1)}, f32[3,3...) conditional(s32[]{:T(128)} %convert_element_type.2, (f32[3,12,16,360]{3,2,1,0:T(8,128)}, ...), branch_computations={%region_0.0_spmd, %region_1.0_spmd} | conditional | flops 4096 | bytes 31721280 | solution.py:706
  0.0 2.9 %branch_1_fun.7 = (f32[16,8,768]{2,1,0:T(8,128)}, f32[3,36,360]{2,1,0:T(8,128)S(1)}, f32[3,36,360]{2,1,0:T(8,128)S(1)}, f32[3,36,360]{2,1,0:T(8,128)S(1)}, f32[2,16,128]{2,1,0:T(8,128)S(1)}) custom-call(f32[3,12,16,360]{3,2,1,0:T(8,128)} %get-tuple-element.102.refs_0_, f32[3,5,12,16,360]{4,3,2,1,0:T(8,128)} %get-tuple-element.103.refs_1_.coeff_in, ...), custom_call_target="tpu_custom_call" | custom-call | bytes 8998592 | tf_op jit(solution)/shard_map/cond/branch_1_fun/pallas_call | solution.py:81
  2.9 0.0 copy-start.4
  2.9 7.4 %all-to-all-start = ((f32[16,8,768]{2,1,0:T(8,128)}), f32[16,8,768]{2,1,0:T(8,128)S(1)}, u32[]{:S(2)}, u32[]{:S(2)}) async-start(f32[16,8,768]{2,1,0:T(8,128)} %get-tuple-element.106), calls=%async_computation | async-start | bytes 786432 | tf_op jit(solution)/shard_map/cond/branch_1_fun/all_to_all | solution.py:628
  10.3 1.3 %branch_1_fun.8.tiles = f32[2,8,128]{2,1,0:T(8,128)S(1)} custom-call(f32[3,5,12,16,360]{4,3,2,1,0:T(8,128)} %get-tuple-element.103.refs_1_.coeff_in), custom_call_target="tpu_custom_call" | custom-call | bytes 4155392 | tf_op jit(solution)/shard_map/cond/branch_1_fun/pallas_call | solution.py:81
  11.6 6.2 %all-to-all-done.received = f32[16,8,768]{2,1,0:T(8,128)S(1)} async-done(((f32[16,8,768]{2,1,0:T(8,128)}), f32[16,8,768]{2,1,0:T(8,128)S(1)}, u32[]{:S(2)}, u32[]{:S(2)}) %all-to-all-start) | async-done | bytes 393248 | tf_op jit(solution)/shard_map/cond/branch_1_fun/all_to_all | solution.py:628
  17.8 0.0 copy-done.4
  17.8 1.4 %branch_1_fun.9 = (f32[16,8,768]{2,1,0:T(8,128)}, f32[2,8,128]{2,1,0:T(8,128)S(1)}) custom-call(f32[16,8,768]{2,1,0:T(8,128)S(1)} %all-to-all-done.received, f32[2,8,128]{2,1,0:T(8,128)S(1)} %branch_1_fun.8.tiles, s32[16]{0:T(128)S(1)} %copy-done.4), custom_call_target="tpu_custom_call" | custom-call | bytes 802880 | tf_op jit(solution)/shard_map/cond/branch_1_fun/pallas_call | solution.py:81
  19.2 1.3 %collective-permute-start.6 = (f32[3,36,360]{2,1,0:T(8,128)S(1)}, f32[3,36,360]{2,1,0:T(8,128)S(1)}, u32[]{:S(2)}, u32[]{:S(2)}) collective-permute-start(f32[3,36,360]{2,1,0:T(8,128)S(1)} %get-tuple-element.187), channel_id=1, source_target_pairs={{16,0},{224,240},{17,1},{225,241},{18,2},{226,242},{19,3},{227,243... | collective-permute-start | bytes 466568 | tf_op jit(solution)/shard_map/ppermute | solution.py:644
  20.5 13.4 %conditional.7 = (f32[16,8,768]{2,1,0:T(8,128)}, f32[3,36,360]{2,1,0:T(8,128)S(1)}, f32[3,36,360]{2,1,0:T(8,128)S(1)}) conditional(s32[]{:T(128)} %convert_element_type.2, (f32[3,36,360]{2,1,0:T(8,128)S(1)}, f32[3,36,360]{2,1,0:T(8,128)S(1)}) %tuple.57, (f32[16,8,768]{2,1,0:T(8,128)}, f32[3,36,360]{2,1,0:T(8,128)S(1)}, ...), branch_computations={%region_2.0_spmd, %region_3.0_spmd} | conditional | bytes 1801784 | solution.py:717
  20.6 5.7 %all-to-all-start.1 = ((f32[16,8,768]{2,1,0:T(8,128)}), f32[16,8,768]{2,1,0:T(8,128)}, u32[]{:S(2)}, u32[]{:S(2)}) async-start(f32[16,8,768]{2,1,0:T(8,128)} %get-tuple-element.116), calls=%async_computation.1 | async-start | bytes 786432 | tf_op jit(solution)/shard_map/cond/branch_1_fun/all_to_all | solution.py:628
  26.3 7.7 %all-to-all-done.1 = f32[16,8,768]{2,1,0:T(8,128)} async-done(((f32[16,8,768]{2,1,0:T(8,128)}), f32[16,8,768]{2,1,0:T(8,128)}, u32[]{:S(2)}, u32[]{:S(2)}) %all-to-all-start.1) | async-done | bytes 393248 | tf_op jit(solution)/shard_map/cond/branch_1_fun/all_to_all | solution.py:628
  33.9 0.0 collective-permute-done.6
  33.9 0.0 copy-start.3
  33.9 5.1 %conditional.8 = ((f32[16,8,640]{2,1,0:T(8,128)S(1)}, f32[2,36,360]{2,1,0:T(8,128)S(1)}, f32[36,360]{1,0:T(8,128)S(1)}, f32[3,16,128]{2,1,0:T(8,128)S(1)}, f32[4...) conditional(s32[]{:T(128)} %convert_element_type.2, () %tuple.59, (f32[16,8,768]{2,1,0:T(8,128)}, ...), branch_computations={%region_4.0_spmd, %region_5.0_spmd} | conditional | bytes 10907464 | solution.py:733
  33.9 5.1 %branch_1_fun.10 = (f32[16,8,640]{2,1,0:T(8,128)S(1)}, f32[2,36,360]{2,1,0:T(8,128)S(1)}, f32[36,360]{1,0:T(8,128)S(1)}, f32[3,16,128]{2,1,0:T(8,128)S(1)}, f32[...) custom-call(f32[16,8,768]{2,1,0:T(8,128)} %get-tuple-element.119.waves_in, ...), custom_call_target="tpu_custom_call" | custom-call | bytes 10907456 | tf_op jit(solution)/shard_map/cond/branch_1_fun/pallas_call | solution.py:81
  39.0 1.3 %collective-permute-start.7 = (f32[2,36,360]{2,1,0:T(8,128)S(1)}, f32[2,36,360]{2,1,0:T(8,128)S(1)}, u32[]{:S(2)}, u32[]{:S(2)}) collective-permute-start(f32[2,36,360]{2,1,0:T(8,128)S(1)} %get-tuple-element.188), channel_id=1, source_target_pairs={{0,16},{240,224},{1,17},{241,225},{2,18},{242,226},{3,19},{243,227... | collective-permute-start | bytes 311048 | tf_op jit(solution)/shard_map/ppermute | solution.py:644
  40.3 0.0 copy-done.3
  40.3 25.8 %conditional.9 = (f32[16,8,640]{2,1,0:T(8,128)}, f32[2,8,128]{2,1,0:T(8,128)S(1)}) conditional(s32[]{:T(128)} %convert_element_type.2, () %tuple.61, (f32[16,8,640]{2,1,0:T(8,128)S(1)}, s32[16]{0:T(128)S(1)}, s32[16]{0:T(128)}) %tuple.84), branch_computations={%region_6.0_spmd, %region_7.0_spmd} | conditional | bytes 1974416 | solution.py:749
  40.3 12.4 %all_to_all.16.received = f32[16,8,640]{2,1,0:T(8,128)S(1)} all-to-all(f32[16,8,640]{2,1,0:T(8,128)S(1)} %get-tuple-element.127), channel_id=1, replica_groups=mesh['lat'=16,'lon'=16] {'lon'}, dimensions={0} | all-to-all | bytes 655360 | tf_op jit(solution)/shard_map/cond/branch_1_fun/all_to_all | solution.py:628
  52.8 1.0 %branch_1_fun.11 = (f32[16,8,640]{2,1,0:T(8,128)S(1)}, f32[2,8,128]{2,1,0:T(8,128)S(1)}) custom-call(f32[16,8,640]{2,1,0:T(8,128)S(1)} %all_to_all.16.received, s32[16]{0:T(128)S(1)} %get-tuple-element.128.cutoff_in, s32[16]{0:T(128)} %get-tuple-element.129.mask_in), custom_call_target="tpu_custom_call" | custom-call | bytes 663680 | tf_op jit(solution)/shard_map/cond/branch_1_fun/pallas_call | solution.py:81
  53.8 12.4 %all_to_all.17 = f32[16,8,640]{2,1,0:T(8,128)} all-to-all(f32[16,8,640]{2,1,0:T(8,128)S(1)} %get-tuple-element.130), channel_id=1, replica_groups=mesh['lat'=16,'lon'=16] {'lon'}, dimensions={0} | all-to-all | bytes 655360 | tf_op jit(solution)/shard_map/cond/branch_1_fun/all_to_all | solution.py:628
  66.2 0.0 collective-permute-done.7.polar
  66.2 1.3 %collective-permute-start.8 = (f32[16,8,640]{2,1,0:T(8,128)}, f32[16,8,640]{2,1,0:T(8,128)S(1)}, u32[]{:S(2)}, u32[]{:S(2)}) collective-permute-start(f32[16,8,640]{2,1,0:T(8,128)} %get-tuple-element.193), channel_id=1, source_target_pairs={{0,16},{240,224},{1,17},{241,225},{2,18},{242,226},{3,19},{243,227... | collective-permute-start | bytes 983048 | tf_op jit(solution)/shard_map/ppermute | solution.py:644
  67.5 4.0 %conditional.11 = (f32[3,12,16,360]{3,2,1,0:T(8,128)}) conditional(s32[]{:T(128)} %convert_element_type.2, f32[3,12,16,360]{3,2,1,0:T(8,128)} %get-tuple-element.195, (f32[16,8,640]{2,1,0:T(8,128)}, f32[16,128,384]{2,1,0:T(8,128)}, f32[3,12,16,360]{3,2,1,0:T(8,128)S(1)}, f32[3,5,12,16,360]{4,3,2,1,0:T(8,128)}, f32[3,16,128]{2,1,0:T(8,128)S(1)}, ...), branch_computations={%region_10.0_spmd, %region_11.0_spmd} | conditional | bytes 9425544 | solution.py:794
  67.5 4.0 %branch_1_fun.13 = f32[3,12,16,360]{3,2,1,0:T(8,128)} custom-call(f32[16,8,640]{2,1,0:T(8,128)} %get-tuple-element.149.waves_in, f32[16,128,384]{2,1,0:T(8,128)} %get-tuple-element.150.table_in, f32[3,12,16,360]{3,2,1,0:T(8,128)S(1)} %get-tuple-element.151.middle_in, f32[3,5,12,16,360]{4,3,2,1,0:T(8,128)} %get-tuple-element.152.coeff_in, ...), custom_call_target="tpu_custom_call" | custom-call | bytes 9425536 | tf_op jit(solution)/shard_map/cond/branch_1_fun/pallas_call | solution.py:81
  71.5 0.0 collective-permute-done.8.waves
  (5 shorter events, 0.1 us)
Async XLA Ops:
  2.9 14.9 %copy-start.4 = (s32[16]{0:T(128)S(1)}, s32[16]{0:T(128)}, u32[]{:S(2)}) copy-start(s32[16]{0:T(128)} %get-tuple-element.107.cutoff_in) | copy-start | bytes 196 | tf_op jit(solution)/shard_map/cond
  2.9 14.9 %all-to-all-start = ((f32[16,8,768]{2,1,0:T(8,128)}), f32[16,8,768]{2,1,0:T(8,128)S(1)}, u32[]{:S(2)}, u32[]{:S(2)}) async-start(f32[16,8,768]{2,1,0:T(8,128)} %get-tuple-element.106), calls=%async_computation | async-start | bytes 786432 | tf_op jit(solution)/shard_map/cond/branch_1_fun/all_to_all | solution.py:628
  19.2 14.7 %collective-permute-start.6 = (f32[3,36,360]{2,1,0:T(8,128)S(1)}, f32[3,36,360]{2,1,0:T(8,128)S(1)}, u32[]{:S(2)}, u32[]{:S(2)}) collective-permute-start(f32[3,36,360]{2,1,0:T(8,128)S(1)} %get-tuple-element.187), channel_id=1, source_target_pairs={{16,0},{224,240},{17,1},{225,241},{18,2},{226,242},{19,3},{227,243... | collective-permute-start | bytes 466568 | tf_op jit(solution)/shard_map/ppermute | solution.py:644
  20.6 13.4 %all-to-all-start.1 = ((f32[16,8,768]{2,1,0:T(8,128)}), f32[16,8,768]{2,1,0:T(8,128)}, u32[]{:S(2)}, u32[]{:S(2)}) async-start(f32[16,8,768]{2,1,0:T(8,128)} %get-tuple-element.116), calls=%async_computation.1 | async-start | bytes 786432 | tf_op jit(solution)/shard_map/cond/branch_1_fun/all_to_all | solution.py:628
  33.9 6.4 %copy-start.3 = (s32[16]{0:T(128)S(1)}, s32[16]{0:T(128)}, u32[]{:S(2)}) copy-start(s32[16]{0:T(128)} %param.22) | copy-start | bytes 196
  39.0 27.2 %collective-permute-start.7 = (f32[2,36,360]{2,1,0:T(8,128)S(1)}, f32[2,36,360]{2,1,0:T(8,128)S(1)}, u32[]{:S(2)}, u32[]{:S(2)}) collective-permute-start(f32[2,36,360]{2,1,0:T(8,128)S(1)} %get-tuple-element.188), channel_id=1, source_target_pairs={{0,16},{240,224},{1,17},{241,225},{2,18},{242,226},{3,19},{243,227... | collective-permute-start | bytes 311048 | tf_op jit(solution)/shard_map/ppermute | solution.py:644
  66.2 5.3 %collective-permute-start.8 = (f32[16,8,640]{2,1,0:T(8,128)}, f32[16,8,640]{2,1,0:T(8,128)S(1)}, u32[]{:S(2)}, u32[]{:S(2)}) collective-permute-start(f32[16,8,640]{2,1,0:T(8,128)} %get-tuple-element.193), channel_id=1, source_target_pairs={{0,16},{240,224},{1,17},{241,225},{2,18},{242,226},{3,19},{243,227... | collective-permute-start | bytes 983048 | tf_op jit(solution)/shard_map/ppermute | solution.py:644

commit v7 on v6

--- a/solution.py
+++ b/solution.py
@@ -338,6 +338,7 @@
 ):
     lon, lat = place()
     top = lat == TOP
+    rows = pl.ds(open_row(lat), HALF)
     waves_copy, table_copy, *rest = begin(
         sems,
         (waves_in, waves),
@@ -345,7 +346,7 @@
         (mask_in, mask),
         (opened_in, opened),
         (beyond_in, beyond),
-        *by_field((state_in, state), (extra_in, extra), (coeff_in, coeff_ref)),
+        *by_field((state_in.at[:, :, rows], state), (extra_in, extra), (coeff_in, coeff_ref)),
     )
     rest, fields = rest[:3], rest[3:]
     finish(waves_copy, table_copy)
@@ -369,10 +370,12 @@
     next_weight = jnp.where(top, weight[0:1], weight[BAND - 1 :])
     row = iota((BAND, WIDTH), 0)
 
+    none = jnp.zeros((HALF, WIDTH), jnp.float32)
+
     def one(field, level, carry):
         slab = field * LEV + level
         here = pl.ds(slab, 1)
-        value = state[field, level]
+        value = whole_band(none, state[field, level], top)
         smooth = filtered[pl.ds(slab * BAND, BAND)]
         value = value + weight * (smooth[:, :WIDTH] - value)
         coeff = load_coeff(coeff_ref, field, level)
@@ -399,7 +402,7 @@
     for field in range(FIELDS):
         finish(*fields[3 * field : 3 * field + 3])
         for_levels(field, one)
-        stored += begin(sems.at[field : field + 1], (middle.at[field], middle_out.at[field]))
+        stored += begin(sems.at[field : field + 1], (middle.at[field, :, rows], middle_out.at[field]))
     sums = dot(table[:, :WIDTH], middle[...].reshape(ROWS, WIDTH), 1, 1)
     send[:, :, :ROWS] = sums.reshape(LON_DEV, SHARE, ROWS)
     east_tile = tile_of(ends[0, :, : WIDTH - LAST], WIDTH - LAST - 1, BAND, open_row(lat))
@@ -443,10 +446,12 @@
         tile = jnp.where(narrow > 0.5, edges[side], whole_band(none, opened[side], top))
         halos[side] = halo_of(tile, filtered[:, LAST:], lane, narrow)
 
+    blank = jnp.zeros((HALF, WIDTH), jnp.float32)
+
     def one(field, level, carry):
         slab = field * LEV + level
         here = pl.ds(slab, 1)
-        value = middle[field, level]
+        value = whole_band(blank, middle[field, level], top)
         smooth = filtered[pl.ds(slab * BAND, BAND)]
         value = value + weight * (smooth[:, :WIDTH] - value)
         coeff = load_coeff(coeff_ref, field, level)
@@ -721,14 +726,14 @@
             middle_kernel,
             [waves, table, polar_mask, adjoint_state, innovation, coefficients, opened, beyond],
             [CHUNKS, (2, *LINE), LINE, EDGES, ACROSS],
-            [FIELD],
-            [in_vmem(FIRST_CHUNKS), table_scratch, small, in_vmem(FIELD), in_vmem(FIELD), in_vmem(COEFF)]
+            [HALF_FIELD],
+            [in_vmem(FIRST_CHUNKS), table_scratch, small, in_vmem(HALF_FIELD), in_vmem(FIELD), in_vmem(COEFF)]
             + [in_vmem(TILES), in_vmem(LINES), in_vmem(FIELD), *wave_scratch, halo_scratch],
             copies=14,
         ))
 
     def plain_third():
-        return blanks(CHUNKS, (2, *LINE), LINE, EDGES, ACROSS, FIELD)
+        return blanks(CHUNKS, (2, *LINE), LINE, EDGES, ACROSS, HALF_FIELD)
 
     send, to_next, next_line, edges, across, middle = lax.cond(polar, polar_third, plain_third)
     reached = next_to_pole(to_next, True)
@@ -784,7 +789,7 @@
             [waves, table, middle, coefficients, edges, opened, next_line, across],
             (),
             [FIELD],
-            [in_vmem(CHUNKS), table_scratch, in_vmem(FIELD), in_vmem(COEFF), in_vmem(EDGES)]
+            [in_vmem(CHUNKS), table_scratch, in_vmem(HALF_FIELD), in_vmem(COEFF), in_vmem(EDGES)]
             + [in_vmem(TILES), in_vmem(LINE), in_vmem(ACROSS), in_vmem(FIELD), *wave_scratch],
             copies=12,
             pinned=True,

time: 73 us -> 72.9 us (level)
  no operation moved by 1% of the time
where the time goes in v7:
time: 72.9 us; the launch traced here: 71.4 us
  blocking collectives  24.8 us (34%)
  starting transfers between devices  16.9 us (23%)
  Pallas kernels  15.5 us (21%)
  waiting for transfers between devices  13.9 us (19%)
    all_to_all x2, blocking collectives, exchanged(): lax.all_to_all(chunks, 'lon', split_axis=0, concat_axis=0, tiled=True)  24.8 us
    pallas_call x8, Pallas kernels, launch(): pl.pallas_call(kernel, in_specs=[pl.BlockSpec(memory_space=pltpu.VMEM)] *...  15.5 us
    all_to_all x2, waiting for transfers between devices, exchanged(): lax.all_to_all(chunks, 'lon', split_axis=0, concat_axis=0, tiled=True)  13.9 us
    all_to_all x2, starting transfers between devices, exchanged(): lax.all_to_all(chunks, 'lon', split_axis=0, concat_axis=0, tiled=True)  13.1 us
    ppermute x3, starting transfers between devices, next_to_pole(): return lax.ppermute(value, ('lat', 'lon'), pairs)  3.89 us
  transfers between devices with their start and end apart: 5, of which 2 were waited for; matrix products, arithmetic and copies ran while one was open for 0% of the time, Pallas kernels for 9%

profile of v7, /device:TPU:8, one launch (start us, length us, event | category | flops | bytes accessed | tf_op | source)
XLA Modules:
  0.0 71.4 jit_solution(4905279886019770811)
XLA Ops:
  0.0 19.2 %conditional.6 = (f32[16,8,768]{2,1,0:T(8,128)}, f32[2,8,128]{2,1,0:T(8,128)S(1)}, f32[3,36,360]{2,1,0:T(8,128)S(1)}, f32[3,36,360]{2,1,0:T(8,128)S(1)}, f32[3,3...) conditional(s32[]{:T(128)} %convert_element_type.2, (f32[3,12,16,360]{3,2,1,0:T(8,128)}, ...), branch_computations={%region_0.0_spmd, %region_1.0_spmd} | conditional | flops 4096 | bytes 31721280 | solution.py:711
  0.0 2.9 %branch_1_fun.7 = (f32[16,8,768]{2,1,0:T(8,128)}, f32[3,36,360]{2,1,0:T(8,128)S(1)}, f32[3,36,360]{2,1,0:T(8,128)S(1)}, f32[3,36,360]{2,1,0:T(8,128)S(1)}, f32[2,16,128]{2,1,0:T(8,128)S(1)}) custom-call(f32[3,12,16,360]{3,2,1,0:T(8,128)} %get-tuple-element.102.refs_0_, f32[3,5,12,16,360]{4,3,2,1,0:T(8,128)} %get-tuple-element.103.refs_1_.coeff_in, ...), custom_call_target="tpu_custom_call" | custom-call | bytes 8998592 | tf_op jit(solution)/shard_map/cond/branch_1_fun/pallas_call | solution.py:81
  2.9 0.0 copy-start.4
  2.9 7.4 %all-to-all-start = ((f32[16,8,768]{2,1,0:T(8,128)}), f32[16,8,768]{2,1,0:T(8,128)S(1)}, u32[]{:S(2)}, u32[]{:S(2)}) async-start(f32[16,8,768]{2,1,0:T(8,128)} %get-tuple-element.106), calls=%async_computation | async-start | bytes 786432 | tf_op jit(solution)/shard_map/cond/branch_1_fun/all_to_all | solution.py:633
  10.3 1.3 %branch_1_fun.8.tiles = f32[2,8,128]{2,1,0:T(8,128)S(1)} custom-call(f32[3,5,12,16,360]{4,3,2,1,0:T(8,128)} %get-tuple-element.103.refs_1_.coeff_in), custom_call_target="tpu_custom_call" | custom-call | bytes 4155392 | tf_op jit(solution)/shard_map/cond/branch_1_fun/pallas_call | solution.py:81
  11.6 6.2 %all-to-all-done.received = f32[16,8,768]{2,1,0:T(8,128)S(1)} async-done(((f32[16,8,768]{2,1,0:T(8,128)}), f32[16,8,768]{2,1,0:T(8,128)S(1)}, u32[]{:S(2)}, u32[]{:S(2)}) %all-to-all-start) | async-done | bytes 393248 | tf_op jit(solution)/shard_map/cond/branch_1_fun/all_to_all | solution.py:633
  17.8 0.0 copy-done.4
  17.8 1.4 %branch_1_fun.9 = (f32[16,8,768]{2,1,0:T(8,128)}, f32[2,8,128]{2,1,0:T(8,128)S(1)}) custom-call(f32[16,8,768]{2,1,0:T(8,128)S(1)} %all-to-all-done.received, f32[2,8,128]{2,1,0:T(8,128)S(1)} %branch_1_fun.8.tiles, s32[16]{0:T(128)S(1)} %copy-done.4), custom_call_target="tpu_custom_call" | custom-call | bytes 802880 | tf_op jit(solution)/shard_map/cond/branch_1_fun/pallas_call | solution.py:81
  19.2 1.3 %collective-permute-start.6 = (f32[3,36,360]{2,1,0:T(8,128)S(1)}, f32[3,36,360]{2,1,0:T(8,128)S(1)}, u32[]{:S(2)}, u32[]{:S(2)}) collective-permute-start(f32[3,36,360]{2,1,0:T(8,128)S(1)} %get-tuple-element.187), channel_id=1, source_target_pairs={{16,0},{224,240},{17,1},{225,241},{18,2},{226,242},{19,3},{227,243... | collective-permute-start | bytes 466568 | tf_op jit(solution)/shard_map/ppermute | solution.py:649
  20.5 13.4 %conditional.7 = (f32[16,8,768]{2,1,0:T(8,128)}, f32[3,36,360]{2,1,0:T(8,128)S(1)}, f32[3,36,360]{2,1,0:T(8,128)S(1)}) conditional(s32[]{:T(128)} %convert_element_type.2, (f32[3,36,360]{2,1,0:T(8,128)S(1)}, f32[3,36,360]{2,1,0:T(8,128)S(1)}) %tuple.57, (f32[16,8,768]{2,1,0:T(8,128)}, f32[3,36,360]{2,1,0:T(8,128)S(1)}, ...), branch_computations={%region_2.0_spmd, %region_3.0_spmd} | conditional | bytes 1801784 | solution.py:722
  20.6 5.7 %all-to-all-start.1 = ((f32[16,8,768]{2,1,0:T(8,128)}), f32[16,8,768]{2,1,0:T(8,128)}, u32[]{:S(2)}, u32[]{:S(2)}) async-start(f32[16,8,768]{2,1,0:T(8,128)} %get-tuple-element.116), calls=%async_computation.1 | async-start | bytes 786432 | tf_op jit(solution)/shard_map/cond/branch_1_fun/all_to_all | solution.py:633
  26.3 7.7 %all-to-all-done.1 = f32[16,8,768]{2,1,0:T(8,128)} async-done(((f32[16,8,768]{2,1,0:T(8,128)}), f32[16,8,768]{2,1,0:T(8,128)}, u32[]{:S(2)}, u32[]{:S(2)}) %all-to-all-start.1) | async-done | bytes 393248 | tf_op jit(solution)/shard_map/cond/branch_1_fun/all_to_all | solution.py:633
  33.9 0.0 collective-permute-done.6
  33.9 0.0 copy-start.3
  33.9 4.9 %conditional.8 = ((f32[16,8,640]{2,1,0:T(8,128)S(1)}, f32[2,36,360]{2,1,0:T(8,128)S(1)}, f32[36,360]{1,0:T(8,128)S(1)}, f32[3,16,128]{2,1,0:T(8,128)S(1)}, f32[4...) conditional(s32[]{:T(128)} %convert_element_type.2, () %tuple.59, (f32[16,8,768]{2,1,0:T(8,128)}, ...), branch_computations={%region_4.0_spmd, %region_5.0_spmd} | conditional | bytes 10492744 | solution.py:738
  33.9 4.9 %branch_1_fun.10 = (f32[16,8,640]{2,1,0:T(8,128)S(1)}, f32[2,36,360]{2,1,0:T(8,128)S(1)}, f32[36,360]{1,0:T(8,128)S(1)}, f32[3,16,128]{2,1,0:T(8,128)S(1)}, f32[...) custom-call(f32[16,8,768]{2,1,0:T(8,128)} %get-tuple-element.119.waves_in, f32[16,128,384]{2,1,0:T(8,128)} %get-tuple-element.120.table_in, ...), custom_call_target="tpu_custom_call" | custom-call | bytes 10492736 | tf_op jit(solution)/shard_map/cond/branch_1_fun/pallas_call | solution.py:81
  38.9 1.3 %collective-permute-start.7 = (f32[2,36,360]{2,1,0:T(8,128)S(1)}, f32[2,36,360]{2,1,0:T(8,128)S(1)}, u32[]{:S(2)}, u32[]{:S(2)}) collective-permute-start(f32[2,36,360]{2,1,0:T(8,128)S(1)} %get-tuple-element.188), channel_id=1, source_target_pairs={{0,16},{240,224},{1,17},{241,225},{2,18},{242,226},{3,19},{243,227... | collective-permute-start | bytes 311048 | tf_op jit(solution)/shard_map/ppermute | solution.py:649
  40.2 0.0 copy-done.3
  40.2 25.8 %conditional.9 = (f32[16,8,640]{2,1,0:T(8,128)}, f32[2,8,128]{2,1,0:T(8,128)S(1)}) conditional(s32[]{:T(128)} %convert_element_type.2, () %tuple.61, (f32[16,8,640]{2,1,0:T(8,128)S(1)}, s32[16]{0:T(128)S(1)}, s32[16]{0:T(128)}) %tuple.84), branch_computations={%region_6.0_spmd, %region_7.0_spmd} | conditional | bytes 1974416 | solution.py:754
  40.2 12.4 %all_to_all.16.received = f32[16,8,640]{2,1,0:T(8,128)S(1)} all-to-all(f32[16,8,640]{2,1,0:T(8,128)S(1)} %get-tuple-element.127), channel_id=1, replica_groups=mesh['lat'=16,'lon'=16] {'lon'}, dimensions={0} | all-to-all | bytes 655360 | tf_op jit(solution)/shard_map/cond/branch_1_fun/all_to_all | solution.py:633
  52.6 1.0 %branch_1_fun.11 = (f32[16,8,640]{2,1,0:T(8,128)S(1)}, f32[2,8,128]{2,1,0:T(8,128)S(1)}) custom-call(f32[16,8,640]{2,1,0:T(8,128)S(1)} %all_to_all.16.received, s32[16]{0:T(128)S(1)} %get-tuple-element.128.cutoff_in, s32[16]{0:T(128)} %get-tuple-element.129.mask_in), custom_call_target="tpu_custom_call" | custom-call | bytes 663680 | tf_op jit(solution)/shard_map/cond/branch_1_fun/pallas_call | solution.py:81
  53.6 12.4 %all_to_all.17 = f32[16,8,640]{2,1,0:T(8,128)} all-to-all(f32[16,8,640]{2,1,0:T(8,128)S(1)} %get-tuple-element.130), channel_id=1, replica_groups=mesh['lat'=16,'lon'=16] {'lon'}, dimensions={0} | all-to-all | bytes 655360 | tf_op jit(solution)/shard_map/cond/branch_1_fun/all_to_all | solution.py:633
  66.0 0.0 collective-permute-done.7.polar
  66.0 1.3 %collective-permute-start.8 = (f32[16,8,640]{2,1,0:T(8,128)}, f32[16,8,640]{2,1,0:T(8,128)S(1)}, u32[]{:S(2)}, u32[]{:S(2)}) collective-permute-start(f32[16,8,640]{2,1,0:T(8,128)} %get-tuple-element.193), channel_id=1, source_target_pairs={{0,16},{240,224},{1,17},{241,225},{2,18},{242,226},{3,19},{243,227... | collective-permute-start | bytes 983048 | tf_op jit(solution)/shard_map/ppermute | solution.py:649
  67.4 4.0 %conditional.11 = (f32[3,12,16,360]{3,2,1,0:T(8,128)}) conditional(s32[]{:T(128)} %convert_element_type.2, f32[3,12,16,360]{3,2,1,0:T(8,128)} %get-tuple-element.195, (f32[16,8,640]{2,1,0:T(8,128)}, f32[16,128,384]{2,1,0:T(8,128)}, f32[3,12,8,360]{3,2,1,0:T(8,128)S(1)}, f32[3,5,12,16,360]{4,3,2,1,0:T(8,128)}, f32[3,16,128]{2,1,0:T(8,128)S(1)}, ...), branch_computations={%region_10.0_spmd, %region_11.0_spmd} | conditional | bytes 9010824 | solution.py:799
  67.4 4.0 %branch_1_fun.13 = f32[3,12,16,360]{3,2,1,0:T(8,128)} custom-call(f32[16,8,640]{2,1,0:T(8,128)} %get-tuple-element.149.waves_in, f32[16,128,384]{2,1,0:T(8,128)} %get-tuple-element.150.table_in, f32[3,12,8,360]{3,2,1,0:T(8,128)S(1)} %get-tuple-element.151.middle_in, f32[3,5,12,16,360]{4,3,2,1,0:T(8,128)} %get-tuple-element.152.coeff_in, ...), custom_call_target="tpu_custom_call" | custom-call | bytes 9010816 | tf_op jit(solution)/shard_map/cond/branch_1_fun/pallas_call | solution.py:81
  71.4 0.0 collective-permute-done.8.waves
  (5 shorter events, 0.1 us)
Async XLA Ops:
  2.9 14.9 %copy-start.4 = (s32[16]{0:T(128)S(1)}, s32[16]{0:T(128)}, u32[]{:S(2)}) copy-start(s32[16]{0:T(128)} %get-tuple-element.107.cutoff_in) | copy-start | bytes 196 | tf_op jit(solution)/shard_map/cond
  2.9 14.9 %all-to-all-start = ((f32[16,8,768]{2,1,0:T(8,128)}), f32[16,8,768]{2,1,0:T(8,128)S(1)}, u32[]{:S(2)}, u32[]{:S(2)}) async-start(f32[16,8,768]{2,1,0:T(8,128)} %get-tuple-element.106), calls=%async_computation | async-start | bytes 786432 | tf_op jit(solution)/shard_map/cond/branch_1_fun/all_to_all | solution.py:633
  19.2 14.7 %collective-permute-start.6 = (f32[3,36,360]{2,1,0:T(8,128)S(1)}, f32[3,36,360]{2,1,0:T(8,128)S(1)}, u32[]{:S(2)}, u32[]{:S(2)}) collective-permute-start(f32[3,36,360]{2,1,0:T(8,128)S(1)} %get-tuple-element.187), channel_id=1, source_target_pairs={{16,0},{224,240},{17,1},{225,241},{18,2},{226,242},{19,3},{227,243... | collective-permute-start | bytes 466568 | tf_op jit(solution)/shard_map/ppermute | solution.py:649
  20.6 13.4 %all-to-all-start.1 = ((f32[16,8,768]{2,1,0:T(8,128)}), f32[16,8,768]{2,1,0:T(8,128)}, u32[]{:S(2)}, u32[]{:S(2)}) async-start(f32[16,8,768]{2,1,0:T(8,128)} %get-tuple-element.116), calls=%async_computation.1 | async-start | bytes 786432 | tf_op jit(solution)/shard_map/cond/branch_1_fun/all_to_all | solution.py:633
  33.9 6.3 %copy-start.3 = (s32[16]{0:T(128)S(1)}, s32[16]{0:T(128)}, u32[]{:S(2)}) copy-start(s32[16]{0:T(128)} %param.22) | copy-start | bytes 196
  38.9 27.2 %collective-permute-start.7 = (f32[2,36,360]{2,1,0:T(8,128)S(1)}, f32[2,36,360]{2,1,0:T(8,128)S(1)}, u32[]{:S(2)}, u32[]{:S(2)}) collective-permute-start(f32[2,36,360]{2,1,0:T(8,128)S(1)} %get-tuple-element.188), channel_id=1, source_target_pairs={{0,16},{240,224},{1,17},{241,225},{2,18},{242,226},{3,19},{243,227... | collective-permute-start | bytes 311048 | tf_op jit(solution)/shard_map/ppermute | solution.py:649
  66.0 5.3 %collective-permute-start.8 = (f32[16,8,640]{2,1,0:T(8,128)}, f32[16,8,640]{2,1,0:T(8,128)S(1)}, u32[]{:S(2)}, u32[]{:S(2)}) collective-permute-start(f32[16,8,640]{2,1,0:T(8,128)} %get-tuple-element.193), channel_id=1, source_target_pairs={{0,16},{240,224},{1,17},{241,225},{2,18},{242,226},{3,19},{243,227... | collective-permute-start | bytes 983048 | tf_op jit(solution)/shard_map/ppermute | solution.py:649
